TPU v7x, 512 devices: a whole 4x4x16 slice. The times are simulated.
512 devices in a mesh: group: 16 (over y, x), curve: 32 (over z, core).
Axes of the slice: x: 4, y: 4, z: 16, core: 2. Of those that a mesh axis runs over, the one named last changes fastest.
Arguments:
- rhs_old: float32 [3584, 24, 576], P(('group', 'curve')), may hold values from -3.1 to 3.1
- coef_old: float32 [3584, 24, 576], P(('group', 'curve')), may hold values from 0.03 to 10
- old_owner: int32 [16, 128], P('group'), may hold values from 0 to 31, as said below
- new_owner: int32 [16, 128], P('group'), may hold values from 0 to 31, as said below
- neighbours: int32 [16, 128, 4], P('group'), may hold values from -1 to 2047, as said below
- coarse_map: int32 [16, 128], P('group'), may hold values from 0 to 31, never falling along the last dimension, each value on 1 to 8 neighbouring positions
Outputs:
- pressure: float32 [2560, 24, 576], P(('group', 'curve'))
Inputs may be any that keep to these rules, and one draw needn't show every extreme that they name: `new_owner`: never falls along the blocks; every device of a segment holds 3 to 5 blocks, and some device holds 5. `old_owner`: never falls along the blocks; every device held at least one block and at most 7, and some device held 7; each block's new owner differs from its old owner by at most one. `neighbours`: the relation is symmetric, low-x with high-x and low-y with high-y; a neighbour is at most 3 places from its block in the global block order. `coarse_map`: never falls along the blocks; every coarse cell holds 1 to 8 consecutive blocks.
All inputs are finite; a program needn't handle non-finite values.
Results may differ from a plain program's by a relative error of at most 0.0003.
Values sent between devices are 32-bit elements; how exact they have to be, the bound alone decides.
No kernel may reach another device: no remote copies, remote signals or barrier semaphores. Data moves between devices by JAX's collectives and lax.ppermute only.
A program may use at most 64 MiB of HBM per device.

v0:
```python
import jax
import jax.numpy as jnp
from jax import lax
from jax.sharding import PartitionSpec as P

SWEEPS = 2
CAP_NEW = 5


OMEGA = 0.8
OPPOSITE = (1, 0, 3, 2)


def shifted(block, axis, distance):
    devices = range(lax.axis_size(axis))
    route = [(i - distance, i) for i in devices if i - distance in devices]
    return lax.ppermute(block, axis, route)


def from_root(block, axis, source):
    block = jnp.where(lax.axis_index(axis) == source, block, jnp.zeros_like(block))
    return lax.psum(block, axis)


def harmonic(left_side, right_side):
    return 2.0 * left_side * right_side / (left_side + right_side)


def block_faces(cell_field):
    block_count, side_cells, plane_cells = cell_field.shape
    lower_y = cell_field[:, :, :side_cells].reshape(block_count, plane_cells)
    upper_y = cell_field[:, :, plane_cells - side_cells :].reshape(block_count, plane_cells)
    return jnp.stack(
        [cell_field[:, 0, :], cell_field[:, side_cells - 1, :], lower_y, upper_y], axis=1
    )


def depth_index(side_cells, plane_cells):
    return lax.broadcasted_iota(jnp.int32, (1, 1, plane_cells), 2) % side_cells


def conduct(coefficient, ghost_cells, factor):
    block_count, side_cells, plane_cells = coefficient.shape
    rows_padded = jnp.concatenate(
        [ghost_cells[:, 0][:, None], coefficient, ghost_cells[:, 1][:, None]], axis=1
    )
    cond_rows = harmonic(rows_padded[:, :-1], rows_padded[:, 1:]) * factor
    cols_padded = jnp.concatenate(
        [
            ghost_cells[:, 2].reshape(block_count, side_cells, side_cells),
            coefficient,
            ghost_cells[:, 3].reshape(block_count, side_cells, side_cells),
        ],
        axis=2,
    )
    cond_cols = harmonic(cols_padded[:, :, :-side_cells], cols_padded[:, :, side_cells:]) * factor
    depth_pos = depth_index(side_cells, plane_cells)
    below_cells = jnp.concatenate([coefficient[:, :, :1], coefficient[:, :, :-1]], axis=2)
    above_cells = jnp.concatenate([coefficient[:, :, 1:], coefficient[:, :, -1:]], axis=2)
    cond_below = harmonic(jnp.where(depth_pos == 0, coefficient, below_cells), coefficient) * factor
    cond_above = (
        harmonic(coefficient, jnp.where(depth_pos == side_cells - 1, coefficient, above_cells))
        * factor
    )
    diagonal = (
        cond_rows[:, :-1]
        + cond_rows[:, 1:]
        + cond_cols[:, :, :-side_cells]
        + cond_cols[:, :, side_cells:]
        + cond_below
        + cond_above
    )
    return (cond_rows, cond_cols, cond_below, cond_above, diagonal)


def operate(cell_field, ghost_cells, cond):
    cond_rows, cond_cols, cond_below, cond_above, diagonal = cond
    block_count, side_cells, plane_cells = cell_field.shape
    rows_padded = jnp.concatenate(
        [ghost_cells[:, 0][:, None], cell_field, ghost_cells[:, 1][:, None]], axis=1
    )
    flux_rows = cond_rows * (rows_padded[:, 1:] - rows_padded[:, :-1])
    cols_padded = jnp.concatenate(
        [
            ghost_cells[:, 2].reshape(block_count, side_cells, side_cells),
            cell_field,
            ghost_cells[:, 3].reshape(block_count, side_cells, side_cells),
        ],
        axis=2,
    )
    flux_cols = cond_cols * (cols_padded[:, :, side_cells:] - cols_padded[:, :, :-side_cells])
    depth_pos = depth_index(side_cells, plane_cells)
    zero_column = jnp.zeros((block_count, side_cells, 1), jnp.float32)
    below_cells = jnp.where(
        depth_pos == 0, 0.0, jnp.concatenate([zero_column, cell_field[:, :, :-1]], axis=2)
    )
    above_cells = jnp.where(
        depth_pos == side_cells - 1,
        0.0,
        jnp.concatenate([cell_field[:, :, 1:], zero_column], axis=2),
    )
    return (
        flux_rows[:, :-1]
        - flux_rows[:, 1:]
        + (flux_cols[:, :, :-side_cells] - flux_cols[:, :, side_cells:])
        + cond_below * (cell_field - below_cells)
        + cond_above * (cell_field - above_cells)
    )


def coarsen(cell_field):
    block_count, side_cells, plane_cells = cell_field.shape
    half_cells = side_cells // 2
    grouped = cell_field.reshape(block_count, half_cells, 2, half_cells, 2, half_cells, 2)
    return grouped.mean(axis=(2, 4, 6)).reshape(block_count, half_cells, half_cells * half_cells)


def refine(cell_field):
    block_count, half_cells, plane_cells = cell_field.shape
    spread = jnp.broadcast_to(
        cell_field.reshape(block_count, half_cells, 1, half_cells, 1, half_cells, 1),
        (block_count, half_cells, 2, half_cells, 2, half_cells, 2),
    )
    return spread.reshape(block_count, 2 * half_cells, 4 * half_cells * half_cells)


def block_totals(cond):
    cond_rows, cond_cols, cond_below, cond_above, diagonal = cond
    block_count, side_cells, plane_cells = cond_below.shape
    depth_pos = depth_index(side_cells, plane_cells)
    low_rows = jnp.sum(cond_rows[:, 0], axis=1)
    high_rows = jnp.sum(cond_rows[:, side_cells], axis=1)
    low_cols = jnp.sum(cond_cols[:, :, :side_cells], axis=(1, 2))
    high_cols = jnp.sum(cond_cols[:, :, plane_cells:], axis=(1, 2))
    outer_depth = jnp.sum(
        jnp.where(depth_pos == 0, cond_below, 0.0)
        + jnp.where(depth_pos == side_cells - 1, cond_above, 0.0),
        axis=(1, 2),
    )
    surface_total = low_rows + high_rows + low_cols + high_cols + outer_depth
    return (surface_total, jnp.stack([low_rows, high_rows, low_cols, high_cols], axis=1))


def coarse_solve(
    surface_total, face_totals, residual_sums, inside, local_ids, cell_map, coarse_cells
):
    block_count = surface_total.shape[0]
    slot_ids = jnp.arange(block_count, dtype=jnp.int32)
    link_table = (local_ids[:, :, None] == slot_ids[None, None, :]) & inside[:, :, None]
    matrix = jnp.diag(surface_total) - jnp.sum(
        jnp.where(link_table, face_totals[:, :, None], 0.0), axis=1
    )
    member = (cell_map[:, None] == jnp.arange(coarse_cells, dtype=jnp.int32)[None, :]).astype(
        jnp.float32
    )
    coarse = jnp.dot(
        member.T,
        jnp.dot(matrix, member, precision=lax.Precision.HIGHEST),
        precision=lax.Precision.HIGHEST,
    )
    target = jnp.dot(member.T, residual_sums[:, None], precision=lax.Precision.HIGHEST)
    lower_factor = jnp.linalg.cholesky(coarse)
    middle = lax.linalg.triangular_solve(lower_factor, target, left_side=True, lower=True)
    solved = lax.linalg.triangular_solve(
        lower_factor, middle, left_side=True, lower=True, transpose_a=True
    )
    return solved[:, 0]


def ghost_faces(cell_field, section, own_fill, layout):
    first_id, finish, held_count, neighbour_ids = layout
    surface = block_faces(cell_field)
    slot_total = surface.shape[0]
    rolled = (held_count - slot_total + jnp.arange(slot_total, dtype=jnp.int32)) % slot_total
    forward = jnp.take(surface, rolled, axis=0)
    if section == 0:
        from_prev = shifted(forward, ("group", "curve"), 1)
        from_next = shifted(surface, ("group", "curve"), -1)
    else:
        from_prev = shifted(forward, ("group", "curve"), 1)
        from_next = shifted(surface, ("group", "curve"), -1)
    candidates = jnp.concatenate([from_prev, surface, from_next], axis=0).reshape(
        -1, surface.shape[2]
    )
    table_row = jnp.where(
        neighbour_ids < first_id,
        neighbour_ids - (first_id - slot_total),
        jnp.where(
            neighbour_ids >= finish,
            slot_total + slot_total + neighbour_ids - finish,
            slot_total + neighbour_ids - first_id,
        ),
    )
    present = neighbour_ids >= 0
    table_row = jnp.where(present, table_row, 0)
    picked_faces = candidates[table_row * 4 + jnp.array(OPPOSITE, dtype=jnp.int32)[None, :]]
    default = surface if own_fill else jnp.zeros_like(surface)
    return jnp.where(present[:, :, None], picked_faces, default)


def jacobi_sweep(cell_field, target, cond, section, layout):
    ghost_cells = ghost_faces(cell_field, section, False, layout)
    return cell_field + OMEGA * (target - operate(cell_field, ghost_cells, cond)) / cond[4]


def body(rhs_old, coef_old, old_owner, new_owner, neighbours, coarse_map):
    old_slots = rhs_old.shape[0]
    blocks = new_owner.shape[1]
    curve_index = lax.axis_index("curve")
    group_index = lax.axis_index("group")
    new_list = new_owner[0]
    old_list = old_owner[0]
    new_first = jnp.sum(new_list < curve_index)
    held_count = jnp.sum(new_list == curve_index)
    old_first = jnp.sum(old_list < curve_index)
    old_count = jnp.sum(old_list == curve_index)
    last_pair = jnp.stack(
        [
            lax.dynamic_index_in_dim(rhs_old, old_count - 1, 0, keepdims=False),
            lax.dynamic_index_in_dim(coef_old, old_count - 1, 0, keepdims=False),
        ]
    )
    first_pair = jnp.stack([rhs_old[0], coef_old[0]])
    prev_block = shifted(last_pair, "curve", 1)
    next_block = shifted(first_pair, "curve", -1)
    slot_ids = jnp.arange(CAP_NEW, dtype=jnp.int32)
    held_block = new_first + slot_ids
    picked = jnp.where(
        held_block < old_first,
        0,
        jnp.where(held_block >= old_first + old_count, old_slots + 1, 1 + held_block - old_first),
    )
    picked = jnp.clip(picked, 0, old_slots + 1)
    occupied = slot_ids < held_count
    rhs_table = jnp.concatenate([prev_block[0:1], rhs_old, next_block[0:1]], axis=0)
    coef_table = jnp.concatenate([prev_block[1:2], coef_old, next_block[1:2]], axis=0)
    source = jnp.where(occupied[:, None, None], rhs_table[picked], 0.0)
    coefficient = jnp.where(occupied[:, None, None], coef_table[picked], 1.0)
    safe_block = jnp.clip(held_block, 0, blocks - 1)
    neighbour_ids = jnp.where(occupied[:, None], neighbours[0][safe_block], -1)
    first_id = group_index * blocks + new_first
    layout = (first_id, first_id + held_count, held_count, neighbour_ids)
    cond_fine = conduct(coefficient, ghost_faces(coefficient, 0, True, layout), 1.0)
    pressure = OMEGA * source / cond_fine[4]
    pressure = jacobi_sweep(pressure, source, cond_fine, 0, layout)
    residual = source - operate(pressure, ghost_faces(pressure, 0, False, layout), cond_fine)
    target = coarsen(residual)
    coef_level = coarsen(coefficient)
    cond_level = conduct(coef_level, ghost_faces(coef_level, 1, True, layout), 0.25)
    correction = OMEGA * target / cond_level[4]
    correction = jacobi_sweep(correction, target, cond_level, 1, layout)
    residual_level = target - operate(
        correction, ghost_faces(correction, 1, False, layout), cond_level
    )
    surface_total, face_totals = block_totals(cond_level)
    residual_sums = jnp.sum(residual_level, axis=(1, 2))
    packed = jnp.concatenate([surface_total[:, None], face_totals, residual_sums[:, None]], axis=1)
    gathered = lax.all_gather(packed, "curve", axis=0, tiled=True)
    curve_size = lax.axis_size("curve")
    device_ids = jnp.arange(curve_size, dtype=jnp.int32)
    firsts = jnp.sum(new_list[None, :] < device_ids[:, None], axis=1)
    gather_rows = new_list * CAP_NEW + jnp.arange(blocks, dtype=jnp.int32) - firsts[new_list]
    values = gathered[gather_rows]
    local_ids = neighbours[0] - group_index * blocks
    inside = (neighbours[0] >= 0) & (local_ids >= 0) & (local_ids < blocks)
    answer = coarse_solve(
        values[:, 0], values[:, 1:5], values[:, 5], inside, local_ids, coarse_map[0], blocks // 4
    )
    owned = jnp.where(curve_index == 0, answer, 0.0)
    answer = from_root(owned, "curve", 0)
    correction = (
        correction + jnp.where(occupied, answer[coarse_map[0][safe_block]], 0.0)[:, None, None]
    )
    for repeat in range(SWEEPS):
        correction = jacobi_sweep(correction, target, cond_level, 1, layout)
    pressure = pressure + refine(correction)
    for repeat in range(SWEEPS):
        pressure = jacobi_sweep(pressure, source, cond_fine, 0, layout)
    return jnp.where(occupied[:, None, None], pressure, 0.0)


def solution(mesh):
    in_specs = (
        P(("group", "curve"), None, None),
        P(("group", "curve"), None, None),
        P("group", None),
        P("group", None),
        P("group", None, None),
        P("group", None),
    )
    out_specs = P(("group", "curve"), None, None)
    return jax.shard_map(body, mesh=mesh, in_specs=in_specs, out_specs=out_specs, check_vma=False)
```

profile of v0, /device:TPU:24, one launch (start us, length us, event | category | flops | bytes accessed | tf_op | source)
XLA Modules:
  0.0 328.1 jit_solution(41537387442528876)
XLA Ops:
  0.0 1.4 fusion.103
  5.0 3.0 collective-permute-start
  8.8 1.4 fusion.100
  21.6 1.3 gather_fusion.11
  33.5 4.3 %copy.201 = f32[5,24,576]{0,2,1:T(8,128)} copy(f32[5,24,576]{2,1,0:T(8,128)S(1)} %gather_fusion.2) | data formatting | bytes 552960 | tf_op jit(solution)/shard_map/gather | solution.py:238
  37.9 8.5 %select_reduce_fusion = f32[5,12,12,12]{0,3,2,1:T(8,128)S(1)} fusion(f32[5,12,2,12,2,12,2]{0,6,5,4,3,2,1:T(2,128)} %bitcast.86, pred[5]{0:T(512)(128)(4,1)S(1)} %iota_compare_fusion.9), kind=kLoop, calls=%fused_computation.27 | loop fusion | flops 129600 | bytes 311045 | tf_op jit(solution)/shard_map/reduce_sum | solution.py:115
  46.4 1.5 copy.202
  51.0 12.8 %collective-permute-start.3 = (f32[5,4,576]{2,1,0:T(4,128)S(1)}, f32[5,4,576]{2,1,0:T(4,128)S(1)}, u32[]{:S(2)}, u32[]{:S(2)}) collective-permute-start(f32[5,4,576]{2,1,0:T(4,128)S(1)} %pad_maximum_fusion.24), channel_id=1, source_target_pairs={{1,0},{2,1},{3,2},{4,3},{5,4},{6,5},{7,6},{8,7},{9,8},{10,9},{11,1... | collective-permute-start | bytes 138248 | tf_op jit(solution)/shard_map/ppermute | solution.py:17
  65.3 3.0 collective-permute-start.9
  69.8 1.9 collective-permute-start.2
  72.4 1.9 collective-permute-start.8
  77.0 4.8 %collective-permute-done.8 = f32[5,4,144]{2,1,0:T(4,128)S(1)} collective-permute-done((f32[5,4,144]{2,1,0:T(4,128)S(1)}, f32[5,4,144]{2,1,0:T(4,128)S(1)}, u32[]{:S(2)}, u32[]{:S(2)}) %collective-permute-start.8) | collective-permute-done | bytes 11552 | tf_op jit(solution)/shard_map/ppermute | solution.py:17
  88.8 3.1 collective-permute-start.5
  92.6 2.1 collective-permute-start.4
  94.8 7.4 %collective-permute-done.4 = f32[5,4,576]{2,1,0:T(4,128)S(1)} collective-permute-done((f32[5,4,576]{2,1,0:T(4,128)S(1)}, f32[5,4,576]{2,1,0:T(4,128)S(1)}, u32[]{:S(2)}, u32[]{:S(2)}) %collective-permute-start.4) | collective-permute-done | bytes 46112 | tf_op jit(solution)/shard_map/ppermute | solution.py:17
  105.9 1.9 collective-permute-start.7
  107.9 2.4 collective-permute-start.6
  110.5 7.1 %collective-permute-done.6 = f32[5,4,576]{2,1,0:T(4,128)S(1)} collective-permute-done((f32[5,4,576]{2,1,0:T(4,128)S(1)}, f32[5,4,576]{2,1,0:T(4,128)S(1)}, u32[]{:S(2)}, u32[]{:S(2)}) %collective-permute-start.6) | collective-permute-done | bytes 46112 | tf_op jit(solution)/shard_map/ppermute | solution.py:17
  119.4 4.3 %copy.199 = f32[5,24,576]{0,2,1:T(8,128)} copy(f32[5,24,576]{2,1,0:T(8,128)S(1)} %fusion.23) | data formatting | bytes 552960 | tf_op jit(solution)/shard_map/sub | solution.py:246
  123.7 7.7 %reduce_sum.140 = f32[5,12,12,12]{0,3,2,1:T(8,128)S(1)} reduce(f32[5,12,2,12,2,12,2]{0,6,5,4,3,2,1:T(2,128)} %bitcast.84, f32[]{:T(128)} %constant.224.clone.1), dimensions={2,4,6}, to_apply=%region_4.6 | reduce | flops 60480 | bytes 311044 | tf_op jit(solution)/shard_map/reduce_sum | solution.py:115
  131.4 2.2 copy.200
  133.7 1.9 broadcast_multiply_fusion.1
  136.8 1.3 fusion.113
  139.2 1.9 collective-permute-start.11
  141.9 2.4 collective-permute-start.10
  145.8 5.5 %collective-permute-done.10 = f32[5,4,144]{2,1,0:T(4,128)S(1)} collective-permute-done((f32[5,4,144]{2,1,0:T(4,128)S(1)}, f32[5,4,144]{2,1,0:T(4,128)S(1)}, u32[]{:S(2)}, u32[]{:S(2)}) %collective-permute-start.10) | collective-permute-done | bytes 11552 | tf_op jit(solution)/shard_map/ppermute | solution.py:17
  154.9 1.9 collective-permute-start.13
  157.6 2.4 collective-permute-start.12
  160.1 6.8 %collective-permute-done.12 = f32[5,4,144]{2,1,0:T(4,128)S(1)} collective-permute-done((f32[5,4,144]{2,1,0:T(4,128)S(1)}, f32[5,4,144]{2,1,0:T(4,128)S(1)}, u32[]{:S(2)}, u32[]{:S(2)}) %collective-permute-start.12) | collective-permute-done | bytes 11552 | tf_op jit(solution)/shard_map/ppermute | solution.py:17
  169.7 27.3 %all-gather = f32[32,5,6]{2,1,0:T(8,128)S(1)} all-gather(f32[1,5,6]{2,1,0:T(8,128)S(1)} %bitcast.88), channel_id=1, replica_groups=mesh['group'=16,'curve'=32] {'curve'}, dimensions={0}, use_global_device_ids=true | all-gather | bytes 3960 | tf_op jit(solution)/shard_map/all_gather | solution.py:258
  200.0 2.9 cholesky.16
  204.3 2.4 custom-call.8
  207.0 47.7 %psum.7 = f32[32]{0:T(128)S(1)} all-reduce(f32[32]{0:T(128)S(1)} %fusion.1), channel_id=1, replica_groups=mesh['group'=16,'curve'=32] {'curve'}, use_global_device_ids=true, to_apply=%region_16.19 | all-reduce | flops 32 | bytes 256 | tf_op jit(solution)/shard_map/psum | solution.py:22
  257.3 1.9 collective-permute-start.15
  259.3 2.4 collective-permute-start.14
  261.8 6.8 %collective-permute-done.14 = f32[5,4,144]{2,1,0:T(4,128)S(1)} collective-permute-done((f32[5,4,144]{2,1,0:T(4,128)S(1)}, f32[5,4,144]{2,1,0:T(4,128)S(1)}, u32[]{:S(2)}, u32[]{:S(2)}) %collective-permute-start.14) | collective-permute-done | bytes 11552 | tf_op jit(solution)/shard_map/ppermute | solution.py:17
  271.6 1.9 collective-permute-start.17
  273.6 2.4 collective-permute-start.16
  276.1 6.8 %collective-permute-done.16 = f32[5,4,144]{2,1,0:T(4,128)S(1)} collective-permute-done((f32[5,4,144]{2,1,0:T(4,128)S(1)}, f32[5,4,144]{2,1,0:T(4,128)S(1)}, u32[]{:S(2)}, u32[]{:S(2)}) %collective-permute-start.16) | collective-permute-done | bytes 11552 | tf_op jit(solution)/shard_map/ppermute | solution.py:17
  285.9 2.0 copy.220
  287.9 5.2 %broadcast_in_dim.405 = f32[5,12,2,12,2,12,2]{0,6,5,4,3,2,1:T(2,128)} broadcast(f32[5,12,12,12]{0,3,2,1:T(8,128)S(1)} %copy.220), dimensions={0,1,3,5} | broadcast | bytes 311040 | tf_op jit(solution)/shard_map/broadcast_in_dim | solution.py:120
  293.1 4.9 %copy.221 = f32[5,24,576]{2,1,0:T(8,128)S(1)} copy(f32[5,24,576]{0,2,1:T(8,128)} %bitcast.85) | data formatting | bytes 552960 | tf_op jit(solution)/shard_map/reshape | solution.py:124
  299.2 1.9 collective-permute-start.19
  301.2 2.4 collective-permute-start.18
  303.7 7.1 %collective-permute-done.18 = f32[5,4,576]{2,1,0:T(4,128)S(1)} collective-permute-done((f32[5,4,576]{2,1,0:T(4,128)S(1)}, f32[5,4,576]{2,1,0:T(4,128)S(1)}, u32[]{:S(2)}, u32[]{:S(2)}) %collective-permute-start.18) | collective-permute-done | bytes 46112 | tf_op jit(solution)/shard_map/ppermute | solution.py:17
  313.8 1.9 collective-permute-start.21
  315.9 2.4 collective-permute-start.20
  318.4 7.1 %collective-permute-done.20 = f32[5,4,576]{2,1,0:T(4,128)S(1)} collective-permute-done((f32[5,4,576]{2,1,0:T(4,128)S(1)}, f32[5,4,576]{2,1,0:T(4,128)S(1)}, u32[]{:S(2)}, u32[]{:S(2)}) %collective-permute-start.20) | collective-permute-done | bytes 46112 | tf_op jit(solution)/shard_map/ppermute | solution.py:17
  (310 shorter events, 76.1 us)
Async XLA Ops:
  3.7 25.3 %collective-permute-start.1 = (f32[2,24,576]{2,1,0:T(8,128)S(1)}, f32[2,24,576]{2,1,0:T(8,128)S(1)}, u32[]{:S(2)}, u32[]{:S(2)}) collective-permute-start(f32[2,24,576]{2,1,0:T(8,128)S(1)} %pad_maximum_fusion.12), channel_id=1, source_target_pairs={{1,0},{2,1},{3,2},{4,3},{5,4},{6,5},{7,6},{8,7},{9,8},{10,9},{11,1... | collective-permute-start | bytes 331784 | tf_op jit(solution)/shard_map/ppermute | solution.py:17
  5.0 24.6 %collective-permute-start = (f32[2,24,576]{2,1,0:T(8,128)S(1)}, f32[2,24,576]{2,1,0:T(8,128)S(1)}, u32[]{:S(2)}, u32[]{:S(2)}) collective-permute-start(f32[2,24,576]{2,1,0:T(8,128)S(1)} %pad_maximum_fusion.11), channel_id=1, source_target_pairs={{0,1},{1,2},{2,3},{3,4},{4,5},{5,6},{6,7},{7,8},{8,9},{9,10},{10,1... | collective-permute-start | bytes 331784 | tf_op jit(solution)/shard_map/ppermute | solution.py:17
  13.3 33.1 %copy-start.6 = (pred[5]{0:T(512)(128)(4,1)}, pred[5]{0:T(512)(128)(4,1)S(1)}, u32[]{:S(2)}) copy-start(pred[5]{0:T(512)(128)(4,1)S(1)} %iota_compare_fusion.9) | copy-start | bytes 19
  21.6 42.2 %copy-start.14 = (s32[1024]{0:T(1024)}, s32[1024]{0:T(1024)S(1)}, u32[]{:S(2)}) copy-start(s32[1024]{0:T(1024)S(1)} %pad_clamp_fusion.4) | copy-start | bytes 12292
  22.9 23.5 %copy-start.15 = (s32[1024]{0:T(1024)}, s32[1024]{0:T(1024)S(1)}, u32[]{:S(2)}) copy-start(s32[1024]{0:T(1024)S(1)} %pad_clamp_fusion.6) | copy-start | bytes 12292
  48.2 38.2 %copy-start.7 = (pred[5]{0:T(512)(128)(4,1)S(1)}, pred[5]{0:T(512)(128)(4,1)}, u32[]{:S(2)}) copy-start(pred[5]{0:T(512)(128)(4,1)} %copy-done.6) | copy-start | bytes 19
  51.0 34.0 %collective-permute-start.3 = (f32[5,4,576]{2,1,0:T(4,128)S(1)}, f32[5,4,576]{2,1,0:T(4,128)S(1)}, u32[]{:S(2)}, u32[]{:S(2)}) collective-permute-start(f32[5,4,576]{2,1,0:T(4,128)S(1)} %pad_maximum_fusion.24), channel_id=1, source_target_pairs={{1,0},{2,1},{3,2},{4,3},{5,4},{6,5},{7,6},{8,7},{9,8},{10,9},{11,1... | collective-permute-start | bytes 138248 | tf_op jit(solution)/shard_map/ppermute | solution.py:17
  65.3 16.5 %collective-permute-start.9 = (f32[5,4,144]{2,1,0:T(4,128)S(1)}, f32[5,4,144]{2,1,0:T(4,128)S(1)}, u32[]{:S(2)}, u32[]{:S(2)}) collective-permute-start(f32[5,4,144]{2,1,0:T(4,128)S(1)} %pad_maximum_fusion.29), channel_id=1, source_target_pairs={{1,0},{2,1},{3,2},{4,3},{5,4},{6,5},{7,6},{8,7},{9,8},{10,9},{11,1... | collective-permute-start | bytes 34568 | tf_op jit(solution)/shard_map/ppermute | solution.py:17
  69.8 15.2 %collective-permute-start.2 = (f32[5,4,576]{2,1,0:T(4,128)S(1)}, f32[5,4,576]{2,1,0:T(4,128)S(1)}, u32[]{:S(2)}, u32[]{:S(2)}) collective-permute-start(f32[5,4,576]{2,1,0:T(4,128)S(1)} %broadcast_select_fusion.5), channel_id=1, source_target_pairs={{0,1},{1,2},{2,3},{3,4},{4,5},{5,6},{6,7},{7,8},{8,9},{9,10},{10,1... | collective-permute-start | bytes 138248 | tf_op jit(solution)/shard_map/ppermute | solution.py:17
  72.4 9.3 %collective-permute-start.8 = (f32[5,4,144]{2,1,0:T(4,128)S(1)}, f32[5,4,144]{2,1,0:T(4,128)S(1)}, u32[]{:S(2)}, u32[]{:S(2)}) collective-permute-start(f32[5,4,144]{2,1,0:T(4,128)S(1)} %broadcast_select_fusion.15), channel_id=1, source_target_pairs={{0,1},{1,2},{2,3},{3,4},{4,5},{5,6},{6,7},{7,8},{8,9},{9,10},{10,1... | collective-permute-start | bytes 34568 | tf_op jit(solution)/shard_map/ppermute | solution.py:17
  82.8 0.6 copy-start.1
  86.3 21.6 %copy-start.2 = (pred[5]{0:T(512)(128)(4,1)S(1)}, pred[5]{0:T(512)(128)(4,1)}, u32[]{:S(2)}) copy-start(pred[5]{0:T(512)(128)(4,1)} %compare_and_fusion) | copy-start | bytes 19
  88.7 30.3 %copy-start.8 = (pred[5]{0:T(512)(128)(4,1)S(1)}, pred[5]{0:T(512)(128)(4,1)}, u32[]{:S(2)}) copy-start(pred[5]{0:T(512)(128)(4,1)} %copy-done.6) | copy-start | bytes 19
  88.7 30.3 %copy-start.10 = (pred[576]{0:T(1024)(128)(4,1)S(1)}, pred[576]{0:T(1024)(128)(4,1)}, u32[]{:S(2)}) copy-start(pred[576]{0:T(1024)(128)(4,1)} %get-tuple-element.144) | copy-start | bytes 1732
  88.7 30.3 %copy-start.12 = (pred[576]{0:T(1024)(128)(4,1)S(1)}, pred[576]{0:T(1024)(128)(4,1)}, u32[]{:S(2)}) copy-start(pred[576]{0:T(1024)(128)(4,1)} %get-tuple-element.145) | copy-start | bytes 1732
  88.8 13.5 %collective-permute-start.5 = (f32[5,4,576]{2,1,0:T(4,128)S(1)}, f32[5,4,576]{2,1,0:T(4,128)S(1)}, u32[]{:S(2)}, u32[]{:S(2)}) collective-permute-start(f32[5,4,576]{2,1,0:T(4,128)S(1)} %pad_maximum_fusion.25), channel_id=1, source_target_pairs={{1,0},{2,1},{3,2},{4,3},{5,4},{6,5},{7,6},{8,7},{9,8},{10,9},{11,1... | collective-permute-start | bytes 138248 | tf_op jit(solution)/shard_map/ppermute | solution.py:17
  92.6 9.6 %collective-permute-start.4 = (f32[5,4,576]{2,1,0:T(4,128)S(1)}, f32[5,4,576]{2,1,0:T(4,128)S(1)}, u32[]{:S(2)}, u32[]{:S(2)}) collective-permute-start(f32[5,4,576]{2,1,0:T(4,128)S(1)} %broadcast_select_fusion.4), channel_id=1, source_target_pairs={{0,1},{1,2},{2,3},{3,4},{4,5},{5,6},{6,7},{7,8},{8,9},{9,10},{10,1... | collective-permute-start | bytes 138248 | tf_op jit(solution)/shard_map/ppermute | solution.py:17
  105.9 11.7 %collective-permute-start.7 = (f32[5,4,576]{2,1,0:T(4,128)S(1)}, f32[5,4,576]{2,1,0:T(4,128)S(1)}, u32[]{:S(2)}, u32[]{:S(2)}) collective-permute-start(f32[5,4,576]{2,1,0:T(4,128)S(1)} %pad_maximum_fusion.26), channel_id=1, source_target_pairs={{1,0},{2,1},{3,2},{4,3},{5,4},{6,5},{7,6},{8,7},{9,8},{10,9},{11,1... | collective-permute-start | bytes 138248 | tf_op jit(solution)/shard_map/ppermute | solution.py:17
  107.9 9.6 %collective-permute-start.6 = (f32[5,4,576]{2,1,0:T(4,128)S(1)}, f32[5,4,576]{2,1,0:T(4,128)S(1)}, u32[]{:S(2)}, u32[]{:S(2)}) collective-permute-start(f32[5,4,576]{2,1,0:T(4,128)S(1)} %broadcast_select_fusion.3), channel_id=1, source_target_pairs={{0,1},{1,2},{2,3},{3,4},{4,5},{5,6},{6,7},{7,8},{8,9},{9,10},{10,1... | collective-permute-start | bytes 138248 | tf_op jit(solution)/shard_map/ppermute | solution.py:17
  131.4 66.8 %copy-start = (s32[1,128]{1,0:T(1,128)S(1)}, s32[1,128]{1,0:T(1,128)}, u32[]{:S(2)}) copy-start(s32[1,128]{1,0:T(1,128)} %param.25) | copy-start | bytes 1540
  133.7 125.6 %copy-start.3 = (pred[5]{0:T(512)(128)(4,1)S(1)}, pred[5]{0:T(512)(128)(4,1)}, u32[]{:S(2)}) copy-start(pred[5]{0:T(512)(128)(4,1)} %compare_and_fusion) | copy-start | bytes 19
  138.1 7.4 %copy-start.4 = (f32[5,1,144]{2,1,0:T(1,128)}, f32[5,1,144]{2,1,0:T(1,128)S(1)}, u32[]{:S(2)}) copy-start(f32[5,1,144]{2,1,0:T(1,128)S(1)} %get-tuple-element.111) | copy-start | bytes 8644
  138.3 7.2 %copy-start.5 = (f32[5,1,144]{2,1,0:T(1,128)}, f32[5,1,144]{2,1,0:T(1,128)S(1)}, u32[]{:S(2)}) copy-start(f32[5,1,144]{2,1,0:T(1,128)S(1)} %stack_reshape.88) | copy-start | bytes 8644
  139.2 12.1 %collective-permute-start.11 = (f32[5,4,144]{2,1,0:T(4,128)S(1)}, f32[5,4,144]{2,1,0:T(4,128)S(1)}, u32[]{:S(2)}, u32[]{:S(2)}) collective-permute-start(f32[5,4,144]{2,1,0:T(4,128)S(1)} %pad_maximum_fusion.30), channel_id=1, source_target_pairs={{1,0},{2,1},{3,2},{4,3},{5,4},{6,5},{7,6},{8,7},{9,8},{10,9},{11,1... | collective-permute-start | bytes 34568 | tf_op jit(solution)/shard_map/ppermute | solution.py:17
  141.9 9.3 %collective-permute-start.10 = (f32[5,4,144]{2,1,0:T(4,128)S(1)}, f32[5,4,144]{2,1,0:T(4,128)S(1)}, u32[]{:S(2)}, u32[]{:S(2)}) collective-permute-start(f32[5,4,144]{2,1,0:T(4,128)S(1)} %broadcast_select_fusion.14), channel_id=1, source_target_pairs={{0,1},{1,2},{2,3},{3,4},{4,5},{5,6},{6,7},{7,8},{8,9},{9,10},{10,1... | collective-permute-start | bytes 34568 | tf_op jit(solution)/shard_map/ppermute | solution.py:17
  154.9 12.0 %collective-permute-start.13 = (f32[5,4,144]{2,1,0:T(4,128)S(1)}, f32[5,4,144]{2,1,0:T(4,128)S(1)}, u32[]{:S(2)}, u32[]{:S(2)}) collective-permute-start(f32[5,4,144]{2,1,0:T(4,128)S(1)} %pad_maximum_fusion.31), channel_id=1, source_target_pairs={{1,0},{2,1},{3,2},{4,3},{5,4},{6,5},{7,6},{8,7},{9,8},{10,9},{11,1... | collective-permute-start | bytes 34568 | tf_op jit(solution)/shard_map/ppermute | solution.py:17
  157.6 9.3 %collective-permute-start.12 = (f32[5,4,144]{2,1,0:T(4,128)S(1)}, f32[5,4,144]{2,1,0:T(4,128)S(1)}, u32[]{:S(2)}, u32[]{:S(2)}) collective-permute-start(f32[5,4,144]{2,1,0:T(4,128)S(1)} %broadcast_select_fusion.13), channel_id=1, source_target_pairs={{0,1},{1,2},{2,3},{3,4},{4,5},{5,6},{6,7},{7,8},{8,9},{9,10},{10,1... | collective-permute-start | bytes 34568 | tf_op jit(solution)/shard_map/ppermute | solution.py:17
  257.3 11.3 %collective-permute-start.15 = (f32[5,4,144]{2,1,0:T(4,128)S(1)}, f32[5,4,144]{2,1,0:T(4,128)S(1)}, u32[]{:S(2)}, u32[]{:S(2)}) collective-permute-start(f32[5,4,144]{2,1,0:T(4,128)S(1)} %pad_maximum_fusion.32), channel_id=1, source_target_pairs={{1,0},{2,1},{3,2},{4,3},{5,4},{6,5},{7,6},{8,7},{9,8},{10,9},{11,1... | collective-permute-start | bytes 34568 | tf_op jit(solution)/shard_map/ppermute | solution.py:17
  259.3 9.3 %collective-permute-start.14 = (f32[5,4,144]{2,1,0:T(4,128)S(1)}, f32[5,4,144]{2,1,0:T(4,128)S(1)}, u32[]{:S(2)}, u32[]{:S(2)}) collective-permute-start(f32[5,4,144]{2,1,0:T(4,128)S(1)} %broadcast_select_fusion.12), channel_id=1, source_target_pairs={{0,1},{1,2},{2,3},{3,4},{4,5},{5,6},{6,7},{7,8},{8,9},{9,10},{10,1... | collective-permute-start | bytes 34568 | tf_op jit(solution)/shard_map/ppermute | solution.py:17
  271.6 11.3 %collective-permute-start.17 = (f32[5,4,144]{2,1,0:T(4,128)S(1)}, f32[5,4,144]{2,1,0:T(4,128)S(1)}, u32[]{:S(2)}, u32[]{:S(2)}) collective-permute-start(f32[5,4,144]{2,1,0:T(4,128)S(1)} %pad_maximum_fusion.33), channel_id=1, source_target_pairs={{1,0},{2,1},{3,2},{4,3},{5,4},{6,5},{7,6},{8,7},{9,8},{10,9},{11,1... | collective-permute-start | bytes 34568 | tf_op jit(solution)/shard_map/ppermute | solution.py:17
  273.6 9.3 %collective-permute-start.16 = (f32[5,4,144]{2,1,0:T(4,128)S(1)}, f32[5,4,144]{2,1,0:T(4,128)S(1)}, u32[]{:S(2)}, u32[]{:S(2)}) collective-permute-start(f32[5,4,144]{2,1,0:T(4,128)S(1)} %broadcast_select_fusion.11), channel_id=1, source_target_pairs={{0,1},{1,2},{2,3},{3,4},{4,5},{5,6},{6,7},{7,8},{8,9},{9,10},{10,1... | collective-permute-start | bytes 34568 | tf_op jit(solution)/shard_map/ppermute | solution.py:17
  293.1 19.2 %copy-start.9 = (pred[5]{0:T(512)(128)(4,1)S(1)}, pred[5]{0:T(512)(128)(4,1)}, u32[]{:S(2)}) copy-start(pred[5]{0:T(512)(128)(4,1)} %copy-done.6) | copy-start | bytes 19
  293.1 19.2 %copy-start.11 = (pred[576]{0:T(1024)(128)(4,1)S(1)}, pred[576]{0:T(1024)(128)(4,1)}, u32[]{:S(2)}) copy-start(pred[576]{0:T(1024)(128)(4,1)} %get-tuple-element.144) | copy-start | bytes 1732
  293.1 19.2 %copy-start.13 = (pred[576]{0:T(1024)(128)(4,1)S(1)}, pred[576]{0:T(1024)(128)(4,1)}, u32[]{:S(2)}) copy-start(pred[576]{0:T(1024)(128)(4,1)} %get-tuple-element.145) | copy-start | bytes 1732
  299.2 11.6 %collective-permute-start.19 = (f32[5,4,576]{2,1,0:T(4,128)S(1)}, f32[5,4,576]{2,1,0:T(4,128)S(1)}, u32[]{:S(2)}, u32[]{:S(2)}) collective-permute-start(f32[5,4,576]{2,1,0:T(4,128)S(1)} %pad_maximum_fusion.27), channel_id=1, source_target_pairs={{1,0},{2,1},{3,2},{4,3},{5,4},{6,5},{7,6},{8,7},{9,8},{10,9},{11,1... | collective-permute-start | bytes 138248 | tf_op jit(solution)/shard_map/ppermute | solution.py:17
  301.2 9.6 %collective-permute-start.18 = (f32[5,4,576]{2,1,0:T(4,128)S(1)}, f32[5,4,576]{2,1,0:T(4,128)S(1)}, u32[]{:S(2)}, u32[]{:S(2)}) collective-permute-start(f32[5,4,576]{2,1,0:T(4,128)S(1)} %broadcast_select_fusion.2), channel_id=1, source_target_pairs={{0,1},{1,2},{2,3},{3,4},{4,5},{5,6},{6,7},{7,8},{8,9},{9,10},{10,1... | collective-permute-start | bytes 138248 | tf_op jit(solution)/shard_map/ppermute | solution.py:17
  313.8 11.6 %collective-permute-start.21 = (f32[5,4,576]{2,1,0:T(4,128)S(1)}, f32[5,4,576]{2,1,0:T(4,128)S(1)}, u32[]{:S(2)}, u32[]{:S(2)}) collective-permute-start(f32[5,4,576]{2,1,0:T(4,128)S(1)} %pad_maximum_fusion.28), channel_id=1, source_target_pairs={{1,0},{2,1},{3,2},{4,3},{5,4},{6,5},{7,6},{8,7},{9,8},{10,9},{11,1... | collective-permute-start | bytes 138248 | tf_op jit(solution)/shard_map/ppermute | solution.py:17
  315.9 9.6 %collective-permute-start.20 = (f32[5,4,576]{2,1,0:T(4,128)S(1)}, f32[5,4,576]{2,1,0:T(4,128)S(1)}, u32[]{:S(2)}, u32[]{:S(2)}) collective-permute-start(f32[5,4,576]{2,1,0:T(4,128)S(1)} %broadcast_select_fusion.1), channel_id=1, source_target_pairs={{0,1},{1,2},{2,3},{3,4},{4,5},{5,6},{6,7},{7,8},{8,9},{9,10},{10,1... | collective-permute-start | bytes 138248 | tf_op jit(solution)/shard_map/ppermute | solution.py:17
where the time goes:
time: 330 us; the launch traced here: 328 us
  blocking collectives  75.1 us (23%)
  local copies, waits for them, and re-layouts  64.2 us (19%)
  other arithmetic  62.9 us (19%)
  waiting for transfers between devices  59.4 us (18%)
  starting transfers between devices  59.3 us (18%)
  between operations  6.12 us (2%)
    ppermute x22, waiting for transfers between devices, shifted(): return lax.ppermute(block, axis, route)  59.4 us
    ppermute x22, starting transfers between devices, shifted(): return lax.ppermute(block, axis, route)  59.3 us
    psum x1, blocking collectives, from_root(): return lax.psum(block, axis)  47.7 us
    all_gather x1, blocking collectives, body(): gathered = lax.all_gather(packed, 'curve', axis=0, tiled=True)  27.3 us
    reduce_sum x2, other arithmetic, coarsen(): grouped.mean(axis=(2, 4, 6))  16.2 us
    broadcast_in_dim x3, local copies, waits for them, and re-layouts, refine(): jnp.broadcast_to(cell_field.reshape(block_count, half_cells, 1, half_cell...  8.27 us
    gather x10, local copies, waits for them, and re-layouts, ghost_faces(): forward = jnp.take(surface, rolled, axis=0)  6.87 us
  transfers between devices with their start and end apart: 22, of which 9 were waited for; matrix products, arithmetic and copies ran while one was open for 10% of the time, Pallas kernels for 0%

commit v1 on v0

v1 whole, which is shorter than its diff:
```python
import jax
import jax.numpy as jnp
from jax import lax
from jax.experimental import pallas as pl
from jax.experimental.pallas import tpu as pltpu
from jax.sharding import PartitionSpec as P

OMEGA = 0.8
KEEP = 1.0 - OMEGA
CAP_OLD = 7
CAP_NEW = 5
REACH = 3
NBG = 128
NCOARSE = 32
AXES = ("group", "curve")
F32 = jnp.float32
I32 = jnp.int32

HELD, PICK, TABLE, CELL, BAND = 0, 1, 8, 32, 40
ABSENT = 2 * REACH + CAP_NEW


class Level:
    def __init__(self, side, rows, width, high_at, x_low, x_high, face_rows, factor):
        self.side, self.rows, self.width = side, rows, width
        self.last = side * side - side - (width - 128)
        self.high_at = high_at
        self.x_low, self.x_high, self.face_rows = x_low, x_high, face_rows
        self.tiles = width // 128
        self.factor = factor


FINE = Level(24, 24, 640, 40, 24, 32, 40, 1.0)
COARSE = Level(12, 16, 256, 68, 16, 20, 24, 0.25)
BOTH_ROWS = FINE.face_rows + COARSE.face_rows


def iota(shape, axis):
    return lax.broadcasted_iota(I32, shape, axis)


def over(value, side):
    return (value * 43691) >> (20 if side == 24 else 19)


def pack_faces(lev, field, faces, k, base):
    lane = iota((lev.rows, 128), 1)
    tail = field[:, lev.width - 128 :]
    move = lev.high_at - lev.last
    if move:
        tail = pltpu.roll(tail, move, 1)
    faces[k, base : base + lev.rows, :] = jnp.where(lane < lev.side, field[:, :128], tail)
    for j in range(lev.tiles):
        part = slice(128 * j, 128 * j + 128)
        low, high = base + lev.x_low + j, base + lev.x_high + j
        faces[k, low : low + 1, :] = field[0:1, part]
        faces[k, high : high + 1, :] = field[lev.side - 1 : lev.side, part]


def send_faces(info, faces, ahead, back):
    first = jnp.maximum(info[HELD] - REACH, 0)
    for j in range(REACH):
        ahead[j] = faces[first + j]
        back[j] = faces[j]


def fill_table(table, before, faces, after):
    table[0:REACH] = before[...]
    table[REACH : REACH + CAP_NEW] = faces[...]
    table[REACH + CAP_NEW : ABSENT] = after[...]
    table[ABSENT] = jnp.zeros(table.shape[1:], F32)


def ghosts_of(lev, info, table, k, base):
    row = [info[TABLE + 4 * k + f] for f in range(4)]
    x_low = jnp.concatenate(
        [table[row[0], pl.ds(base + lev.x_high + j, 1), :] for j in range(lev.tiles)], axis=1
    )
    x_high = jnp.concatenate(
        [table[row[1], pl.ds(base + lev.x_low + j, 1), :] for j in range(lev.tiles)], axis=1
    )
    y_low = pltpu.roll(table[row[2], pl.ds(base, lev.rows), :], 128 - lev.high_at, 1)
    y_high = pltpu.roll(table[row[3], pl.ds(base, lev.rows), :], lev.last, 1)
    return row, x_low, x_high, y_low, y_high


def neighbour_sum(lev, field, g, ghosts):
    _, x_low, x_high, y_low, y_high = ghosts
    rows, width, side = lev.rows, lev.width, lev.side
    row = iota((rows, width), 0)
    lane = iota((rows, 128), 1)
    total = g[0] * pltpu.roll(field, 1, 1) + g[1] * pltpu.roll(field, width - 1, 1)
    total += g[2] * pltpu.roll(field, side, 1) + g[3] * pltpu.roll(field, width - side, 1)
    total += g[4] * jnp.where(row == 0, x_low, pltpu.roll(field, 1, 0))
    total += g[5] * jnp.where(row == side - 1, x_high, pltpu.roll(field, rows - 1, 0))
    low = jnp.where(lane < side, g[2][:, :128] * y_low, 0.0)
    on_high = (lane >= lev.last) & (lane < lev.last + side)
    high = jnp.where(on_high, g[3][:, width - 128 :] * y_high, 0.0)
    parts = [low, high]
    if width > 256:
        parts = [low, jnp.zeros((rows, width - 256), F32), high]
    return total + jnp.concatenate(parts, axis=1)


def conductances(lev, cell, ghosts):
    present, x_low, x_high, y_low, y_high = ghosts
    present = [p != ABSENT for p in present]
    rows, width, side = lev.rows, lev.width, lev.side
    row, lane = iota((rows, width), 0), iota((rows, width), 1)
    depth = lane - side * over(lane, side)
    last = side - 1
    end = side * side
    x_low = jnp.where(present[0], x_low, cell[0:1, :])
    x_high = jnp.where(present[1], x_high, cell[last : last + 1, :])
    y_low = jnp.where(present[2], y_low, cell[:, :128])
    y_high = jnp.where(present[3], y_high, cell[:, width - 128 :])
    spare = jnp.ones((rows, width - 128), F32)
    y_low = jnp.concatenate([y_low, spare], axis=1)
    y_high = jnp.concatenate([spare, y_high], axis=1)
    high_y = (lane >= end - side) & (lane < end)
    across = [
        jnp.where(depth == 0, cell, pltpu.roll(cell, 1, 1)),
        jnp.where(depth == last, cell, pltpu.roll(cell, width - 1, 1)),
        jnp.where(lane < side, y_low, pltpu.roll(cell, side, 1)),
        jnp.where(high_y, y_high, pltpu.roll(cell, width - side, 1)),
        jnp.where(row == 0, x_low, pltpu.roll(cell, 1, 0)),
        jnp.where(row == last, x_high, pltpu.roll(cell, rows - 1, 0)),
    ]
    q = [2.0 * cell * other / (cell + other) * lev.factor for other in across]
    diagonal = q[0] + q[1] + q[2] + q[3] + q[4] + q[5]
    inside = (lane < end) & (row < side)
    weight = jnp.where(inside, OMEGA / diagonal, 0.0)
    g = [weight * one for one in q]
    g[0] = jnp.where(depth == 0, 0.0, g[0])
    g[1] = jnp.where(depth == last, 0.0, g[1])
    masks = (row, lane, depth, inside, high_y)
    return q, g, weight, diagonal, masks


def both_totals(values):
    return jnp.sum(jnp.sum(values, axis=0, keepdims=True), axis=1, keepdims=True)


def spread_matrix():
    lane = iota((1, FINE.width), 1)
    y = over(lane, 24)
    group = 12 * (y >> 1) + ((lane - 24 * y) >> 1)
    group = jnp.where(lane < 576, group, -1)
    return (iota((COARSE.width, FINE.width), 0) == group).astype(F32).astype(jnp.bfloat16)


def split_three(values):
    high = values.astype(jnp.bfloat16)
    rest = values - high.astype(F32)
    mid = rest.astype(jnp.bfloat16)
    low = (rest - mid.astype(F32)).astype(jnp.bfloat16)
    return high, mid, low


def coarsen_blocks(fine, scratch):
    spread = spread_matrix()
    total = None
    for part in split_three(fine):
        one = lax.dot_general(
            part, spread, (((1,), (1,)), ((), ())), preferred_element_type=F32
        )
        total = one if total is None else total + one
    scratch[0] = total[:, :128]
    scratch[1] = total[:, 128:]


def coarse_rows(scratch, k):
    even, odd = pl.ds(24 * k, 12, stride=2), pl.ds(24 * k + 1, 12, stride=2)
    halves = [scratch[t, even, :] + scratch[t, odd, :] for t in range(2)]
    return 0.125 * jnp.concatenate(halves, axis=1)


def first_kernel(new_ref, old_ref, near_ref, map_ref, rhs_ref, coef_ref, ahead, back, info):
    curve = lax.axis_index("curve")
    group = lax.axis_index("group")
    new, old = new_ref[...], old_ref[...]

    def count(mask):
        return jnp.sum(jnp.where(mask, 1.0, 0.0)).astype(I32)

    new_first, held = count(new < curve), count(new == curve)
    old_first, old_count = count(old < curve), count(old == curve)
    last = jnp.clip(old_count - 1, 0, CAP_OLD - 1)
    ahead[0] = rhs_ref[last]
    ahead[1] = coef_ref[last]
    back[0] = rhs_ref[0]
    back[1] = coef_ref[0]
    info[HELD] = held
    first_id = group * NBG + new_first
    finish = first_id + held
    for k in range(CAP_NEW):
        block = new_first + k
        pick = jnp.where(block >= old_first + old_count, CAP_OLD + 1, 1 + block - old_first)
        pick = jnp.where(block < old_first, 0, pick)
        info[PICK + k] = jnp.clip(pick, 0, CAP_OLD + 1)
        occupied = k < held
        safe = jnp.clip(block, 0, NBG - 1)
        cell = map_ref[0, safe]
        info[CELL + k] = jnp.where(occupied, cell, -1)
        for f in range(4):
            near = near_ref[f, safe]
            present = occupied & (near >= 0)
            slot = jnp.where(near >= finish, REACH + CAP_NEW - finish, REACH - first_id) + near
            slot = jnp.clip(slot, 0, ABSENT - 1)
            info[TABLE + 4 * k + f] = jnp.where(present, slot, ABSENT)
            local = near - group * NBG
            inside = present & (local >= 0) & (local < NBG)
            other = map_ref[0, jnp.clip(local, 0, NBG - 1)]
            info[BAND + 4 * k + f] = jnp.where(inside, 8 * k + 3 + other - cell, -1)


def gather_kernel(
    info, rhs_ref, coef_ref, before, after, source, coef, faces, ahead, back, level, scratch
):
    source[...] = jnp.zeros(source.shape, F32)
    coef[...] = jnp.ones(coef.shape, F32)
    for k in range(CAP_NEW):
        pick = info[PICK + k]
        slot = jnp.clip(pick - 1, 0, CAP_OLD - 1)
        occupied = k < info[HELD]
        for i, (table, out, rest) in enumerate(((rhs_ref, source, 0.0), (coef_ref, coef, 1.0))):
            block = jnp.where(pick == 0, before[i], table[slot])
            block = jnp.where(pick == CAP_OLD + 1, after[i], block)
            out[k, :, 0:576] = jnp.where(occupied, block, rest)
    coarsen_blocks(coef[...].reshape(CAP_NEW * 24, FINE.width), scratch)
    row, lane = iota((16, 256), 0), iota((16, 256), 1)
    for k in range(CAP_NEW):
        pack_faces(FINE, coef[k], faces, k, 0)
        level[k] = jnp.ones((16, 256), F32)
        level[k, 0:12, :] = coarse_rows(scratch, k)
        level[k] = jnp.where((row < 12) & (lane < 144), level[k], 1.0)
        pack_faces(COARSE, level[k], faces, k, FINE.face_rows)
    send_faces(info, faces, ahead, back)


def conduct_kernel(
    info, source, coef, level, faces_in, before, after,
    fine_g, fine_s, fine_d, coarse_g, coarse_w, coarse_d, row_out, u, faces, ahead, back, table,
):
    fill_table(table, before, faces_in, after)
    lane_row = iota((1, 128), 1)
    band = jnp.zeros((1, 128), F32)
    for k in range(CAP_NEW):
        ghosts = ghosts_of(FINE, info, table, k, 0)
        _, g, weight, diagonal, _ = conductances(FINE, coef[k], ghosts)
        for i in range(6):
            fine_g[k, i] = g[i]
        fine_d[k] = (1.0 / OMEGA) * diagonal
        start = weight * source[k]
        fine_s[k] = start
        u[k] = start
        pack_faces(FINE, start, faces, k, 0)

        ghosts = ghosts_of(COARSE, info, table, k, FINE.face_rows)
        q, g, weight, diagonal, masks = conductances(COARSE, level[k], ghosts)
        row, lane, depth, inside, high_y = masks
        for i in range(6):
            coarse_g[k, i] = g[i]
        coarse_w[k] = weight
        coarse_d[k] = (1.0 / OMEGA) * diagonal
        face = [
            both_totals(jnp.where(inside & (row == 0), q[4], 0.0)),
            both_totals(jnp.where(inside & (row == 11), q[5], 0.0)),
            both_totals(jnp.where(inside & (lane < 12), q[2], 0.0)),
            both_totals(jnp.where(inside & high_y, q[3], 0.0)),
        ]
        ends = jnp.where(inside & (depth == 0), q[0], 0.0)
        ends += jnp.where(inside & (depth == 11), q[1], 0.0)
        surface = face[0] + face[1] + face[2] + face[3] + both_totals(ends)
        occupied = k < info[HELD]
        band += jnp.where((lane_row == 8 * k + 3) & occupied, surface, 0.0)
        for f in range(4):
            band -= jnp.where(lane_row == info[BAND + 4 * k + f], face[f], 0.0)
        band += jnp.where(lane_row == 64 + k, info[CELL + k].astype(F32), 0.0)
    row_out[...] = band
    send_faces(info, faces, ahead, back)


def sweep_kernel(lev, info, u_in, g, start, faces_in, before, after, u, faces, ahead, back, table):
    fill_table(table, before, faces_in, after)
    for k in range(CAP_NEW):
        field = u_in[k]
        ghosts = ghosts_of(lev, info, table, k, 0)
        new = KEEP * field + (start[k] + neighbour_sum(lev, field, g.at[k], ghosts))
        u[k] = new
        pack_faces(lev, new, faces, k, 0)
    send_faces(info, faces, ahead, back)


def residual_kernel(
    info, u_in, g, start, diagonal, weight, faces_in, before, after,
    coarse_s, faces, ahead, back, table, rest, scratch,
):
    fill_table(table, before, faces_in, after)
    for k in range(CAP_NEW):
        field = u_in[k]
        ghosts = ghosts_of(FINE, info, table, k, 0)
        inner = start[k] + neighbour_sum(FINE, field, g.at[k], ghosts)
        rest[k] = diagonal[k] * (inner - OMEGA * field)
    coarsen_blocks(rest[...].reshape(CAP_NEW * 24, FINE.width), scratch)
    for k in range(CAP_NEW):
        coarse_s[k] = jnp.zeros((16, 256), F32)
        coarse_s[k, 0:12, :] = weight[k, 0:12, :] * coarse_rows(scratch, k)
        pack_faces(COARSE, coarse_s[k], faces, k, 0)
    send_faces(info, faces, ahead, back)


def total_kernel(info, u_in, g, start, diagonal, row_in, faces_in, before, after, rows_out, table):
    fill_table(table, before, faces_in, after)
    lane_row = iota((1, 128), 1)
    row, lane = iota((16, 256), 0), iota((16, 256), 1)
    inside = (row < 12) & (lane < 144)
    band = row_in[...]
    for k in range(CAP_NEW):
        field = u_in[k]
        ghosts = ghosts_of(COARSE, info, table, k, 0)
        inner = start[k] + neighbour_sum(COARSE, field, g.at[k], ghosts)
        rest = jnp.where(inside, diagonal[k] * (inner - OMEGA * field), 0.0)
        occupied = k < info[HELD]
        band += jnp.where((lane_row == 8 * k + 7) & occupied, both_totals(rest), 0.0)
    rows_out[...] = jnp.broadcast_to(band, rows_out.shape)


def solve_kernel(info, rows_in, u_in, u, faces, ahead, back):
    rows = rows_in[...]
    shape = (NCOARSE, 128)
    row, lane = iota(shape, 0), iota(shape, 1)
    cells = iota((NCOARSE, NCOARSE), 1).astype(F32)
    band = jnp.zeros(shape, F32)
    for k in range(CAP_NEW):
        member = (rows[:, 64 + k : 65 + k] == cells).astype(F32)
        part = rows if k == 0 else pltpu.roll(rows, 128 - 8 * k, 1)
        part = jnp.where(lane < 8, part, 0.0)
        band += lax.dot_general(
            member, part, (((0,), (0,)), ((), ())),
            precision=lax.Precision.HIGHEST, preferred_element_type=F32,
        )
    matrix = jnp.where(lane == 64, band[:, 7:8], 0.0)
    for o in range(7):
        matrix += jnp.where(lane == row + (o - REACH), band[:, o : o + 1], 0.0)

    def drop(current, j):
        pivot = current[j : j + 1, :]
        share = current[:, j : j + 1] / pivot[:, j : j + 1]
        return jnp.where(iota((NCOARSE, 1), 0) == j, 0.0, share) * pivot

    apart = (NCOARSE - REACH - 1) // 2
    for j in range(apart):
        matrix = matrix - (drop(matrix, j) + drop(matrix, NCOARSE - 1 - j))
    for j in range(apart, NCOARSE - apart):
        matrix = matrix - drop(matrix, j)
    pivots = jnp.sum(jnp.where(lane == row, matrix, 0.0), axis=1, keepdims=True)
    answer = matrix[:, 64:65] / pivots
    at = iota((NCOARSE, 1), 0)
    row, lane = iota((16, 256), 0), iota((16, 256), 1)
    inside = (row < 12) & (lane < 144)
    for k in range(CAP_NEW):
        lift = jnp.sum(jnp.where(at == info[CELL + k], answer, 0.0), axis=0, keepdims=True)
        new = u_in[k] + jnp.where(inside, lift, 0.0)
        u[k] = new
        pack_faces(COARSE, new, faces, k, 0)
    send_faces(info, faces, ahead, back)


def refine_kernel(
    info, e_in, g, start, faces_in, before, after, u_in, u, faces, ahead, back, table, coarse, rest
):
    fill_table(table, before, faces_in, after)
    for k in range(CAP_NEW):
        field = e_in[k]
        ghosts = ghosts_of(COARSE, info, table, k, 0)
        coarse[k] = KEEP * field + (start[k] + neighbour_sum(COARSE, field, g.at[k], ghosts))
    spread = spread_matrix()
    total = None
    for part in split_three(coarse[...].reshape(CAP_NEW * 16, 256)):
        one = jnp.dot(part, spread, preferred_element_type=F32)
        total = one if total is None else total + one
    for k in range(CAP_NEW):
        twelve = total[16 * k : 16 * k + 12, :]
        for t in range(FINE.tiles):
            part = slice(128 * t, 128 * t + 128)
            rest[t, pl.ds(0, 12, stride=2), :] = twelve[:, part]
            rest[t, pl.ds(1, 12, stride=2), :] = twelve[:, part]
        new = u_in[k] + jnp.concatenate([rest[t] for t in range(FINE.tiles)], axis=1)
        u[k] = new
        pack_faces(FINE, new, faces, k, 0)
    send_faces(info, faces, ahead, back)


def last_kernel(info, u_in, g, start, faces_in, before, after, out, table):
    fill_table(table, before, faces_in, after)
    for k in range(CAP_NEW):
        field = u_in[k]
        ghosts = ghosts_of(FINE, info, table, k, 0)
        new = KEEP * field + (start[k] + neighbour_sum(FINE, field, g.at[k], ghosts))
        out[k] = jnp.where(k < info[HELD], new[:, 0:576], 0.0)


def sds(*shape):
    return jax.ShapeDtypeStruct(shape, F32)


SMEM = pl.BlockSpec(memory_space=pltpu.SMEM)
VMEM = pl.BlockSpec(memory_space=pltpu.VMEM)


def call(kernel, name, outs, scratch, args, in_specs=None, out_specs=None):
    many = len(outs) > 1
    return pl.pallas_call(
        kernel,
        out_shape=outs if many else outs[0],
        in_specs=in_specs or [SMEM] + [VMEM] * (len(args) - 1),
        out_specs=out_specs or ([VMEM] * len(outs) if many else VMEM),
        scratch_shapes=[pltpu.VMEM(s, F32) for s in scratch],
        compiler_params=pltpu.CompilerParams(vmem_limit_bytes=24 * 1024 * 1024),
        name=name,
    )(*args)


def shifted(block, axis, distance):
    devices = range(lax.axis_size(axis))
    route = [(i - distance, i) for i in devices if i - distance in devices]
    return lax.ppermute(block, axis, route)


def exchange(ahead, back):
    return shifted(ahead, AXES, 1), shifted(back, AXES, -1)


def face_outs(rows):
    return [sds(CAP_NEW, rows, 128), sds(REACH, rows, 128), sds(REACH, rows, 128)]


def body(rhs_old, coef_old, old_owner, new_owner, neighbours, coarse_map):
    near = jnp.transpose(neighbours[0])
    pair = sds(2, 24, 576)
    ahead, back, info = call(
        first_kernel, "owners",
        [pair, pair, jax.ShapeDtypeStruct((128,), I32)], [],
        (new_owner, old_owner, near, coarse_map, rhs_old, coef_old),
        [VMEM, VMEM, SMEM, SMEM, VMEM, VMEM], [VMEM, VMEM, SMEM],
    )
    before, after = shifted(ahead, "curve", 1), shifted(back, "curve", -1)

    fine = sds(CAP_NEW, 24, FINE.width)
    coarse = sds(CAP_NEW, 16, 256)
    fine_table = [(ABSENT + 1, FINE.face_rows, 128)]
    coarse_table = [(ABSENT + 1, COARSE.face_rows, 128)]
    fine_faces, coarse_faces = face_outs(FINE.face_rows), face_outs(COARSE.face_rows)
    sums = (2, CAP_NEW * 24, 128)

    source, coef, faces, ahead, back, level = call(
        gather_kernel, "collect", [fine, fine] + face_outs(BOTH_ROWS) + [coarse], [sums],
        (info, rhs_old, coef_old, before, after),
    )
    before, after = exchange(ahead, back)
    fine_g, fine_s, fine_d, coarse_g, coarse_w, coarse_d, row, u, faces, ahead, back = call(
        conduct_kernel, "conduct",
        [sds(CAP_NEW, 6, 24, FINE.width), fine, fine, sds(CAP_NEW, 6, 16, 256), coarse, coarse,
         sds(1, 128), fine] + fine_faces,
        [(ABSENT + 1, BOTH_ROWS, 128)],
        (info, source, coef, level, faces, before, after),
    )

    def sweep(lev, u, g, start, faces, ahead, back, name):
        before, after = exchange(ahead, back)
        return call(
            lambda *refs: sweep_kernel(lev, *refs), name,
            [fine, *fine_faces] if lev is FINE else [coarse, *coarse_faces],
            fine_table if lev is FINE else coarse_table,
            (info, u, g, start, faces, before, after),
        )

    u0, faces, ahead, back = sweep(FINE, u, fine_g, fine_s, faces, ahead, back, "pre")
    before, after = exchange(ahead, back)
    coarse_s, faces, ahead, back = call(
        residual_kernel, "residual", [coarse, *coarse_faces],
        fine_table + [(CAP_NEW, 24, FINE.width), sums],
        (info, u0, fine_g, fine_s, fine_d, coarse_w, faces, before, after),
    )
    e, faces, ahead, back = sweep(
        COARSE, coarse_s, coarse_g, coarse_s, faces, ahead, back, "coarse_pre"
    )
    before, after = exchange(ahead, back)
    rows = call(
        total_kernel, "totals", [sds(NCOARSE, 128)], coarse_table,
        (info, e, coarse_g, coarse_s, coarse_d, row, faces, before, after),
    )
    rows = lax.all_to_all(rows, "curve", 0, 0, tiled=True)
    e, faces, ahead, back = call(
        solve_kernel, "solve", [coarse, *coarse_faces], [], (info, rows, e)
    )
    e, faces, ahead, back = sweep(COARSE, e, coarse_g, coarse_s, faces, ahead, back, "coarse_post")
    before, after = exchange(ahead, back)
    u, faces, ahead, back = call(
        refine_kernel, "refine", [fine, *fine_faces],
        coarse_table + [(CAP_NEW, 16, 256), (FINE.tiles, 24, 128)],
        (info, e, coarse_g, coarse_s, faces, before, after, u0),
    )
    u, faces, ahead, back = sweep(FINE, u, fine_g, fine_s, faces, ahead, back, "post")
    before, after = exchange(ahead, back)
    return call(
        last_kernel, "last", [sds(CAP_NEW, 24, 576)], fine_table,
        (info, u, fine_g, fine_s, faces, before, after),
    )


def solution(mesh):
    in_specs = (
        P(("group", "curve"), None, None),
        P(("group", "curve"), None, None),
        P("group", None),
        P("group", None),
        P("group", None, None),
        P("group", None),
    )
    out_specs = P(("group", "curve"), None, None)
    return jax.shard_map(body, mesh=mesh, in_specs=in_specs, out_specs=out_specs, check_vma=False)
```

time: 330 us -> 155 us (0.47)
  other arithmetic: 62.9 us -> 0 us
  blocking collectives: 75.1 us -> 15.4 us
  local copies, waits for them, and re-layouts: 64.2 us -> 6.68 us
  waiting for transfers between devices: 59.4 us -> 19.6 us
  starting transfers between devices: 59.3 us -> 95.5 us
  Pallas kernels: 0 us -> 16.2 us
  between operations: 6.12 us -> 0.32 us
    psum x1 -> x0, blocking collectives: 47.7 us -> none  [from_root(): return lax.psum(block, axis)]
    ppermute x22 -> x20, waiting for transfers between devices: 59.4 us -> 19.6 us  [shifted(): return lax.ppermute(block, axis, route)]
    ppermute x22 -> x20, starting transfers between devices: 59.3 us -> 95.5 us  [shifted(): return lax.ppermute(block, axis, route)]
    all_gather x1 -> x0, blocking collectives: 27.3 us -> none  [body(): gathered = lax.all_gather(packed, 'curve', axis=0, tiled=True)]
    gather x39 -> x0, local copies, waits for them, and re-layouts: 23.2 us -> none  [the longest x10 6.87 us: ghost_faces(): forward = jnp.take(surface, rolled, axis=0)]
    reduce_sum x9 -> x0, other arithmetic: 23 us -> none  [the longest x2 16.2 us: coarsen(): grouped.mean(axis=(2, 4, 6))]
    pallas_call x0 -> x12, Pallas kernels: none -> 16.2 us  [call(): pl.pallas_call(kernel, out_shape=outs if many else outs[0], in_specs=in_s...]
    all_to_all x0 -> x1, blocking collectives: none -> 15.4 us  [body(): rows = lax.all_to_all(rows, 'curve', 0, 0, tiled=True)]
  transfers between devices with their start and end apart: 22 -> 20, of which waited for: 9 -> 11; matrix products, arithmetic and copies ran while one was open for 10% -> 0% of each run, Pallas kernels for 0% -> 0%
where the time goes in v1:
time: 155 us; the launch traced here: 154 us
  starting transfers between devices  95.5 us (62%)
  waiting for transfers between devices  19.6 us (13%)
  Pallas kernels  16.2 us (10%)
  blocking collectives  15.4 us (10%)
  local copies, waits for them, and re-layouts  6.68 us (4%)
    ppermute x20, starting transfers between devices, shifted(): return lax.ppermute(block, axis, route)  95.5 us
    ppermute x20, waiting for transfers between devices, shifted(): return lax.ppermute(block, axis, route)  19.6 us
    pallas_call x12, Pallas kernels, call(): pl.pallas_call(kernel, out_shape=outs if many else outs[0], in_specs=in_s...  16.2 us
    all_to_all x1, blocking collectives, body(): rows = lax.all_to_all(rows, 'curve', 0, 0, tiled=True)  15.4 us
    unnamed x16, local copies, waits for them, and re-layouts  6.68 us
  transfers between devices with their start and end apart: 20, of which 11 were waited for; matrix products, arithmetic and copies ran while one was open for 0% of the time, Pallas kernels for 0%

profile of v1, /device:TPU:24, one launch (start us, length us, event | category | flops | bytes accessed | tf_op | source)
XLA Modules:
  0.0 153.7 jit_solution(3888909859221175836)
XLA Ops:
  0.0 1.0 copy-done
  1.0 1.0 copy-done.2
  2.0 0.7 copy-done.4
  4.7 1.5 owners.1
  6.2 1.7 %collective-permute-start = (f32[2,24,576]{2,1,0:T(8,128)S(1)}, f32[2,24,576]{2,1,0:T(8,128)S(1)}, u32[]{:S(2)}, u32[]{:S(2)}) collective-permute-start(f32[2,24,576]{2,1,0:T(8,128)S(1)} %get-tuple-element.54), channel_id=1, source_target_pairs={{0,1},{1,2},{2,3},{3,4},{4,5},{5,6},{6,7},{7,8},{8,9},{9,10},{10,1... | collective-permute-start | bytes 331784 | tf_op jit(solution)/shard_map/ppermute | solution.py:428
  7.9 1.3 collective-permute-start.1
  9.2 3.6 %collective-permute-done.1.after = f32[2,24,576]{2,1,0:T(8,128)S(1)} collective-permute-done((f32[2,24,576]{2,1,0:T(8,128)S(1)}, f32[2,24,576]{2,1,0:T(8,128)S(1)}, u32[]{:S(2)}, u32[]{:S(2)}) %collective-permute-start.1) | collective-permute-done | bytes 110624 | tf_op jit(solution)/shard_map/ppermute | solution.py:428
  12.9 1.0 copy-done.1
  13.9 1.0 copy-done.3
  14.9 1.2 collect.1
  16.1 5.4 %collective-permute-start.2 = (f32[3,64,128]{2,1,0:T(8,128)S(1)}, f32[3,64,128]{2,1,0:T(8,128)S(1)}, u32[]{:S(2)}, u32[]{:S(2)}) collective-permute-start(f32[3,64,128]{2,1,0:T(8,128)S(1)} %get-tuple-element.60), channel_id=1, source_target_pairs={{0,1},{1,2},{2,3},{3,4},{4,5},{5,6},{6,7},{7,8},{8,9},{9,10},{10,1... | collective-permute-start | bytes 294920 | tf_op jit(solution)/shard_map/ppermute | solution.py:428
  21.4 8.6 %collective-permute-start.3 = (f32[3,64,128]{2,1,0:T(8,128)S(1)}, f32[3,64,128]{2,1,0:T(8,128)S(1)}, u32[]{:S(2)}, u32[]{:S(2)}) collective-permute-start(f32[3,64,128]{2,1,0:T(8,128)S(1)} %get-tuple-element.61), channel_id=1, source_target_pairs={{1,0},{2,1},{3,2},{4,3},{5,4},{6,5},{7,6},{8,7},{9,8},{10,9},{11,1... | collective-permute-start | bytes 294920 | tf_op jit(solution)/shard_map/ppermute | solution.py:428
  30.4 1.8 %collective-permute-done.3.after = f32[3,64,128]{2,1,0:T(8,128)S(1)} collective-permute-done((f32[3,64,128]{2,1,0:T(8,128)S(1)}, f32[3,64,128]{2,1,0:T(8,128)S(1)}, u32[]{:S(2)}, u32[]{:S(2)}) %collective-permute-start.3) | collective-permute-done | bytes 98336 | tf_op jit(solution)/shard_map/ppermute | solution.py:428
  32.2 1.9 %conduct.1 = (f32[5,6,24,640]{3,2,1,0:T(8,128)S(1)}, f32[5,24,640]{2,1,0:T(8,128)S(1)}, f32[5,24,640]{2,1,0:T(8,128)S(1)}, f32[5,6,16,256]{3,2,1,0:T(8,128)S(1)}...) custom-call(s32[128]{0:T(128)S(1)} %get-tuple-element.53.info.refs_0, ...), custom_call_target="tpu_custom_call" | custom-call | tf_op jit(solution)/shard_map/conduct/pallas_call | solution.py:414
  34.1 1.9 %collective-permute-start.4 = (f32[3,40,128]{2,1,0:T(8,128)S(1)}, f32[3,40,128]{2,1,0:T(8,128)S(1)}, u32[]{:S(2)}, u32[]{:S(2)}) collective-permute-start(f32[3,40,128]{2,1,0:T(8,128)S(1)} %get-tuple-element.66), channel_id=1, source_target_pairs={{0,1},{1,2},{2,3},{3,4},{4,5},{5,6},{6,7},{7,8},{8,9},{9,10},{10,1... | collective-permute-start | bytes 184328 | tf_op jit(solution)/shard_map/ppermute | solution.py:428
  36.0 8.0 %collective-permute-start.5 = (f32[3,40,128]{2,1,0:T(8,128)S(1)}, f32[3,40,128]{2,1,0:T(8,128)S(1)}, u32[]{:S(2)}, u32[]{:S(2)}) collective-permute-start(f32[3,40,128]{2,1,0:T(8,128)S(1)} %get-tuple-element.67), channel_id=1, source_target_pairs={{1,0},{2,1},{3,2},{4,3},{5,4},{6,5},{7,6},{8,7},{9,8},{10,9},{11,1... | collective-permute-start | bytes 184328 | tf_op jit(solution)/shard_map/ppermute | solution.py:428
  44.0 1.8 %collective-permute-done.5.refs_6_ = f32[3,40,128]{2,1,0:T(8,128)S(1)} collective-permute-done((f32[3,40,128]{2,1,0:T(8,128)S(1)}, f32[3,40,128]{2,1,0:T(8,128)S(1)}, u32[]{:S(2)}, u32[]{:S(2)}) %collective-permute-start.5) | collective-permute-done | bytes 61472 | tf_op jit(solution)/shard_map/ppermute | solution.py:428
  45.8 1.0 pre.1
  46.9 1.9 %collective-permute-start.6 = (f32[3,40,128]{2,1,0:T(8,128)S(1)}, f32[3,40,128]{2,1,0:T(8,128)S(1)}, u32[]{:S(2)}, u32[]{:S(2)}) collective-permute-start(f32[3,40,128]{2,1,0:T(8,128)S(1)} %get-tuple-element.72), channel_id=1, source_target_pairs={{0,1},{1,2},{2,3},{3,4},{4,5},{5,6},{6,7},{7,8},{8,9},{9,10},{10,1... | collective-permute-start | bytes 184328 | tf_op jit(solution)/shard_map/ppermute | solution.py:428
  48.8 7.9 %collective-permute-start.7 = (f32[3,40,128]{2,1,0:T(8,128)S(1)}, f32[3,40,128]{2,1,0:T(8,128)S(1)}, u32[]{:S(2)}, u32[]{:S(2)}) collective-permute-start(f32[3,40,128]{2,1,0:T(8,128)S(1)} %get-tuple-element.73), channel_id=1, source_target_pairs={{1,0},{2,1},{3,2},{4,3},{5,4},{6,5},{7,6},{8,7},{9,8},{10,9},{11,1... | collective-permute-start | bytes 184328 | tf_op jit(solution)/shard_map/ppermute | solution.py:428
  56.7 1.8 %collective-permute-done.7.after = f32[3,40,128]{2,1,0:T(8,128)S(1)} collective-permute-done((f32[3,40,128]{2,1,0:T(8,128)S(1)}, f32[3,40,128]{2,1,0:T(8,128)S(1)}, u32[]{:S(2)}, u32[]{:S(2)}) %collective-permute-start.7) | collective-permute-done | bytes 61472 | tf_op jit(solution)/shard_map/ppermute | solution.py:428
  58.6 1.5 residual.1
  60.0 1.9 %collective-permute-start.8 = (f32[3,24,128]{2,1,0:T(8,128)S(1)}, f32[3,24,128]{2,1,0:T(8,128)S(1)}, u32[]{:S(2)}, u32[]{:S(2)}) collective-permute-start(f32[3,24,128]{2,1,0:T(8,128)S(1)} %get-tuple-element.77), channel_id=1, source_target_pairs={{0,1},{1,2},{2,3},{3,4},{4,5},{5,6},{6,7},{7,8},{8,9},{9,10},{10,1... | collective-permute-start | bytes 110600 | tf_op jit(solution)/shard_map/ppermute | solution.py:428
  62.0 7.9 %collective-permute-start.9 = (f32[3,24,128]{2,1,0:T(8,128)S(1)}, f32[3,24,128]{2,1,0:T(8,128)S(1)}, u32[]{:S(2)}, u32[]{:S(2)}) collective-permute-start(f32[3,24,128]{2,1,0:T(8,128)S(1)} %get-tuple-element.78), channel_id=1, source_target_pairs={{1,0},{2,1},{3,2},{4,3},{5,4},{6,5},{7,6},{8,7},{9,8},{10,9},{11,1... | collective-permute-start | bytes 110600 | tf_op jit(solution)/shard_map/ppermute | solution.py:428
  69.9 1.6 %collective-permute-done.9.refs_6_ = f32[3,24,128]{2,1,0:T(8,128)S(1)} collective-permute-done((f32[3,24,128]{2,1,0:T(8,128)S(1)}, f32[3,24,128]{2,1,0:T(8,128)S(1)}, u32[]{:S(2)}, u32[]{:S(2)}) %collective-permute-start.9) | collective-permute-done | bytes 36896 | tf_op jit(solution)/shard_map/ppermute | solution.py:428
  71.5 0.8 coarse_pre.1
  72.3 1.9 %collective-permute-start.10 = (f32[3,24,128]{2,1,0:T(8,128)S(1)}, f32[3,24,128]{2,1,0:T(8,128)S(1)}, u32[]{:S(2)}, u32[]{:S(2)}) collective-permute-start(f32[3,24,128]{2,1,0:T(8,128)S(1)} %get-tuple-element.83), channel_id=1, source_target_pairs={{0,1},{1,2},{2,3},{3,4},{4,5},{5,6},{6,7},{7,8},{8,9},{9,10},{10,1... | collective-permute-start | bytes 110600 | tf_op jit(solution)/shard_map/ppermute | solution.py:428
  74.2 7.9 %collective-permute-start.11 = (f32[3,24,128]{2,1,0:T(8,128)S(1)}, f32[3,24,128]{2,1,0:T(8,128)S(1)}, u32[]{:S(2)}, u32[]{:S(2)}) collective-permute-start(f32[3,24,128]{2,1,0:T(8,128)S(1)} %get-tuple-element.84), channel_id=1, source_target_pairs={{1,0},{2,1},{3,2},{4,3},{5,4},{6,5},{7,6},{8,7},{9,8},{10,9},{11,1... | collective-permute-start | bytes 110600 | tf_op jit(solution)/shard_map/ppermute | solution.py:428
  82.1 1.6 %collective-permute-done.11.after = f32[3,24,128]{2,1,0:T(8,128)S(1)} collective-permute-done((f32[3,24,128]{2,1,0:T(8,128)S(1)}, f32[3,24,128]{2,1,0:T(8,128)S(1)}, u32[]{:S(2)}, u32[]{:S(2)}) %collective-permute-start.11) | collective-permute-done | bytes 36896 | tf_op jit(solution)/shard_map/ppermute | solution.py:428
  83.7 0.9 totals.1
  84.6 15.4 %all_to_all.11 = f32[32,1,128]{2,1,0:T(1,128)S(1)} all-to-all(f32[32,1,128]{2,1,0:T(1,128)S(1)} %bitcast.7), channel_id=1, replica_groups=mesh['group'=16,'curve'=32] {'curve'}, dimensions={0} | all-to-all | bytes 32768 | tf_op jit(solution)/shard_map/all_to_all | solution.py:494
  100.0 2.8 %solve.1 = (f32[5,16,256]{2,1,0:T(8,128)S(1)}, f32[5,24,128]{2,1,0:T(8,128)S(1)}, f32[3,24,128]{2,1,0:T(8,128)S(1)}, f32[3,24,128]{2,1,0:T(8,128)S(1)}) custom-call(s32[128]{0:T(128)S(1)} %get-tuple-element.53.info.refs_0_, f32[32,128]{1,0:T(8,128)S(1)} %bitcast.8, f32[5,16,256]{2,1,0:T(8,128)S(1)} %get-tuple-element.79.u_in), custom_call_target="tpu_custom_call" | custom-call | tf_op jit(solution)/shard_map/solve/pallas_call | solution.py:414
  102.8 1.9 %collective-permute-start.12 = (f32[3,24,128]{2,1,0:T(8,128)S(1)}, f32[3,24,128]{2,1,0:T(8,128)S(1)}, u32[]{:S(2)}, u32[]{:S(2)}) collective-permute-start(f32[3,24,128]{2,1,0:T(8,128)S(1)} %get-tuple-element.87), channel_id=1, source_target_pairs={{0,1},{1,2},{2,3},{3,4},{4,5},{5,6},{6,7},{7,8},{8,9},{9,10},{10,1... | collective-permute-start | bytes 110600 | tf_op jit(solution)/shard_map/ppermute | solution.py:428
  104.7 7.9 %collective-permute-start.13 = (f32[3,24,128]{2,1,0:T(8,128)S(1)}, f32[3,24,128]{2,1,0:T(8,128)S(1)}, u32[]{:S(2)}, u32[]{:S(2)}) collective-permute-start(f32[3,24,128]{2,1,0:T(8,128)S(1)} %get-tuple-element.88), channel_id=1, source_target_pairs={{1,0},{2,1},{3,2},{4,3},{5,4},{6,5},{7,6},{8,7},{9,8},{10,9},{11,1... | collective-permute-start | bytes 110600 | tf_op jit(solution)/shard_map/ppermute | solution.py:428
  112.6 1.6 %collective-permute-done.13.refs_6_ = f32[3,24,128]{2,1,0:T(8,128)S(1)} collective-permute-done((f32[3,24,128]{2,1,0:T(8,128)S(1)}, f32[3,24,128]{2,1,0:T(8,128)S(1)}, u32[]{:S(2)}, u32[]{:S(2)}) %collective-permute-start.13) | collective-permute-done | bytes 36896 | tf_op jit(solution)/shard_map/ppermute | solution.py:428
  114.2 0.8 coarse_post.1
  115.0 1.9 %collective-permute-start.14 = (f32[3,24,128]{2,1,0:T(8,128)S(1)}, f32[3,24,128]{2,1,0:T(8,128)S(1)}, u32[]{:S(2)}, u32[]{:S(2)}) collective-permute-start(f32[3,24,128]{2,1,0:T(8,128)S(1)} %get-tuple-element.91), channel_id=1, source_target_pairs={{0,1},{1,2},{2,3},{3,4},{4,5},{5,6},{6,7},{7,8},{8,9},{9,10},{10,1... | collective-permute-start | bytes 110600 | tf_op jit(solution)/shard_map/ppermute | solution.py:428
  117.0 7.9 %collective-permute-start.15 = (f32[3,24,128]{2,1,0:T(8,128)S(1)}, f32[3,24,128]{2,1,0:T(8,128)S(1)}, u32[]{:S(2)}, u32[]{:S(2)}) collective-permute-start(f32[3,24,128]{2,1,0:T(8,128)S(1)} %get-tuple-element.92), channel_id=1, source_target_pairs={{1,0},{2,1},{3,2},{4,3},{5,4},{6,5},{7,6},{8,7},{9,8},{10,9},{11,1... | collective-permute-start | bytes 110600 | tf_op jit(solution)/shard_map/ppermute | solution.py:428
  124.8 1.6 %collective-permute-done.15.after = f32[3,24,128]{2,1,0:T(8,128)S(1)} collective-permute-done((f32[3,24,128]{2,1,0:T(8,128)S(1)}, f32[3,24,128]{2,1,0:T(8,128)S(1)}, u32[]{:S(2)}, u32[]{:S(2)}) %collective-permute-start.15) | collective-permute-done | bytes 36896 | tf_op jit(solution)/shard_map/ppermute | solution.py:428
  126.4 1.0 refine.1
  127.5 1.9 %collective-permute-start.16 = (f32[3,40,128]{2,1,0:T(8,128)S(1)}, f32[3,40,128]{2,1,0:T(8,128)S(1)}, u32[]{:S(2)}, u32[]{:S(2)}) collective-permute-start(f32[3,40,128]{2,1,0:T(8,128)S(1)} %get-tuple-element.95), channel_id=1, source_target_pairs={{0,1},{1,2},{2,3},{3,4},{4,5},{5,6},{6,7},{7,8},{8,9},{9,10},{10,1... | collective-permute-start | bytes 184328 | tf_op jit(solution)/shard_map/ppermute | solution.py:428
  129.4 7.9 %collective-permute-start.17 = (f32[3,40,128]{2,1,0:T(8,128)S(1)}, f32[3,40,128]{2,1,0:T(8,128)S(1)}, u32[]{:S(2)}, u32[]{:S(2)}) collective-permute-start(f32[3,40,128]{2,1,0:T(8,128)S(1)} %get-tuple-element.96), channel_id=1, source_target_pairs={{1,0},{2,1},{3,2},{4,3},{5,4},{6,5},{7,6},{8,7},{9,8},{10,9},{11,1... | collective-permute-start | bytes 184328 | tf_op jit(solution)/shard_map/ppermute | solution.py:428
  137.3 1.8 %collective-permute-done.17.refs_6_ = f32[3,40,128]{2,1,0:T(8,128)S(1)} collective-permute-done((f32[3,40,128]{2,1,0:T(8,128)S(1)}, f32[3,40,128]{2,1,0:T(8,128)S(1)}, u32[]{:S(2)}, u32[]{:S(2)}) %collective-permute-start.17) | collective-permute-done | bytes 61472 | tf_op jit(solution)/shard_map/ppermute | solution.py:428
  139.1 1.1 post.1
  140.2 1.9 %collective-permute-start.18 = (f32[3,40,128]{2,1,0:T(8,128)S(1)}, f32[3,40,128]{2,1,0:T(8,128)S(1)}, u32[]{:S(2)}, u32[]{:S(2)}) collective-permute-start(f32[3,40,128]{2,1,0:T(8,128)S(1)} %get-tuple-element.99), channel_id=1, source_target_pairs={{0,1},{1,2},{2,3},{3,4},{4,5},{5,6},{6,7},{7,8},{8,9},{9,10},{10,1... | collective-permute-start | bytes 184328 | tf_op jit(solution)/shard_map/ppermute | solution.py:428
  142.1 7.9 %collective-permute-start.19 = (f32[3,40,128]{2,1,0:T(8,128)S(1)}, f32[3,40,128]{2,1,0:T(8,128)S(1)}, u32[]{:S(2)}, u32[]{:S(2)}) collective-permute-start(f32[3,40,128]{2,1,0:T(8,128)S(1)} %get-tuple-element.100), channel_id=1, source_target_pairs={{1,0},{2,1},{3,2},{4,3},{5,4},{6,5},{7,6},{8,7},{9,8},{10,9},{11,1... | collective-permute-start | bytes 184328 | tf_op jit(solution)/shard_map/ppermute | solution.py:428
  150.1 1.8 %collective-permute-done.19.after = f32[3,40,128]{2,1,0:T(8,128)S(1)} collective-permute-done((f32[3,40,128]{2,1,0:T(8,128)S(1)}, f32[3,40,128]{2,1,0:T(8,128)S(1)}, u32[]{:S(2)}, u32[]{:S(2)}) %collective-permute-start.19) | collective-permute-done | bytes 61472 | tf_op jit(solution)/shard_map/ppermute | solution.py:428
  151.9 1.8 %last.1 = f32[5,24,576]{2,1,0:T(8,128)} custom-call(s32[128]{0:T(128)S(1)} %get-tuple-element.53.info.refs_0_, f32[5,24,640]{2,1,0:T(8,128)S(1)} %get-tuple-element.97.u_in, f32[5,6,24,640]{3,2,1,0:T(8,128)S(1)} %get-tuple-element.63.refs_2_.g, f32[5,24,640]{2,1,0:T(8,128)S(1)} %get-tuple-element.64.refs_3_.start, ...), custom_call_target="tpu_custom_call" | custom-call | tf_op jit(solution)/shard_map/last/pallas_call | solution.py:414
  (21 shorter events, 2.4 us)
Async XLA Ops:
  0.0 1.0 copy-start
  1.0 1.0 copy-start.2
  2.0 0.7 copy-start.4
  2.7 0.7 copy-start.5
  3.4 0.7 copy-start.6
  4.0 0.7 copy-start.7
  6.2 3.1 %collective-permute-start = (f32[2,24,576]{2,1,0:T(8,128)S(1)}, f32[2,24,576]{2,1,0:T(8,128)S(1)}, u32[]{:S(2)}, u32[]{:S(2)}) collective-permute-start(f32[2,24,576]{2,1,0:T(8,128)S(1)} %get-tuple-element.54), channel_id=1, source_target_pairs={{0,1},{1,2},{2,3},{3,4},{4,5},{5,6},{6,7},{7,8},{8,9},{9,10},{10,1... | collective-permute-start | bytes 331784 | tf_op jit(solution)/shard_map/ppermute | solution.py:428
  7.9 4.9 %collective-permute-start.1 = (f32[2,24,576]{2,1,0:T(8,128)S(1)}, f32[2,24,576]{2,1,0:T(8,128)S(1)}, u32[]{:S(2)}, u32[]{:S(2)}) collective-permute-start(f32[2,24,576]{2,1,0:T(8,128)S(1)} %get-tuple-element.55), channel_id=1, source_target_pairs={{1,0},{2,1},{3,2},{4,3},{5,4},{6,5},{7,6},{8,7},{9,8},{10,9},{11,1... | collective-permute-start | bytes 331784 | tf_op jit(solution)/shard_map/ppermute | solution.py:428
  12.9 1.0 copy-start.1
  13.9 1.0 copy-start.3
  16.1 14.3 %collective-permute-start.2 = (f32[3,64,128]{2,1,0:T(8,128)S(1)}, f32[3,64,128]{2,1,0:T(8,128)S(1)}, u32[]{:S(2)}, u32[]{:S(2)}) collective-permute-start(f32[3,64,128]{2,1,0:T(8,128)S(1)} %get-tuple-element.60), channel_id=1, source_target_pairs={{0,1},{1,2},{2,3},{3,4},{4,5},{5,6},{6,7},{7,8},{8,9},{9,10},{10,1... | collective-permute-start | bytes 294920 | tf_op jit(solution)/shard_map/ppermute | solution.py:428
  21.4 10.7 %collective-permute-start.3 = (f32[3,64,128]{2,1,0:T(8,128)S(1)}, f32[3,64,128]{2,1,0:T(8,128)S(1)}, u32[]{:S(2)}, u32[]{:S(2)}) collective-permute-start(f32[3,64,128]{2,1,0:T(8,128)S(1)} %get-tuple-element.61), channel_id=1, source_target_pairs={{1,0},{2,1},{3,2},{4,3},{5,4},{6,5},{7,6},{8,7},{9,8},{10,9},{11,1... | collective-permute-start | bytes 294920 | tf_op jit(solution)/shard_map/ppermute | solution.py:428
  34.1 9.9 %collective-permute-start.4 = (f32[3,40,128]{2,1,0:T(8,128)S(1)}, f32[3,40,128]{2,1,0:T(8,128)S(1)}, u32[]{:S(2)}, u32[]{:S(2)}) collective-permute-start(f32[3,40,128]{2,1,0:T(8,128)S(1)} %get-tuple-element.66), channel_id=1, source_target_pairs={{0,1},{1,2},{2,3},{3,4},{4,5},{5,6},{6,7},{7,8},{8,9},{9,10},{10,1... | collective-permute-start | bytes 184328 | tf_op jit(solution)/shard_map/ppermute | solution.py:428
  36.0 9.8 %collective-permute-start.5 = (f32[3,40,128]{2,1,0:T(8,128)S(1)}, f32[3,40,128]{2,1,0:T(8,128)S(1)}, u32[]{:S(2)}, u32[]{:S(2)}) collective-permute-start(f32[3,40,128]{2,1,0:T(8,128)S(1)} %get-tuple-element.67), channel_id=1, source_target_pairs={{1,0},{2,1},{3,2},{4,3},{5,4},{6,5},{7,6},{8,7},{9,8},{10,9},{11,1... | collective-permute-start | bytes 184328 | tf_op jit(solution)/shard_map/ppermute | solution.py:428
  46.9 9.8 %collective-permute-start.6 = (f32[3,40,128]{2,1,0:T(8,128)S(1)}, f32[3,40,128]{2,1,0:T(8,128)S(1)}, u32[]{:S(2)}, u32[]{:S(2)}) collective-permute-start(f32[3,40,128]{2,1,0:T(8,128)S(1)} %get-tuple-element.72), channel_id=1, source_target_pairs={{0,1},{1,2},{2,3},{3,4},{4,5},{5,6},{6,7},{7,8},{8,9},{9,10},{10,1... | collective-permute-start | bytes 184328 | tf_op jit(solution)/shard_map/ppermute | solution.py:428
  48.8 9.8 %collective-permute-start.7 = (f32[3,40,128]{2,1,0:T(8,128)S(1)}, f32[3,40,128]{2,1,0:T(8,128)S(1)}, u32[]{:S(2)}, u32[]{:S(2)}) collective-permute-start(f32[3,40,128]{2,1,0:T(8,128)S(1)} %get-tuple-element.73), channel_id=1, source_target_pairs={{1,0},{2,1},{3,2},{4,3},{5,4},{6,5},{7,6},{8,7},{9,8},{10,9},{11,1... | collective-permute-start | bytes 184328 | tf_op jit(solution)/shard_map/ppermute | solution.py:428
  60.0 9.8 %collective-permute-start.8 = (f32[3,24,128]{2,1,0:T(8,128)S(1)}, f32[3,24,128]{2,1,0:T(8,128)S(1)}, u32[]{:S(2)}, u32[]{:S(2)}) collective-permute-start(f32[3,24,128]{2,1,0:T(8,128)S(1)} %get-tuple-element.77), channel_id=1, source_target_pairs={{0,1},{1,2},{2,3},{3,4},{4,5},{5,6},{6,7},{7,8},{8,9},{9,10},{10,1... | collective-permute-start | bytes 110600 | tf_op jit(solution)/shard_map/ppermute | solution.py:428
  62.0 9.5 %collective-permute-start.9 = (f32[3,24,128]{2,1,0:T(8,128)S(1)}, f32[3,24,128]{2,1,0:T(8,128)S(1)}, u32[]{:S(2)}, u32[]{:S(2)}) collective-permute-start(f32[3,24,128]{2,1,0:T(8,128)S(1)} %get-tuple-element.78), channel_id=1, source_target_pairs={{1,0},{2,1},{3,2},{4,3},{5,4},{6,5},{7,6},{8,7},{9,8},{10,9},{11,1... | collective-permute-start | bytes 110600 | tf_op jit(solution)/shard_map/ppermute | solution.py:428
  72.3 9.8 %collective-permute-start.10 = (f32[3,24,128]{2,1,0:T(8,128)S(1)}, f32[3,24,128]{2,1,0:T(8,128)S(1)}, u32[]{:S(2)}, u32[]{:S(2)}) collective-permute-start(f32[3,24,128]{2,1,0:T(8,128)S(1)} %get-tuple-element.83), channel_id=1, source_target_pairs={{0,1},{1,2},{2,3},{3,4},{4,5},{5,6},{6,7},{7,8},{8,9},{9,10},{10,1... | collective-permute-start | bytes 110600 | tf_op jit(solution)/shard_map/ppermute | solution.py:428
  74.2 9.5 %collective-permute-start.11 = (f32[3,24,128]{2,1,0:T(8,128)S(1)}, f32[3,24,128]{2,1,0:T(8,128)S(1)}, u32[]{:S(2)}, u32[]{:S(2)}) collective-permute-start(f32[3,24,128]{2,1,0:T(8,128)S(1)} %get-tuple-element.84), channel_id=1, source_target_pairs={{1,0},{2,1},{3,2},{4,3},{5,4},{6,5},{7,6},{8,7},{9,8},{10,9},{11,1... | collective-permute-start | bytes 110600 | tf_op jit(solution)/shard_map/ppermute | solution.py:428
  102.8 9.8 %collective-permute-start.12 = (f32[3,24,128]{2,1,0:T(8,128)S(1)}, f32[3,24,128]{2,1,0:T(8,128)S(1)}, u32[]{:S(2)}, u32[]{:S(2)}) collective-permute-start(f32[3,24,128]{2,1,0:T(8,128)S(1)} %get-tuple-element.87), channel_id=1, source_target_pairs={{0,1},{1,2},{2,3},{3,4},{4,5},{5,6},{6,7},{7,8},{8,9},{9,10},{10,1... | collective-permute-start | bytes 110600 | tf_op jit(solution)/shard_map/ppermute | solution.py:428
  104.7 9.5 %collective-permute-start.13 = (f32[3,24,128]{2,1,0:T(8,128)S(1)}, f32[3,24,128]{2,1,0:T(8,128)S(1)}, u32[]{:S(2)}, u32[]{:S(2)}) collective-permute-start(f32[3,24,128]{2,1,0:T(8,128)S(1)} %get-tuple-element.88), channel_id=1, source_target_pairs={{1,0},{2,1},{3,2},{4,3},{5,4},{6,5},{7,6},{8,7},{9,8},{10,9},{11,1... | collective-permute-start | bytes 110600 | tf_op jit(solution)/shard_map/ppermute | solution.py:428
  115.0 9.8 %collective-permute-start.14 = (f32[3,24,128]{2,1,0:T(8,128)S(1)}, f32[3,24,128]{2,1,0:T(8,128)S(1)}, u32[]{:S(2)}, u32[]{:S(2)}) collective-permute-start(f32[3,24,128]{2,1,0:T(8,128)S(1)} %get-tuple-element.91), channel_id=1, source_target_pairs={{0,1},{1,2},{2,3},{3,4},{4,5},{5,6},{6,7},{7,8},{8,9},{9,10},{10,1... | collective-permute-start | bytes 110600 | tf_op jit(solution)/shard_map/ppermute | solution.py:428
  117.0 9.5 %collective-permute-start.15 = (f32[3,24,128]{2,1,0:T(8,128)S(1)}, f32[3,24,128]{2,1,0:T(8,128)S(1)}, u32[]{:S(2)}, u32[]{:S(2)}) collective-permute-start(f32[3,24,128]{2,1,0:T(8,128)S(1)} %get-tuple-element.92), channel_id=1, source_target_pairs={{1,0},{2,1},{3,2},{4,3},{5,4},{6,5},{7,6},{8,7},{9,8},{10,9},{11,1... | collective-permute-start | bytes 110600 | tf_op jit(solution)/shard_map/ppermute | solution.py:428
  127.5 9.8 %collective-permute-start.16 = (f32[3,40,128]{2,1,0:T(8,128)S(1)}, f32[3,40,128]{2,1,0:T(8,128)S(1)}, u32[]{:S(2)}, u32[]{:S(2)}) collective-permute-start(f32[3,40,128]{2,1,0:T(8,128)S(1)} %get-tuple-element.95), channel_id=1, source_target_pairs={{0,1},{1,2},{2,3},{3,4},{4,5},{5,6},{6,7},{7,8},{8,9},{9,10},{10,1... | collective-permute-start | bytes 184328 | tf_op jit(solution)/shard_map/ppermute | solution.py:428
  129.4 9.7 %collective-permute-start.17 = (f32[3,40,128]{2,1,0:T(8,128)S(1)}, f32[3,40,128]{2,1,0:T(8,128)S(1)}, u32[]{:S(2)}, u32[]{:S(2)}) collective-permute-start(f32[3,40,128]{2,1,0:T(8,128)S(1)} %get-tuple-element.96), channel_id=1, source_target_pairs={{1,0},{2,1},{3,2},{4,3},{5,4},{6,5},{7,6},{8,7},{9,8},{10,9},{11,1... | collective-permute-start | bytes 184328 | tf_op jit(solution)/shard_map/ppermute | solution.py:428
  140.2 9.8 %collective-permute-start.18 = (f32[3,40,128]{2,1,0:T(8,128)S(1)}, f32[3,40,128]{2,1,0:T(8,128)S(1)}, u32[]{:S(2)}, u32[]{:S(2)}) collective-permute-start(f32[3,40,128]{2,1,0:T(8,128)S(1)} %get-tuple-element.99), channel_id=1, source_target_pairs={{0,1},{1,2},{2,3},{3,4},{4,5},{5,6},{6,7},{7,8},{8,9},{9,10},{10,1... | collective-permute-start | bytes 184328 | tf_op jit(solution)/shard_map/ppermute | solution.py:428
  142.1 9.8 %collective-permute-start.19 = (f32[3,40,128]{2,1,0:T(8,128)S(1)}, f32[3,40,128]{2,1,0:T(8,128)S(1)}, u32[]{:S(2)}, u32[]{:S(2)}) collective-permute-start(f32[3,40,128]{2,1,0:T(8,128)S(1)} %get-tuple-element.100), channel_id=1, source_target_pairs={{1,0},{2,1},{3,2},{4,3},{5,4},{6,5},{7,6},{8,7},{9,8},{10,9},{11,1... | collective-permute-start | bytes 184328 | tf_op jit(solution)/shard_map/ppermute | solution.py:428

commit v2 on v1

--- a/solution.py
+++ b/solution.py
@@ -17,6 +17,7 @@
 I32 = jnp.int32
 
 HELD, PICK, TABLE, CELL, BAND = 0, 1, 8, 32, 40
+SEND_X, SEND_Y, AT_X, AT_Y = 64, 65, 66, 67
 ABSENT = 2 * REACH + CAP_NEW
 
 
@@ -31,7 +32,7 @@
 
 
 FINE = Level(24, 24, 640, 40, 24, 32, 40, 1.0)
-COARSE = Level(12, 16, 256, 68, 16, 20, 24, 0.25)
+COARSE = Level(12, 16, 256, 68, 12, 14, 16, 0.25)
 BOTH_ROWS = FINE.face_rows + COARSE.face_rows
 
 
@@ -57,17 +58,19 @@
         faces[k, high : high + 1, :] = field[lev.side - 1 : lev.side, part]
 
 
-def send_faces(info, faces, ahead, back):
-    first = jnp.maximum(info[HELD] - REACH, 0)
+def send_faces(info, faces, x_out, y_out):
+    x_first, y_first = info[SEND_X], info[SEND_Y]
     for j in range(REACH):
-        ahead[j] = faces[first + j]
-        back[j] = faces[j]
-
-
-def fill_table(table, before, faces, after):
-    table[0:REACH] = before[...]
+        x_out[j] = faces[x_first + j]
+        y_out[j] = faces[y_first + j]
+
+
+def fill_table(info, table, x_in, faces, y_in):
+    x_first, y_first = info[AT_X], info[AT_Y]
+    for j in range(REACH):
+        table[x_first + j] = x_in[j]
+        table[y_first + j] = y_in[j]
     table[REACH : REACH + CAP_NEW] = faces[...]
-    table[REACH + CAP_NEW : ABSENT] = after[...]
     table[ABSENT] = jnp.zeros(table.shape[1:], F32)
 
 
@@ -175,9 +178,22 @@
     return 0.125 * jnp.concatenate(halves, axis=1)
 
 
-def first_kernel(new_ref, old_ref, near_ref, map_ref, rhs_ref, coef_ref, ahead, back, info):
+def first_kernel(
+    new_in, old_in, near_in, map_in, rhs_in, coef_in,
+    x_out, y_out, info, rhs_ref, coef_ref, new_ref, old_ref, near_ref, map_ref, sems,
+):
+    pairs = (
+        (new_in, new_ref), (old_in, old_ref), (near_in, near_ref), (map_in, map_ref),
+        (rhs_in, rhs_ref), (coef_in, coef_ref),
+    )
+    copies = [pltpu.make_async_copy(a, b, sems.at[i]) for i, (a, b) in enumerate(pairs)]
+    for copy in copies:
+        copy.start()
     curve = lax.axis_index("curve")
     group = lax.axis_index("group")
+    up = lax.rem(curve, 2) == 1
+    for copy in copies[:4]:
+        copy.wait()
     new, old = new_ref[...], old_ref[...]
 
     def count(mask):
@@ -186,17 +202,25 @@
     new_first, held = count(new < curve), count(new == curve)
     old_first, old_count = count(old < curve), count(old == curve)
     last = jnp.clip(old_count - 1, 0, CAP_OLD - 1)
-    ahead[0] = rhs_ref[last]
-    ahead[1] = coef_ref[last]
-    back[0] = rhs_ref[0]
-    back[1] = coef_ref[0]
+    x_slot, y_slot = jnp.where(up, last, 0), jnp.where(up, 0, last)
+    for copy in copies[4:]:
+        copy.wait()
+    x_out[0] = rhs_ref[x_slot]
+    x_out[1] = coef_ref[x_slot]
+    y_out[0] = rhs_ref[y_slot]
+    y_out[1] = coef_ref[y_slot]
     info[HELD] = held
+    final = jnp.maximum(held - REACH, 0)
+    info[SEND_X], info[SEND_Y] = jnp.where(up, final, 0), jnp.where(up, 0, final)
+    info[AT_X] = jnp.where(up, REACH + CAP_NEW, 0)
+    info[AT_Y] = jnp.where(up, 0, REACH + CAP_NEW)
+    from_next, from_previous = jnp.where(up, 0, CAP_OLD + 1), jnp.where(up, CAP_OLD + 1, 0)
     first_id = group * NBG + new_first
     finish = first_id + held
     for k in range(CAP_NEW):
         block = new_first + k
-        pick = jnp.where(block >= old_first + old_count, CAP_OLD + 1, 1 + block - old_first)
-        pick = jnp.where(block < old_first, 0, pick)
+        pick = jnp.where(block >= old_first + old_count, from_next, 1 + block - old_first)
+        pick = jnp.where(block < old_first, from_previous, pick)
         info[PICK + k] = jnp.clip(pick, 0, CAP_OLD + 1)
         occupied = k < held
         safe = jnp.clip(block, 0, NBG - 1)
@@ -215,7 +239,7 @@
 
 
 def gather_kernel(
-    info, rhs_ref, coef_ref, before, after, source, coef, faces, ahead, back, level, scratch
+    info, rhs_ref, coef_ref, x_in, y_in, source, coef, faces, x_out, y_out, level, scratch
 ):
     source[...] = jnp.zeros(source.shape, F32)
     coef[...] = jnp.ones(coef.shape, F32)
@@ -224,8 +248,8 @@
         slot = jnp.clip(pick - 1, 0, CAP_OLD - 1)
         occupied = k < info[HELD]
         for i, (table, out, rest) in enumerate(((rhs_ref, source, 0.0), (coef_ref, coef, 1.0))):
-            block = jnp.where(pick == 0, before[i], table[slot])
-            block = jnp.where(pick == CAP_OLD + 1, after[i], block)
+            block = jnp.where(pick == 0, x_in[i], table[slot])
+            block = jnp.where(pick == CAP_OLD + 1, y_in[i], block)
             out[k, :, 0:576] = jnp.where(occupied, block, rest)
     coarsen_blocks(coef[...].reshape(CAP_NEW * 24, FINE.width), scratch)
     row, lane = iota((16, 256), 0), iota((16, 256), 1)
@@ -235,14 +259,14 @@
         level[k, 0:12, :] = coarse_rows(scratch, k)
         level[k] = jnp.where((row < 12) & (lane < 144), level[k], 1.0)
         pack_faces(COARSE, level[k], faces, k, FINE.face_rows)
-    send_faces(info, faces, ahead, back)
+    send_faces(info, faces, x_out, y_out)
 
 
 def conduct_kernel(
-    info, source, coef, level, faces_in, before, after,
-    fine_g, fine_s, fine_d, coarse_g, coarse_w, coarse_d, row_out, u, faces, ahead, back, table,
+    info, source, coef, level, faces_in, x_in, y_in,
+    fine_g, fine_s, fine_d, coarse_g, coarse_w, coarse_d, row_out, u, faces, x_out, y_out, table,
 ):
-    fill_table(table, before, faces_in, after)
+    fill_table(info, table, x_in, faces_in, y_in)
     lane_row = iota((1, 128), 1)
     band = jnp.zeros((1, 128), F32)
     for k in range(CAP_NEW):
@@ -278,25 +302,25 @@
             band -= jnp.where(lane_row == info[BAND + 4 * k + f], face[f], 0.0)
         band += jnp.where(lane_row == 64 + k, info[CELL + k].astype(F32), 0.0)
     row_out[...] = band
-    send_faces(info, faces, ahead, back)
-
-
-def sweep_kernel(lev, info, u_in, g, start, faces_in, before, after, u, faces, ahead, back, table):
-    fill_table(table, before, faces_in, after)
+    send_faces(info, faces, x_out, y_out)
+
+
+def sweep_kernel(lev, info, u_in, g, start, faces_in, x_in, y_in, u, faces, x_out, y_out, table):
+    fill_table(info, table, x_in, faces_in, y_in)
     for k in range(CAP_NEW):
         field = u_in[k]
         ghosts = ghosts_of(lev, info, table, k, 0)
         new = KEEP * field + (start[k] + neighbour_sum(lev, field, g.at[k], ghosts))
         u[k] = new
         pack_faces(lev, new, faces, k, 0)
-    send_faces(info, faces, ahead, back)
+    send_faces(info, faces, x_out, y_out)
 
 
 def residual_kernel(
-    info, u_in, g, start, diagonal, weight, faces_in, before, after,
-    coarse_s, faces, ahead, back, table, rest, scratch,
+    info, u_in, g, start, diagonal, weight, faces_in, x_in, y_in,
+    coarse_s, faces, x_out, y_out, table, rest, scratch,
 ):
-    fill_table(table, before, faces_in, after)
+    fill_table(info, table, x_in, faces_in, y_in)
     for k in range(CAP_NEW):
         field = u_in[k]
         ghosts = ghosts_of(FINE, info, table, k, 0)
@@ -307,11 +331,11 @@
         coarse_s[k] = jnp.zeros((16, 256), F32)
         coarse_s[k, 0:12, :] = weight[k, 0:12, :] * coarse_rows(scratch, k)
         pack_faces(COARSE, coarse_s[k], faces, k, 0)
-    send_faces(info, faces, ahead, back)
-
-
-def total_kernel(info, u_in, g, start, diagonal, row_in, faces_in, before, after, rows_out, table):
-    fill_table(table, before, faces_in, after)
+    send_faces(info, faces, x_out, y_out)
+
+
+def total_kernel(info, u_in, g, start, diagonal, row_in, faces_in, x_in, y_in, rows_out, table):
+    fill_table(info, table, x_in, faces_in, y_in)
     lane_row = iota((1, 128), 1)
     row, lane = iota((16, 256), 0), iota((16, 256), 1)
     inside = (row < 12) & (lane < 144)
@@ -326,7 +350,7 @@
     rows_out[...] = jnp.broadcast_to(band, rows_out.shape)
 
 
-def solve_kernel(info, rows_in, u_in, u, faces, ahead, back):
+def solve_kernel(info, rows_in, u_in, u, faces, x_out, y_out):
     rows = rows_in[...]
     shape = (NCOARSE, 128)
     row, lane = iota(shape, 0), iota(shape, 1)
@@ -364,13 +388,13 @@
         new = u_in[k] + jnp.where(inside, lift, 0.0)
         u[k] = new
         pack_faces(COARSE, new, faces, k, 0)
-    send_faces(info, faces, ahead, back)
+    send_faces(info, faces, x_out, y_out)
 
 
 def refine_kernel(
-    info, e_in, g, start, faces_in, before, after, u_in, u, faces, ahead, back, table, coarse, rest
+    info, e_in, g, start, faces_in, x_in, y_in, u_in, u, faces, x_out, y_out, table, coarse, rest
 ):
-    fill_table(table, before, faces_in, after)
+    fill_table(info, table, x_in, faces_in, y_in)
     for k in range(CAP_NEW):
         field = e_in[k]
         ghosts = ghosts_of(COARSE, info, table, k, 0)
@@ -389,11 +413,11 @@
         new = u_in[k] + jnp.concatenate([rest[t] for t in range(FINE.tiles)], axis=1)
         u[k] = new
         pack_faces(FINE, new, faces, k, 0)
-    send_faces(info, faces, ahead, back)
-
-
-def last_kernel(info, u_in, g, start, faces_in, before, after, out, table):
-    fill_table(table, before, faces_in, after)
+    send_faces(info, faces, x_out, y_out)
+
+
+def last_kernel(info, u_in, g, start, faces_in, x_in, y_in, out, table):
+    fill_table(info, table, x_in, faces_in, y_in)
     for k in range(CAP_NEW):
         field = u_in[k]
         ghosts = ghosts_of(FINE, info, table, k, 0)
@@ -405,31 +429,33 @@
     return jax.ShapeDtypeStruct(shape, F32)
 
 
+ROOM = 63
 SMEM = pl.BlockSpec(memory_space=pltpu.SMEM)
 VMEM = pl.BlockSpec(memory_space=pltpu.VMEM)
-
-
-def call(kernel, name, outs, scratch, args, in_specs=None, out_specs=None):
+HBM = pl.BlockSpec(memory_space=pltpu.HBM)
+
+
+def call(kernel, name, outs, scratch, args, in_specs=None, out_specs=None, room=24):
     many = len(outs) > 1
     return pl.pallas_call(
         kernel,
         out_shape=outs if many else outs[0],
         in_specs=in_specs or [SMEM] + [VMEM] * (len(args) - 1),
         out_specs=out_specs or ([VMEM] * len(outs) if many else VMEM),
-        scratch_shapes=[pltpu.VMEM(s, F32) for s in scratch],
-        compiler_params=pltpu.CompilerParams(vmem_limit_bytes=24 * 1024 * 1024),
+        scratch_shapes=[pltpu.VMEM(s, F32) if isinstance(s, tuple) else s for s in scratch],
+        compiler_params=pltpu.CompilerParams(vmem_limit_bytes=room * 1024 * 1024),
         name=name,
     )(*args)
 
 
-def shifted(block, axis, distance):
-    devices = range(lax.axis_size(axis))
-    route = [(i - distance, i) for i in devices if i - distance in devices]
-    return lax.ppermute(block, axis, route)
-
-
-def exchange(ahead, back):
-    return shifted(ahead, AXES, 1), shifted(back, AXES, -1)
+def swap(block, axis, first):
+    starts = range(first, lax.axis_size(axis) - 1, 2)
+    return lax.ppermute(block, axis, [(i, i + 1) for i in starts] + [(i + 1, i) for i in starts])
+
+
+def exchange(x_out, y_out, axis=AXES):
+    x_in = swap(x_out, axis, 1)
+    return x_in, swap(y_out, axis, 0)
 
 
 def face_outs(rows):
@@ -438,14 +464,19 @@
 
 def body(rhs_old, coef_old, old_owner, new_owner, neighbours, coarse_map):
     near = jnp.transpose(neighbours[0])
-    pair = sds(2, 24, 576)
-    ahead, back, info = call(
+    pair, old = sds(2, 24, 576), sds(CAP_OLD, 24, 576)
+    x_out, y_out, info, rhs_old, coef_old = call(
         first_kernel, "owners",
-        [pair, pair, jax.ShapeDtypeStruct((128,), I32)], [],
+        [pair, pair, jax.ShapeDtypeStruct((128,), I32), old, old],
+        [
+            pltpu.VMEM((1, 128), I32), pltpu.VMEM((1, 128), I32),
+            pltpu.SMEM((4, 128), I32), pltpu.SMEM((1, 128), I32),
+            pltpu.SemaphoreType.DMA((6,)),
+        ],
         (new_owner, old_owner, near, coarse_map, rhs_old, coef_old),
-        [VMEM, VMEM, SMEM, SMEM, VMEM, VMEM], [VMEM, VMEM, SMEM],
-    )
-    before, after = shifted(ahead, "curve", 1), shifted(back, "curve", -1)
+        [HBM] * 6, [VMEM, VMEM, SMEM, VMEM, VMEM], ROOM,
+    )
+    x_in, y_in = exchange(x_out, y_out, "curve")
 
     fine = sds(CAP_NEW, 24, FINE.width)
     coarse = sds(CAP_NEW, 16, 256)
@@ -454,59 +485,59 @@
     fine_faces, coarse_faces = face_outs(FINE.face_rows), face_outs(COARSE.face_rows)
     sums = (2, CAP_NEW * 24, 128)
 
-    source, coef, faces, ahead, back, level = call(
+    source, coef, faces, x_out, y_out, level = call(
         gather_kernel, "collect", [fine, fine] + face_outs(BOTH_ROWS) + [coarse], [sums],
-        (info, rhs_old, coef_old, before, after),
-    )
-    before, after = exchange(ahead, back)
-    fine_g, fine_s, fine_d, coarse_g, coarse_w, coarse_d, row, u, faces, ahead, back = call(
+        (info, rhs_old, coef_old, x_in, y_in),
+    )
+    x_in, y_in = exchange(x_out, y_out)
+    fine_g, fine_s, fine_d, coarse_g, coarse_w, coarse_d, row, u, faces, x_out, y_out = call(
         conduct_kernel, "conduct",
         [sds(CAP_NEW, 6, 24, FINE.width), fine, fine, sds(CAP_NEW, 6, 16, 256), coarse, coarse,
          sds(1, 128), fine] + fine_faces,
         [(ABSENT + 1, BOTH_ROWS, 128)],
-        (info, source, coef, level, faces, before, after),
-    )
-
-    def sweep(lev, u, g, start, faces, ahead, back, name):
-        before, after = exchange(ahead, back)
+        (info, source, coef, level, faces, x_in, y_in),
+    )
+
+    def sweep(lev, u, g, start, faces, x_out, y_out, name):
+        x_in, y_in = exchange(x_out, y_out)
         return call(
             lambda *refs: sweep_kernel(lev, *refs), name,
             [fine, *fine_faces] if lev is FINE else [coarse, *coarse_faces],
             fine_table if lev is FINE else coarse_table,
-            (info, u, g, start, faces, before, after),
+            (info, u, g, start, faces, x_in, y_in),
         )
 
-    u0, faces, ahead, back = sweep(FINE, u, fine_g, fine_s, faces, ahead, back, "pre")
-    before, after = exchange(ahead, back)
-    coarse_s, faces, ahead, back = call(
+    u0, faces, x_out, y_out = sweep(FINE, u, fine_g, fine_s, faces, x_out, y_out, "pre")
+    x_in, y_in = exchange(x_out, y_out)
+    coarse_s, faces, x_out, y_out = call(
         residual_kernel, "residual", [coarse, *coarse_faces],
         fine_table + [(CAP_NEW, 24, FINE.width), sums],
-        (info, u0, fine_g, fine_s, fine_d, coarse_w, faces, before, after),
-    )
-    e, faces, ahead, back = sweep(
-        COARSE, coarse_s, coarse_g, coarse_s, faces, ahead, back, "coarse_pre"
-    )
-    before, after = exchange(ahead, back)
+        (info, u0, fine_g, fine_s, fine_d, coarse_w, faces, x_in, y_in),
+    )
+    e, faces, x_out, y_out = sweep(
+        COARSE, coarse_s, coarse_g, coarse_s, faces, x_out, y_out, "coarse_pre"
+    )
+    x_in, y_in = exchange(x_out, y_out)
     rows = call(
         total_kernel, "totals", [sds(NCOARSE, 128)], coarse_table,
-        (info, e, coarse_g, coarse_s, coarse_d, row, faces, before, after),
+        (info, e, coarse_g, coarse_s, coarse_d, row, faces, x_in, y_in),
     )
     rows = lax.all_to_all(rows, "curve", 0, 0, tiled=True)
-    e, faces, ahead, back = call(
+    e, faces, x_out, y_out = call(
         solve_kernel, "solve", [coarse, *coarse_faces], [], (info, rows, e)
     )
-    e, faces, ahead, back = sweep(COARSE, e, coarse_g, coarse_s, faces, ahead, back, "coarse_post")
-    before, after = exchange(ahead, back)
-    u, faces, ahead, back = call(
+    e, faces, x_out, y_out = sweep(COARSE, e, coarse_g, coarse_s, faces, x_out, y_out, "coarse_post")
+    x_in, y_in = exchange(x_out, y_out)
+    u, faces, x_out, y_out = call(
         refine_kernel, "refine", [fine, *fine_faces],
         coarse_table + [(CAP_NEW, 16, 256), (FINE.tiles, 24, 128)],
-        (info, e, coarse_g, coarse_s, faces, before, after, u0),
-    )
-    u, faces, ahead, back = sweep(FINE, u, fine_g, fine_s, faces, ahead, back, "post")
-    before, after = exchange(ahead, back)
+        (info, e, coarse_g, coarse_s, faces, x_in, y_in, u0),
+    )
+    u, faces, x_out, y_out = sweep(FINE, u, fine_g, fine_s, faces, x_out, y_out, "post")
+    x_in, y_in = exchange(x_out, y_out)
     return call(
         last_kernel, "last", [sds(CAP_NEW, 24, 576)], fine_table,
-        (info, u, fine_g, fine_s, faces, before, after),
+        (info, u, fine_g, fine_s, faces, x_in, y_in),
     )
 
 

time: 155 us -> 135 us (0.87)
  starting transfers between devices: 95.5 us -> 80.4 us
  local copies, waits for them, and re-layouts: 6.68 us -> 2.61 us
    ppermute x20, starting transfers between devices: 95.5 us -> 80.4 us  [swap(): lax.ppermute(block, axis, [(i, i + 1) for i in starts] + [(i + 1, i) for...]
    unnamed x16 -> x6, local copies, waits for them, and re-layouts: 6.68 us -> 2.61 us
  transfers between devices with their start and end apart: 20 -> 20, of which waited for: 11 -> 13; matrix products, arithmetic and copies ran while one was open for 0% -> 0% of each run, Pallas kernels for 0% -> 0%
where the time goes in v2:
time: 135 us
  starting transfers between devices  80.4 us (60%)
  waiting for transfers between devices  19 us (14%)
  Pallas kernels  17.1 us (13%)
  blocking collectives  15.4 us (11%)
  local copies, waits for them, and re-layouts  2.61 us (2%)
    ppermute x20, starting transfers between devices, swap(): lax.ppermute(block, axis, [(i, i + 1) for i in starts] + [(i + 1, i) for...  80.4 us
    ppermute x20, waiting for transfers between devices, swap(): lax.ppermute(block, axis, [(i, i + 1) for i in starts] + [(i + 1, i) for...  19 us
    pallas_call x12, Pallas kernels, call(): pl.pallas_call(kernel, out_shape=outs if many else outs[0], in_specs=in_s...  17.1 us
    all_to_all x1, blocking collectives, body(): rows = lax.all_to_all(rows, 'curve', 0, 0, tiled=True)  15.4 us
  transfers between devices with their start and end apart: 20, of which 13 were waited for; matrix products, arithmetic and copies ran while one was open for 0% of the time, Pallas kernels for 0%

profile of v2, /device:TPU:24, one launch (start us, length us, event | category | flops | bytes accessed | tf_op | source)
XLA Modules:
  0.0 134.7 jit_solution(10305152588848155151)
XLA Ops:
  0.0 2.3 %owners.1 = (f32[2,24,576]{2,1,0:T(8,128)}, f32[2,24,576]{2,1,0:T(8,128)}, s32[128]{0:T(128)}, f32[7,24,576]{2,1,0:T(8,128)}, f32[7,24,576]{2,1,0:T(8,128)}) custom-call(s32[1,128]{1,0:T(1,128)} %new_in.1, s32[1,128]{1,0:T(1,128)} %old_in.1, s32[4,128]{1,0:T(4,128)} %bitcast.9, s32[1,128]{1,0:T(1,128)} %map_in.1, f32[7,24,576]{2,1,0:T(8,128)} %rhs_in.1, ...), custom_call_target="tpu_custom_call" | custom-call | tf_op jit(solution)/shard_map/owners/pallas_call | solution.py:440
  2.3 0.7 collective-permute-start
  3.0 5.2 %collective-permute-start.1 = (f32[2,24,576]{2,1,0:T(8,128)}, f32[2,24,576]{2,1,0:T(8,128)S(1)}, u32[]{:S(2)}, u32[]{:S(2)}) collective-permute-start(f32[2,24,576]{2,1,0:T(8,128)} %get-tuple-element.59), channel_id=1, source_target_pairs={{0,1},{2,3},{4,5},{6,7},{8,9},{10,11},{12,13},{14,15},{16,17},{18,... | collective-permute-start | bytes 331784 | tf_op jit(solution)/shard_map/ppermute | solution.py:453
  8.2 1.2 collective-permute-done.1.y_in
  9.3 1.0 copy-done
  10.4 1.0 copy-done.1
  11.4 0.6 copy-done.2
  12.0 1.2 collect.1
  13.1 12.3 %collective-permute-start.2 = (f32[3,56,128]{2,1,0:T(8,128)S(1)}, f32[3,56,128]{2,1,0:T(8,128)S(1)}, u32[]{:S(2)}, u32[]{:S(2)}) collective-permute-start(f32[3,56,128]{2,1,0:T(8,128)S(1)} %get-tuple-element.64), channel_id=1, source_target_pairs={{1,2},{3,4},{5,6},{7,8},{9,10},{11,12},{13,14},{15,16},{17,18},{19... | collective-permute-start | bytes 258056 | tf_op jit(solution)/shard_map/ppermute | solution.py:453
  25.4 1.9 %collective-permute-start.3 = (f32[3,56,128]{2,1,0:T(8,128)S(1)}, f32[3,56,128]{2,1,0:T(8,128)S(1)}, u32[]{:S(2)}, u32[]{:S(2)}) collective-permute-start(f32[3,56,128]{2,1,0:T(8,128)S(1)} %get-tuple-element.65), channel_id=1, source_target_pairs={{0,1},{2,3},{4,5},{6,7},{8,9},{10,11},{12,13},{14,15},{16,17},{18,... | collective-permute-start | bytes 258056 | tf_op jit(solution)/shard_map/ppermute | solution.py:453
  27.6 1.0 collective-permute-done.3.y_in
  28.6 1.9 %conduct.1 = (f32[5,6,24,640]{3,2,1,0:T(8,128)S(1)}, f32[5,24,640]{2,1,0:T(8,128)S(1)}, f32[5,24,640]{2,1,0:T(8,128)S(1)}, f32[5,6,16,256]{3,2,1,0:T(8,128)S(1)}...) custom-call(s32[128]{0:T(128)S(1)} %copy-done.2, ...), custom_call_target="tpu_custom_call" | custom-call | tf_op jit(solution)/shard_map/conduct/pallas_call | solution.py:440
  30.5 6.8 %collective-permute-start.4 = (f32[3,40,128]{2,1,0:T(8,128)S(1)}, f32[3,40,128]{2,1,0:T(8,128)S(1)}, u32[]{:S(2)}, u32[]{:S(2)}) collective-permute-start(f32[3,40,128]{2,1,0:T(8,128)S(1)} %get-tuple-element.70), channel_id=1, source_target_pairs={{1,2},{3,4},{5,6},{7,8},{9,10},{11,12},{13,14},{15,16},{17,18},{19... | collective-permute-start | bytes 184328 | tf_op jit(solution)/shard_map/ppermute | solution.py:453
  37.4 1.9 %collective-permute-start.5 = (f32[3,40,128]{2,1,0:T(8,128)S(1)}, f32[3,40,128]{2,1,0:T(8,128)S(1)}, u32[]{:S(2)}, u32[]{:S(2)}) collective-permute-start(f32[3,40,128]{2,1,0:T(8,128)S(1)} %get-tuple-element.71), channel_id=1, source_target_pairs={{0,1},{2,3},{4,5},{6,7},{8,9},{10,11},{12,13},{14,15},{16,17},{18,... | collective-permute-start | bytes 184328 | tf_op jit(solution)/shard_map/ppermute | solution.py:453
  39.3 1.0 collective-permute-done.4.refs_5_
  40.3 0.2 collective-permute-done.5.refs_6_
  40.5 1.1 pre.1
  41.6 6.6 %collective-permute-start.6 = (f32[3,40,128]{2,1,0:T(8,128)S(1)}, f32[3,40,128]{2,1,0:T(8,128)S(1)}, u32[]{:S(2)}, u32[]{:S(2)}) collective-permute-start(f32[3,40,128]{2,1,0:T(8,128)S(1)} %get-tuple-element.76), channel_id=1, source_target_pairs={{1,2},{3,4},{5,6},{7,8},{9,10},{11,12},{13,14},{15,16},{17,18},{19... | collective-permute-start | bytes 184328 | tf_op jit(solution)/shard_map/ppermute | solution.py:453
  48.2 1.9 %collective-permute-start.7 = (f32[3,40,128]{2,1,0:T(8,128)S(1)}, f32[3,40,128]{2,1,0:T(8,128)S(1)}, u32[]{:S(2)}, u32[]{:S(2)}) collective-permute-start(f32[3,40,128]{2,1,0:T(8,128)S(1)} %get-tuple-element.77), channel_id=1, source_target_pairs={{0,1},{2,3},{4,5},{6,7},{8,9},{10,11},{12,13},{14,15},{16,17},{18,... | collective-permute-start | bytes 184328 | tf_op jit(solution)/shard_map/ppermute | solution.py:453
  50.1 1.2 collective-permute-done.6.x_in
  51.4 1.5 %residual.1 = (f32[5,16,256]{2,1,0:T(8,128)S(1)}, f32[5,16,128]{2,1,0:T(8,128)S(1)}, f32[3,16,128]{2,1,0:T(8,128)S(1)}, f32[3,16,128]{2,1,0:T(8,128)S(1)}) custom-call(s32[128]{0:T(128)S(1)} %copy-done.2, f32[5,24,640]{2,1,0:T(8,128)S(1)} %get-tuple-element.72.u_in, f32[5,6,24,640]{3,2,1,0:T(8,128)S(1)} %get-tuple-element.67.refs_2_.g, ...), custom_call_target="tpu_custom_call" | custom-call | tf_op jit(solution)/shard_map/residual/pallas_call | solution.py:440
  52.8 6.6 %collective-permute-start.8 = (f32[3,16,128]{2,1,0:T(8,128)S(1)}, f32[3,16,128]{2,1,0:T(8,128)S(1)}, u32[]{:S(2)}, u32[]{:S(2)}) collective-permute-start(f32[3,16,128]{2,1,0:T(8,128)S(1)} %get-tuple-element.81), channel_id=1, source_target_pairs={{1,2},{3,4},{5,6},{7,8},{9,10},{11,12},{13,14},{15,16},{17,18},{19... | collective-permute-start | bytes 73736 | tf_op jit(solution)/shard_map/ppermute | solution.py:453
  59.4 1.9 %collective-permute-start.9 = (f32[3,16,128]{2,1,0:T(8,128)S(1)}, f32[3,16,128]{2,1,0:T(8,128)S(1)}, u32[]{:S(2)}, u32[]{:S(2)}) collective-permute-start(f32[3,16,128]{2,1,0:T(8,128)S(1)} %get-tuple-element.82), channel_id=1, source_target_pairs={{0,1},{2,3},{4,5},{6,7},{8,9},{10,11},{12,13},{14,15},{16,17},{18,... | collective-permute-start | bytes 73736 | tf_op jit(solution)/shard_map/ppermute | solution.py:453
  61.4 0.8 collective-permute-done.8.refs_5_
  62.2 0.3 collective-permute-done.9.refs_6_
  62.5 0.8 coarse_pre.1
  63.3 6.3 %collective-permute-start.10 = (f32[3,16,128]{2,1,0:T(8,128)S(1)}, f32[3,16,128]{2,1,0:T(8,128)S(1)}, u32[]{:S(2)}, u32[]{:S(2)}) collective-permute-start(f32[3,16,128]{2,1,0:T(8,128)S(1)} %get-tuple-element.87), channel_id=1, source_target_pairs={{1,2},{3,4},{5,6},{7,8},{9,10},{11,12},{13,14},{15,16},{17,18},{19... | collective-permute-start | bytes 73736 | tf_op jit(solution)/shard_map/ppermute | solution.py:453
  69.6 1.9 %collective-permute-start.11 = (f32[3,16,128]{2,1,0:T(8,128)S(1)}, f32[3,16,128]{2,1,0:T(8,128)S(1)}, u32[]{:S(2)}, u32[]{:S(2)}) collective-permute-start(f32[3,16,128]{2,1,0:T(8,128)S(1)} %get-tuple-element.88), channel_id=1, source_target_pairs={{0,1},{2,3},{4,5},{6,7},{8,9},{10,11},{12,13},{14,15},{16,17},{18,... | collective-permute-start | bytes 73736 | tf_op jit(solution)/shard_map/ppermute | solution.py:453
  71.6 1.2 collective-permute-done.10.x_in
  72.7 0.9 totals.1
  73.6 15.4 %all_to_all.11 = f32[32,1,128]{2,1,0:T(1,128)S(1)} all-to-all(f32[32,1,128]{2,1,0:T(1,128)S(1)} %bitcast.7), channel_id=1, replica_groups=mesh['group'=16,'curve'=32] {'curve'}, dimensions={0} | all-to-all | bytes 32768 | tf_op jit(solution)/shard_map/all_to_all | solution.py:525
  89.0 2.8 %solve.1 = (f32[5,16,256]{2,1,0:T(8,128)S(1)}, f32[5,16,128]{2,1,0:T(8,128)S(1)}, f32[3,16,128]{2,1,0:T(8,128)S(1)}, f32[3,16,128]{2,1,0:T(8,128)S(1)}) custom-call(s32[128]{0:T(128)S(1)} %copy-done.2, f32[32,128]{1,0:T(8,128)S(1)} %bitcast.8, f32[5,16,256]{2,1,0:T(8,128)S(1)} %get-tuple-element.83.u_in), custom_call_target="tpu_custom_call" | custom-call | tf_op jit(solution)/shard_map/solve/pallas_call | solution.py:440
  91.8 4.7 %collective-permute-start.12 = (f32[3,16,128]{2,1,0:T(8,128)S(1)}, f32[3,16,128]{2,1,0:T(8,128)S(1)}, u32[]{:S(2)}, u32[]{:S(2)}) collective-permute-start(f32[3,16,128]{2,1,0:T(8,128)S(1)} %get-tuple-element.91), channel_id=1, source_target_pairs={{1,2},{3,4},{5,6},{7,8},{9,10},{11,12},{13,14},{15,16},{17,18},{19... | collective-permute-start | bytes 73736 | tf_op jit(solution)/shard_map/ppermute | solution.py:453
  96.4 1.9 %collective-permute-start.13 = (f32[3,16,128]{2,1,0:T(8,128)S(1)}, f32[3,16,128]{2,1,0:T(8,128)S(1)}, u32[]{:S(2)}, u32[]{:S(2)}) collective-permute-start(f32[3,16,128]{2,1,0:T(8,128)S(1)} %get-tuple-element.92), channel_id=1, source_target_pairs={{0,1},{2,3},{4,5},{6,7},{8,9},{10,11},{12,13},{14,15},{16,17},{18,... | collective-permute-start | bytes 73736 | tf_op jit(solution)/shard_map/ppermute | solution.py:453
  98.4 2.8 %collective-permute-done.12.refs_5_ = f32[3,16,128]{2,1,0:T(8,128)S(1)} collective-permute-done((f32[3,16,128]{2,1,0:T(8,128)S(1)}, f32[3,16,128]{2,1,0:T(8,128)S(1)}, u32[]{:S(2)}, u32[]{:S(2)}) %collective-permute-start.12) | collective-permute-done | bytes 24608 | tf_op jit(solution)/shard_map/ppermute | solution.py:453
  101.1 0.8 coarse_post.1
  101.9 4.7 %collective-permute-start.14 = (f32[3,16,128]{2,1,0:T(8,128)S(1)}, f32[3,16,128]{2,1,0:T(8,128)S(1)}, u32[]{:S(2)}, u32[]{:S(2)}) collective-permute-start(f32[3,16,128]{2,1,0:T(8,128)S(1)} %get-tuple-element.95), channel_id=1, source_target_pairs={{1,2},{3,4},{5,6},{7,8},{9,10},{11,12},{13,14},{15,16},{17,18},{19... | collective-permute-start | bytes 73736 | tf_op jit(solution)/shard_map/ppermute | solution.py:453
  106.6 1.9 %collective-permute-start.15 = (f32[3,16,128]{2,1,0:T(8,128)S(1)}, f32[3,16,128]{2,1,0:T(8,128)S(1)}, u32[]{:S(2)}, u32[]{:S(2)}) collective-permute-start(f32[3,16,128]{2,1,0:T(8,128)S(1)} %get-tuple-element.96), channel_id=1, source_target_pairs={{0,1},{2,3},{4,5},{6,7},{8,9},{10,11},{12,13},{14,15},{16,17},{18,... | collective-permute-start | bytes 73736 | tf_op jit(solution)/shard_map/ppermute | solution.py:453
  108.5 2.8 %collective-permute-done.14.x_in = f32[3,16,128]{2,1,0:T(8,128)S(1)} collective-permute-done((f32[3,16,128]{2,1,0:T(8,128)S(1)}, f32[3,16,128]{2,1,0:T(8,128)S(1)}, u32[]{:S(2)}, u32[]{:S(2)}) %collective-permute-start.14) | collective-permute-done | bytes 24608 | tf_op jit(solution)/shard_map/ppermute | solution.py:453
  111.3 1.0 refine.1
  112.3 4.7 %collective-permute-start.16 = (f32[3,40,128]{2,1,0:T(8,128)S(1)}, f32[3,40,128]{2,1,0:T(8,128)S(1)}, u32[]{:S(2)}, u32[]{:S(2)}) collective-permute-start(f32[3,40,128]{2,1,0:T(8,128)S(1)} %get-tuple-element.99), channel_id=1, source_target_pairs={{1,2},{3,4},{5,6},{7,8},{9,10},{11,12},{13,14},{15,16},{17,18},{19... | collective-permute-start | bytes 184328 | tf_op jit(solution)/shard_map/ppermute | solution.py:453
  117.0 1.9 %collective-permute-start.17 = (f32[3,40,128]{2,1,0:T(8,128)S(1)}, f32[3,40,128]{2,1,0:T(8,128)S(1)}, u32[]{:S(2)}, u32[]{:S(2)}) collective-permute-start(f32[3,40,128]{2,1,0:T(8,128)S(1)} %get-tuple-element.100), channel_id=1, source_target_pairs={{0,1},{2,3},{4,5},{6,7},{8,9},{10,11},{12,13},{14,15},{16,17},{18,... | collective-permute-start | bytes 184328 | tf_op jit(solution)/shard_map/ppermute | solution.py:453
  118.9 3.2 %collective-permute-done.16.refs_5_ = f32[3,40,128]{2,1,0:T(8,128)S(1)} collective-permute-done((f32[3,40,128]{2,1,0:T(8,128)S(1)}, f32[3,40,128]{2,1,0:T(8,128)S(1)}, u32[]{:S(2)}, u32[]{:S(2)}) %collective-permute-start.16) | collective-permute-done | bytes 61472 | tf_op jit(solution)/shard_map/ppermute | solution.py:453
  122.1 1.1 post.1
  123.2 4.7 %collective-permute-start.18 = (f32[3,40,128]{2,1,0:T(8,128)S(1)}, f32[3,40,128]{2,1,0:T(8,128)S(1)}, u32[]{:S(2)}, u32[]{:S(2)}) collective-permute-start(f32[3,40,128]{2,1,0:T(8,128)S(1)} %get-tuple-element.103), channel_id=1, source_target_pairs={{1,2},{3,4},{5,6},{7,8},{9,10},{11,12},{13,14},{15,16},{17,18},{19... | collective-permute-start | bytes 184328 | tf_op jit(solution)/shard_map/ppermute | solution.py:453
  127.9 1.9 %collective-permute-start.19 = (f32[3,40,128]{2,1,0:T(8,128)S(1)}, f32[3,40,128]{2,1,0:T(8,128)S(1)}, u32[]{:S(2)}, u32[]{:S(2)}) collective-permute-start(f32[3,40,128]{2,1,0:T(8,128)S(1)} %get-tuple-element.104), channel_id=1, source_target_pairs={{0,1},{2,3},{4,5},{6,7},{8,9},{10,11},{12,13},{14,15},{16,17},{18,... | collective-permute-start | bytes 184328 | tf_op jit(solution)/shard_map/ppermute | solution.py:453
  129.8 3.2 %collective-permute-done.18.x_in = f32[3,40,128]{2,1,0:T(8,128)S(1)} collective-permute-done((f32[3,40,128]{2,1,0:T(8,128)S(1)}, f32[3,40,128]{2,1,0:T(8,128)S(1)}, u32[]{:S(2)}, u32[]{:S(2)}) %collective-permute-start.18) | collective-permute-done | bytes 61472 | tf_op jit(solution)/shard_map/ppermute | solution.py:453
  133.0 1.8 %last.1 = f32[5,24,576]{2,1,0:T(8,128)} custom-call(s32[128]{0:T(128)S(1)} %copy-done.2, f32[5,24,640]{2,1,0:T(8,128)S(1)} %get-tuple-element.101.u_in, f32[5,6,24,640]{3,2,1,0:T(8,128)S(1)} %get-tuple-element.67.refs_2_.g, f32[5,24,640]{2,1,0:T(8,128)S(1)} %get-tuple-element.68.refs_3_.start, f32[5,40,128]{2,1,0:T(8,128)S(1)} %get-tuple-element.102.faces_in, ...), custom_call_target="tpu_custom_call" | custom-call | tf_op jit(solution)/shard_map/last/pallas_call | solution.py:440
  (11 shorter events, 0.3 us)
Async XLA Ops:
  2.3 5.9 %collective-permute-start = (f32[2,24,576]{2,1,0:T(8,128)}, f32[2,24,576]{2,1,0:T(8,128)S(1)}, u32[]{:S(2)}, u32[]{:S(2)}) collective-permute-start(f32[2,24,576]{2,1,0:T(8,128)} %get-tuple-element.58), channel_id=1, source_target_pairs={{1,2},{3,4},{5,6},{7,8},{9,10},{11,12},{13,14},{15,16},{17,18},{19... | collective-permute-start | bytes 331784 | tf_op jit(solution)/shard_map/ppermute | solution.py:453
  3.0 6.4 %collective-permute-start.1 = (f32[2,24,576]{2,1,0:T(8,128)}, f32[2,24,576]{2,1,0:T(8,128)S(1)}, u32[]{:S(2)}, u32[]{:S(2)}) collective-permute-start(f32[2,24,576]{2,1,0:T(8,128)} %get-tuple-element.59), channel_id=1, source_target_pairs={{0,1},{2,3},{4,5},{6,7},{8,9},{10,11},{12,13},{14,15},{16,17},{18,... | collective-permute-start | bytes 331784 | tf_op jit(solution)/shard_map/ppermute | solution.py:453
  9.3 1.0 copy-start
  10.4 1.0 copy-start.1
  11.4 0.6 copy-start.2
  13.1 14.5 %collective-permute-start.2 = (f32[3,56,128]{2,1,0:T(8,128)S(1)}, f32[3,56,128]{2,1,0:T(8,128)S(1)}, u32[]{:S(2)}, u32[]{:S(2)}) collective-permute-start(f32[3,56,128]{2,1,0:T(8,128)S(1)} %get-tuple-element.64), channel_id=1, source_target_pairs={{1,2},{3,4},{5,6},{7,8},{9,10},{11,12},{13,14},{15,16},{17,18},{19... | collective-permute-start | bytes 258056 | tf_op jit(solution)/shard_map/ppermute | solution.py:453
  25.4 3.2 %collective-permute-start.3 = (f32[3,56,128]{2,1,0:T(8,128)S(1)}, f32[3,56,128]{2,1,0:T(8,128)S(1)}, u32[]{:S(2)}, u32[]{:S(2)}) collective-permute-start(f32[3,56,128]{2,1,0:T(8,128)S(1)} %get-tuple-element.65), channel_id=1, source_target_pairs={{0,1},{2,3},{4,5},{6,7},{8,9},{10,11},{12,13},{14,15},{16,17},{18,... | collective-permute-start | bytes 258056 | tf_op jit(solution)/shard_map/ppermute | solution.py:453
  30.5 9.8 %collective-permute-start.4 = (f32[3,40,128]{2,1,0:T(8,128)S(1)}, f32[3,40,128]{2,1,0:T(8,128)S(1)}, u32[]{:S(2)}, u32[]{:S(2)}) collective-permute-start(f32[3,40,128]{2,1,0:T(8,128)S(1)} %get-tuple-element.70), channel_id=1, source_target_pairs={{1,2},{3,4},{5,6},{7,8},{9,10},{11,12},{13,14},{15,16},{17,18},{19... | collective-permute-start | bytes 184328 | tf_op jit(solution)/shard_map/ppermute | solution.py:453
  37.4 3.1 %collective-permute-start.5 = (f32[3,40,128]{2,1,0:T(8,128)S(1)}, f32[3,40,128]{2,1,0:T(8,128)S(1)}, u32[]{:S(2)}, u32[]{:S(2)}) collective-permute-start(f32[3,40,128]{2,1,0:T(8,128)S(1)} %get-tuple-element.71), channel_id=1, source_target_pairs={{0,1},{2,3},{4,5},{6,7},{8,9},{10,11},{12,13},{14,15},{16,17},{18,... | collective-permute-start | bytes 184328 | tf_op jit(solution)/shard_map/ppermute | solution.py:453
  41.6 9.8 %collective-permute-start.6 = (f32[3,40,128]{2,1,0:T(8,128)S(1)}, f32[3,40,128]{2,1,0:T(8,128)S(1)}, u32[]{:S(2)}, u32[]{:S(2)}) collective-permute-start(f32[3,40,128]{2,1,0:T(8,128)S(1)} %get-tuple-element.76), channel_id=1, source_target_pairs={{1,2},{3,4},{5,6},{7,8},{9,10},{11,12},{13,14},{15,16},{17,18},{19... | collective-permute-start | bytes 184328 | tf_op jit(solution)/shard_map/ppermute | solution.py:453
  48.2 3.1 %collective-permute-start.7 = (f32[3,40,128]{2,1,0:T(8,128)S(1)}, f32[3,40,128]{2,1,0:T(8,128)S(1)}, u32[]{:S(2)}, u32[]{:S(2)}) collective-permute-start(f32[3,40,128]{2,1,0:T(8,128)S(1)} %get-tuple-element.77), channel_id=1, source_target_pairs={{0,1},{2,3},{4,5},{6,7},{8,9},{10,11},{12,13},{14,15},{16,17},{18,... | collective-permute-start | bytes 184328 | tf_op jit(solution)/shard_map/ppermute | solution.py:453
  52.8 9.4 %collective-permute-start.8 = (f32[3,16,128]{2,1,0:T(8,128)S(1)}, f32[3,16,128]{2,1,0:T(8,128)S(1)}, u32[]{:S(2)}, u32[]{:S(2)}) collective-permute-start(f32[3,16,128]{2,1,0:T(8,128)S(1)} %get-tuple-element.81), channel_id=1, source_target_pairs={{1,2},{3,4},{5,6},{7,8},{9,10},{11,12},{13,14},{15,16},{17,18},{19... | collective-permute-start | bytes 73736 | tf_op jit(solution)/shard_map/ppermute | solution.py:453
  59.4 3.1 %collective-permute-start.9 = (f32[3,16,128]{2,1,0:T(8,128)S(1)}, f32[3,16,128]{2,1,0:T(8,128)S(1)}, u32[]{:S(2)}, u32[]{:S(2)}) collective-permute-start(f32[3,16,128]{2,1,0:T(8,128)S(1)} %get-tuple-element.82), channel_id=1, source_target_pairs={{0,1},{2,3},{4,5},{6,7},{8,9},{10,11},{12,13},{14,15},{16,17},{18,... | collective-permute-start | bytes 73736 | tf_op jit(solution)/shard_map/ppermute | solution.py:453
  63.3 9.4 %collective-permute-start.10 = (f32[3,16,128]{2,1,0:T(8,128)S(1)}, f32[3,16,128]{2,1,0:T(8,128)S(1)}, u32[]{:S(2)}, u32[]{:S(2)}) collective-permute-start(f32[3,16,128]{2,1,0:T(8,128)S(1)} %get-tuple-element.87), channel_id=1, source_target_pairs={{1,2},{3,4},{5,6},{7,8},{9,10},{11,12},{13,14},{15,16},{17,18},{19... | collective-permute-start | bytes 73736 | tf_op jit(solution)/shard_map/ppermute | solution.py:453
  69.6 3.1 %collective-permute-start.11 = (f32[3,16,128]{2,1,0:T(8,128)S(1)}, f32[3,16,128]{2,1,0:T(8,128)S(1)}, u32[]{:S(2)}, u32[]{:S(2)}) collective-permute-start(f32[3,16,128]{2,1,0:T(8,128)S(1)} %get-tuple-element.88), channel_id=1, source_target_pairs={{0,1},{2,3},{4,5},{6,7},{8,9},{10,11},{12,13},{14,15},{16,17},{18,... | collective-permute-start | bytes 73736 | tf_op jit(solution)/shard_map/ppermute | solution.py:453
  91.8 9.4 %collective-permute-start.12 = (f32[3,16,128]{2,1,0:T(8,128)S(1)}, f32[3,16,128]{2,1,0:T(8,128)S(1)}, u32[]{:S(2)}, u32[]{:S(2)}) collective-permute-start(f32[3,16,128]{2,1,0:T(8,128)S(1)} %get-tuple-element.91), channel_id=1, source_target_pairs={{1,2},{3,4},{5,6},{7,8},{9,10},{11,12},{13,14},{15,16},{17,18},{19... | collective-permute-start | bytes 73736 | tf_op jit(solution)/shard_map/ppermute | solution.py:453
  96.4 4.7 %collective-permute-start.13 = (f32[3,16,128]{2,1,0:T(8,128)S(1)}, f32[3,16,128]{2,1,0:T(8,128)S(1)}, u32[]{:S(2)}, u32[]{:S(2)}) collective-permute-start(f32[3,16,128]{2,1,0:T(8,128)S(1)} %get-tuple-element.92), channel_id=1, source_target_pairs={{0,1},{2,3},{4,5},{6,7},{8,9},{10,11},{12,13},{14,15},{16,17},{18,... | collective-permute-start | bytes 73736 | tf_op jit(solution)/shard_map/ppermute | solution.py:453
  101.9 9.4 %collective-permute-start.14 = (f32[3,16,128]{2,1,0:T(8,128)S(1)}, f32[3,16,128]{2,1,0:T(8,128)S(1)}, u32[]{:S(2)}, u32[]{:S(2)}) collective-permute-start(f32[3,16,128]{2,1,0:T(8,128)S(1)} %get-tuple-element.95), channel_id=1, source_target_pairs={{1,2},{3,4},{5,6},{7,8},{9,10},{11,12},{13,14},{15,16},{17,18},{19... | collective-permute-start | bytes 73736 | tf_op jit(solution)/shard_map/ppermute | solution.py:453
  106.6 4.7 %collective-permute-start.15 = (f32[3,16,128]{2,1,0:T(8,128)S(1)}, f32[3,16,128]{2,1,0:T(8,128)S(1)}, u32[]{:S(2)}, u32[]{:S(2)}) collective-permute-start(f32[3,16,128]{2,1,0:T(8,128)S(1)} %get-tuple-element.96), channel_id=1, source_target_pairs={{0,1},{2,3},{4,5},{6,7},{8,9},{10,11},{12,13},{14,15},{16,17},{18,... | collective-permute-start | bytes 73736 | tf_op jit(solution)/shard_map/ppermute | solution.py:453
  112.3 9.8 %collective-permute-start.16 = (f32[3,40,128]{2,1,0:T(8,128)S(1)}, f32[3,40,128]{2,1,0:T(8,128)S(1)}, u32[]{:S(2)}, u32[]{:S(2)}) collective-permute-start(f32[3,40,128]{2,1,0:T(8,128)S(1)} %get-tuple-element.99), channel_id=1, source_target_pairs={{1,2},{3,4},{5,6},{7,8},{9,10},{11,12},{13,14},{15,16},{17,18},{19... | collective-permute-start | bytes 184328 | tf_op jit(solution)/shard_map/ppermute | solution.py:453
  117.0 5.1 %collective-permute-start.17 = (f32[3,40,128]{2,1,0:T(8,128)S(1)}, f32[3,40,128]{2,1,0:T(8,128)S(1)}, u32[]{:S(2)}, u32[]{:S(2)}) collective-permute-start(f32[3,40,128]{2,1,0:T(8,128)S(1)} %get-tuple-element.100), channel_id=1, source_target_pairs={{0,1},{2,3},{4,5},{6,7},{8,9},{10,11},{12,13},{14,15},{16,17},{18,... | collective-permute-start | bytes 184328 | tf_op jit(solution)/shard_map/ppermute | solution.py:453
  123.2 9.8 %collective-permute-start.18 = (f32[3,40,128]{2,1,0:T(8,128)S(1)}, f32[3,40,128]{2,1,0:T(8,128)S(1)}, u32[]{:S(2)}, u32[]{:S(2)}) collective-permute-start(f32[3,40,128]{2,1,0:T(8,128)S(1)} %get-tuple-element.103), channel_id=1, source_target_pairs={{1,2},{3,4},{5,6},{7,8},{9,10},{11,12},{13,14},{15,16},{17,18},{19... | collective-permute-start | bytes 184328 | tf_op jit(solution)/shard_map/ppermute | solution.py:453
  127.9 5.1 %collective-permute-start.19 = (f32[3,40,128]{2,1,0:T(8,128)S(1)}, f32[3,40,128]{2,1,0:T(8,128)S(1)}, u32[]{:S(2)}, u32[]{:S(2)}) collective-permute-start(f32[3,40,128]{2,1,0:T(8,128)S(1)} %get-tuple-element.104), channel_id=1, source_target_pairs={{0,1},{2,3},{4,5},{6,7},{8,9},{10,11},{12,13},{14,15},{16,17},{18,... | collective-permute-start | bytes 184328 | tf_op jit(solution)/shard_map/ppermute | solution.py:453

commit v3 on v2

--- a/solution.py
+++ b/solution.py
@@ -180,7 +180,7 @@
 
 def first_kernel(
     new_in, old_in, near_in, map_in, rhs_in, coef_in,
-    x_out, y_out, info, rhs_ref, coef_ref, new_ref, old_ref, near_ref, map_ref, sems,
+    y_out, x_out, info, rhs_ref, coef_ref, new_ref, old_ref, near_ref, map_ref, sems,
 ):
     pairs = (
         (new_in, new_ref), (old_in, old_ref), (near_in, near_ref), (map_in, map_ref),
@@ -238,37 +238,49 @@
             info[BAND + 4 * k + f] = jnp.where(inside, 8 * k + 3 + other - cell, -1)
 
 
-def gather_kernel(
-    info, rhs_ref, coef_ref, x_in, y_in, source, coef, faces, x_out, y_out, level, scratch
-):
+def place_kernel(info, rhs_ref, coef_ref, source, coef):
     source[...] = jnp.zeros(source.shape, F32)
     coef[...] = jnp.ones(coef.shape, F32)
     for k in range(CAP_NEW):
-        pick = info[PICK + k]
-        slot = jnp.clip(pick - 1, 0, CAP_OLD - 1)
+        slot = jnp.clip(info[PICK + k] - 1, 0, CAP_OLD - 1)
         occupied = k < info[HELD]
-        for i, (table, out, rest) in enumerate(((rhs_ref, source, 0.0), (coef_ref, coef, 1.0))):
-            block = jnp.where(pick == 0, x_in[i], table[slot])
-            block = jnp.where(pick == CAP_OLD + 1, y_in[i], block)
-            out[k, :, 0:576] = jnp.where(occupied, block, rest)
+        source[k, :, 0:576] = jnp.where(occupied, rhs_ref[slot], 0.0)
+        coef[k, :, 0:576] = jnp.where(occupied, coef_ref[slot], 1.0)
+
+
+def patched(info, field, i, k, x_in, y_in):
+    pick = info[PICK + k]
+    occupied = k < info[HELD]
+    block = jnp.where(occupied & (pick == 0), x_in[i], field[k, :, 0:576])
+    return jnp.where(occupied & (pick == CAP_OLD + 1), y_in[i], block)
+
+
+def collect_kernel(info, kept, y_in, x_in, coef, faces, x_out, y_out):
+    coef[...] = kept[...]
+    for k in range(CAP_NEW):
+        coef[k, :, 0:576] = patched(info, kept, 1, k, x_in, y_in)
+        pack_faces(FINE, coef[k], faces, k, 0)
+    send_faces(info, faces, x_out, y_out)
+
+
+def level_kernel(info, kept, y_in, x_in, coef, source, level, faces, scratch):
+    source[...] = kept[...]
+    for k in range(CAP_NEW):
+        source[k, :, 0:576] = patched(info, kept, 0, k, x_in, y_in)
     coarsen_blocks(coef[...].reshape(CAP_NEW * 24, FINE.width), scratch)
     row, lane = iota((16, 256), 0), iota((16, 256), 1)
     for k in range(CAP_NEW):
-        pack_faces(FINE, coef[k], faces, k, 0)
         level[k] = jnp.ones((16, 256), F32)
         level[k, 0:12, :] = coarse_rows(scratch, k)
         level[k] = jnp.where((row < 12) & (lane < 144), level[k], 1.0)
-        pack_faces(COARSE, level[k], faces, k, FINE.face_rows)
-    send_faces(info, faces, x_out, y_out)
+        pack_faces(COARSE, level[k], faces, k, 0)
 
 
 def conduct_kernel(
-    info, source, coef, level, faces_in, x_in, y_in,
-    fine_g, fine_s, fine_d, coarse_g, coarse_w, coarse_d, row_out, u, faces, x_out, y_out, table,
+    info, source, coef, faces_in, coarse_faces, x_in, y_in,
+    fine_g, fine_s, fine_d, u, faces, x_out, y_out, table,
 ):
     fill_table(info, table, x_in, faces_in, y_in)
-    lane_row = iota((1, 128), 1)
-    band = jnp.zeros((1, 128), F32)
     for k in range(CAP_NEW):
         ghosts = ghosts_of(FINE, info, table, k, 0)
         _, g, weight, diagonal, _ = conductances(FINE, coef[k], ghosts)
@@ -279,7 +291,17 @@
         fine_s[k] = start
         u[k] = start
         pack_faces(FINE, start, faces, k, 0)
-
+    faces[:, FINE.face_rows : BOTH_ROWS, :] = coarse_faces[...]
+    send_faces(info, faces, x_out, y_out)
+
+
+def coarse_conduct_kernel(
+    info, level, faces_in, x_in, y_in, coarse_g, coarse_w, coarse_d, row_out, table
+):
+    fill_table(info, table, x_in, faces_in, y_in)
+    lane_row = iota((1, 128), 1)
+    band = jnp.zeros((1, 128), F32)
+    for k in range(CAP_NEW):
         ghosts = ghosts_of(COARSE, info, table, k, FINE.face_rows)
         q, g, weight, diagonal, masks = conductances(COARSE, level[k], ghosts)
         row, lane, depth, inside, high_y = masks
@@ -302,7 +324,6 @@
             band -= jnp.where(lane_row == info[BAND + 4 * k + f], face[f], 0.0)
         band += jnp.where(lane_row == 64 + k, info[CELL + k].astype(F32), 0.0)
     row_out[...] = band
-    send_faces(info, faces, x_out, y_out)
 
 
 def sweep_kernel(lev, info, u_in, g, start, faces_in, x_in, y_in, u, faces, x_out, y_out, table):
@@ -429,13 +450,12 @@
     return jax.ShapeDtypeStruct(shape, F32)
 
 
-ROOM = 63
 SMEM = pl.BlockSpec(memory_space=pltpu.SMEM)
 VMEM = pl.BlockSpec(memory_space=pltpu.VMEM)
 HBM = pl.BlockSpec(memory_space=pltpu.HBM)
 
 
-def call(kernel, name, outs, scratch, args, in_specs=None, out_specs=None, room=24):
+def call(kernel, name, outs, scratch, args, in_specs=None, out_specs=None):
     many = len(outs) > 1
     return pl.pallas_call(
         kernel,
@@ -443,7 +463,8 @@
         in_specs=in_specs or [SMEM] + [VMEM] * (len(args) - 1),
         out_specs=out_specs or ([VMEM] * len(outs) if many else VMEM),
         scratch_shapes=[pltpu.VMEM(s, F32) if isinstance(s, tuple) else s for s in scratch],
-        compiler_params=pltpu.CompilerParams(vmem_limit_bytes=room * 1024 * 1024),
+        cost_estimate=pl.CostEstimate(flops=10_000_000, bytes_accessed=4_000_000, transcendentals=0),
+        compiler_params=pltpu.CompilerParams(vmem_limit_bytes=24 * 1024 * 1024),
         name=name,
     )(*args)
 
@@ -453,9 +474,9 @@
     return lax.ppermute(block, axis, [(i, i + 1) for i in starts] + [(i + 1, i) for i in starts])
 
 
-def exchange(x_out, y_out, axis=AXES):
-    x_in = swap(x_out, axis, 1)
-    return x_in, swap(y_out, axis, 0)
+def exchange(x_out, y_out):
+    x_in = swap(x_out, AXES, 1)
+    return x_in, swap(y_out, AXES, 0)
 
 
 def face_outs(rows):
@@ -464,8 +485,12 @@
 
 def body(rhs_old, coef_old, old_owner, new_owner, neighbours, coarse_map):
     near = jnp.transpose(neighbours[0])
+    rhs_old, coef_old, new_owner, old_owner, near, coarse_map = (
+        pltpu.with_memory_space_constraint(a, pltpu.HBM)
+        for a in (rhs_old, coef_old, new_owner, old_owner, near, coarse_map)
+    )
     pair, old = sds(2, 24, 576), sds(CAP_OLD, 24, 576)
-    x_out, y_out, info, rhs_old, coef_old = call(
+    y_out, x_out, info, rhs_old, coef_old = call(
         first_kernel, "owners",
         [pair, pair, jax.ShapeDtypeStruct((128,), I32), old, old],
         [
@@ -474,9 +499,9 @@
             pltpu.SemaphoreType.DMA((6,)),
         ],
         (new_owner, old_owner, near, coarse_map, rhs_old, coef_old),
-        [HBM] * 6, [VMEM, VMEM, SMEM, VMEM, VMEM], ROOM,
-    )
-    x_in, y_in = exchange(x_out, y_out, "curve")
+        [HBM] * 6, [VMEM, VMEM, SMEM, VMEM, VMEM],
+    )
+    y_in, x_in = swap(y_out, "curve", 0), swap(x_out, "curve", 1)
 
     fine = sds(CAP_NEW, 24, FINE.width)
     coarse = sds(CAP_NEW, 16, 256)
@@ -485,17 +510,31 @@
     fine_faces, coarse_faces = face_outs(FINE.face_rows), face_outs(COARSE.face_rows)
     sums = (2, CAP_NEW * 24, 128)
 
-    source, coef, faces, x_out, y_out, level = call(
-        gather_kernel, "collect", [fine, fine] + face_outs(BOTH_ROWS) + [coarse], [sums],
-        (info, rhs_old, coef_old, x_in, y_in),
+    source, coef = call(place_kernel, "place", [fine, fine], [], (info, rhs_old, coef_old))
+    coef, faces, x_out, y_out = call(
+        collect_kernel, "collect", [fine] + fine_faces, [], (info, coef, y_in, x_in)
+    )
+    source, level, coarse_own = call(
+        level_kernel, "level", [fine, coarse, coarse_faces[0]], [sums],
+        (info, source, y_in, x_in, coef),
     )
     x_in, y_in = exchange(x_out, y_out)
-    fine_g, fine_s, fine_d, coarse_g, coarse_w, coarse_d, row, u, faces, x_out, y_out = call(
+    fine_g, fine_s, fine_d, u, faces, x_out, y_out = call(
         conduct_kernel, "conduct",
-        [sds(CAP_NEW, 6, 24, FINE.width), fine, fine, sds(CAP_NEW, 6, 16, 256), coarse, coarse,
-         sds(1, 128), fine] + fine_faces,
+        [sds(CAP_NEW, 6, 24, FINE.width), fine, fine, fine] + face_outs(BOTH_ROWS), fine_table,
+        (info, source, coef, faces, coarse_own, x_in, y_in),
+    )
+    x_in, y_in = exchange(x_out, y_out)
+    coarse_g, coarse_w, coarse_d, row = call(
+        coarse_conduct_kernel, "coarse_conduct",
+        [sds(CAP_NEW, 6, 16, 256), coarse, coarse, sds(1, 128)],
         [(ABSENT + 1, BOTH_ROWS, 128)],
-        (info, source, coef, level, faces, x_in, y_in),
+        (info, level, faces, x_in, y_in),
+    )
+    u0, faces, x_out, y_out = call(
+        lambda *refs: sweep_kernel(FINE, *refs), "pre", [fine, *fine_faces],
+        [(ABSENT + 1, BOTH_ROWS, 128)],
+        (info, u, fine_g, fine_s, faces, x_in, y_in),
     )
 
     def sweep(lev, u, g, start, faces, x_out, y_out, name):
@@ -507,7 +546,6 @@
             (info, u, g, start, faces, x_in, y_in),
         )
 
-    u0, faces, x_out, y_out = sweep(FINE, u, fine_g, fine_s, faces, x_out, y_out, "pre")
     x_in, y_in = exchange(x_out, y_out)
     coarse_s, faces, x_out, y_out = call(
         residual_kernel, "residual", [coarse, *coarse_faces],

time: 135 us -> 130 us (0.963)
  waiting for transfers between devices: 19 us -> 15.7 us
  local copies, waits for them, and re-layouts: 2.61 us -> 0 us
    ppermute x20, waiting for transfers between devices: 19 us -> 15.7 us  [swap(): lax.ppermute(block, axis, [(i, i + 1) for i in starts] + [(i + 1, i) for...]
    unnamed x6 -> x0, local copies, waits for them, and re-layouts: 2.61 us -> none
    pallas_call x12 -> x15, Pallas kernels: 17.1 us -> 18.3 us  [call(): pl.pallas_call(kernel, out_shape=outs if many else outs[0], in_specs=in_s...]
  transfers between devices with their start and end apart: 20 -> 20, of which waited for: 13 -> 11; matrix products, arithmetic and copies ran while one was open for 0% -> 0% of each run, Pallas kernels for 0% -> 2%
where the time goes in v3:
time: 130 us
  starting transfers between devices  80 us (62%)
  Pallas kernels  18.3 us (14%)
  waiting for transfers between devices  15.7 us (12%)
  blocking collectives  15.4 us (12%)
    ppermute x20, starting transfers between devices, swap(): lax.ppermute(block, axis, [(i, i + 1) for i in starts] + [(i + 1, i) for...  80 us
    pallas_call x15, Pallas kernels, call(): pl.pallas_call(kernel, out_shape=outs if many else outs[0], in_specs=in_s...  18.3 us
    ppermute x20, waiting for transfers between devices, swap(): lax.ppermute(block, axis, [(i, i + 1) for i in starts] + [(i + 1, i) for...  15.7 us
    all_to_all x1, blocking collectives, body(): rows = lax.all_to_all(rows, 'curve', 0, 0, tiled=True)  15.4 us
  transfers between devices with their start and end apart: 20, of which 11 were waited for; matrix products, arithmetic and copies ran while one was open for 0% of the time, Pallas kernels for 2%

profile of v3, /device:TPU:24, one launch (start us, length us, event | category | flops | bytes accessed | tf_op | source)
XLA Modules:
  0.0 129.6 jit_solution(7953123086236661230)
XLA Ops:
  0.0 2.0 %owners.1 = (f32[2,24,576]{2,1,0:T(8,128)S(1)}, f32[2,24,576]{2,1,0:T(8,128)S(1)}, s32[128]{0:T(128)S(1)}, f32[7,24,576]{2,1,0:T(8,128)S(1)}, f32[7,24,576]{2,1,0:T(8,128)S(1)}) custom-call(s32[1,128]{1,0:T(1,128)} %new_in.1, s32[1,128]{1,0:T(1,128)} %old_in.1, s32[4,128]{1,0:T(4,128)} %bitcast.9, s32[1,128]{1,0:T(1,128)} %map_in.1, f32[7,24,576]{2,1,0:T(8,128)} %rhs_in.1, ...), custom_call_target="tpu_custom_call" | custom-call | flops 10000000 | bytes 4000000 | tf_op jit(solution)/shard_map/owners/pallas_call | solution.py:460
  2.0 1.9 %collective-permute-start = (f32[2,24,576]{2,1,0:T(8,128)S(1)}, f32[2,24,576]{2,1,0:T(8,128)S(1)}, u32[]{:S(2)}, u32[]{:S(2)}) collective-permute-start(f32[2,24,576]{2,1,0:T(8,128)S(1)} %get-tuple-element.62), channel_id=1, source_target_pairs={{0,1},{2,3},{4,5},{6,7},{8,9},{10,11},{12,13},{14,15},{16,17},{18,... | collective-permute-start | bytes 331784 | tf_op jit(solution)/shard_map/ppermute | solution.py:474
  4.0 0.7 collective-permute-start.1
  4.6 0.6 place.1
  5.2 0.0 collective-permute-done.y_in
  5.3 0.6 collect.1
  5.9 13.9 %collective-permute-start.2 = (f32[3,40,128]{2,1,0:T(8,128)S(1)}, f32[3,40,128]{2,1,0:T(8,128)S(1)}, u32[]{:S(2)}, u32[]{:S(2)}) collective-permute-start(f32[3,40,128]{2,1,0:T(8,128)S(1)} %get-tuple-element.69), channel_id=1, source_target_pairs={{1,2},{3,4},{5,6},{7,8},{9,10},{11,12},{13,14},{15,16},{17,18},{19... | collective-permute-start | bytes 184328 | tf_op jit(solution)/shard_map/ppermute | solution.py:474
  19.8 1.9 %collective-permute-start.3 = (f32[3,40,128]{2,1,0:T(8,128)S(1)}, f32[3,40,128]{2,1,0:T(8,128)S(1)}, u32[]{:S(2)}, u32[]{:S(2)}) collective-permute-start(f32[3,40,128]{2,1,0:T(8,128)S(1)} %get-tuple-element.70), channel_id=1, source_target_pairs={{0,1},{2,3},{4,5},{6,7},{8,9},{10,11},{12,13},{14,15},{16,17},{18,... | collective-permute-start | bytes 184328 | tf_op jit(solution)/shard_map/ppermute | solution.py:474
  21.7 1.1 level.1
  22.8 0.1 collective-permute-done.3.y_in
  22.9 1.3 %conduct.1 = (f32[5,6,24,640]{3,2,1,0:T(8,128)S(1)}, f32[5,24,640]{2,1,0:T(8,128)S(1)}, f32[5,24,640]{2,1,0:T(8,128)S(1)}, f32[5,24,640]{2,1,0:T(8,128)S(1)}, f3...) custom-call(s32[128]{0:T(128)S(1)} %get-tuple-element.58.info.refs_0_, ...), custom_call_target="tpu_custom_call" | custom-call | flops 10000000 | bytes 4000000 | tf_op jit(solution)/shard_map/conduct/pallas_call | solution.py:460
  24.2 7.8 %collective-permute-start.4 = (f32[3,56,128]{2,1,0:T(8,128)S(1)}, f32[3,56,128]{2,1,0:T(8,128)S(1)}, u32[]{:S(2)}, u32[]{:S(2)}) collective-permute-start(f32[3,56,128]{2,1,0:T(8,128)S(1)} %get-tuple-element.75), channel_id=1, source_target_pairs={{1,2},{3,4},{5,6},{7,8},{9,10},{11,12},{13,14},{15,16},{17,18},{19... | collective-permute-start | bytes 258056 | tf_op jit(solution)/shard_map/ppermute | solution.py:474
  32.1 1.9 %collective-permute-start.5 = (f32[3,56,128]{2,1,0:T(8,128)S(1)}, f32[3,56,128]{2,1,0:T(8,128)S(1)}, u32[]{:S(2)}, u32[]{:S(2)}) collective-permute-start(f32[3,56,128]{2,1,0:T(8,128)S(1)} %get-tuple-element.76), channel_id=1, source_target_pairs={{0,1},{2,3},{4,5},{6,7},{8,9},{10,11},{12,13},{14,15},{16,17},{18,... | collective-permute-start | bytes 258056 | tf_op jit(solution)/shard_map/ppermute | solution.py:474
  34.0 0.2 collective-permute-done.4.refs_5_.x_in
  34.3 1.0 collective-permute-done.5.refs_6_.y_in
  35.3 1.0 pre.1
  36.3 6.8 %collective-permute-start.6 = (f32[3,40,128]{2,1,0:T(8,128)S(1)}, f32[3,40,128]{2,1,0:T(8,128)S(1)}, u32[]{:S(2)}, u32[]{:S(2)}) collective-permute-start(f32[3,40,128]{2,1,0:T(8,128)S(1)} %get-tuple-element.82), channel_id=1, source_target_pairs={{1,2},{3,4},{5,6},{7,8},{9,10},{11,12},{13,14},{15,16},{17,18},{19... | collective-permute-start | bytes 184328 | tf_op jit(solution)/shard_map/ppermute | solution.py:474
  43.2 1.9 %collective-permute-start.7 = (f32[3,40,128]{2,1,0:T(8,128)S(1)}, f32[3,40,128]{2,1,0:T(8,128)S(1)}, u32[]{:S(2)}, u32[]{:S(2)}) collective-permute-start(f32[3,40,128]{2,1,0:T(8,128)S(1)} %get-tuple-element.83), channel_id=1, source_target_pairs={{0,1},{2,3},{4,5},{6,7},{8,9},{10,11},{12,13},{14,15},{16,17},{18,... | collective-permute-start | bytes 184328 | tf_op jit(solution)/shard_map/ppermute | solution.py:474
  45.1 1.0 coarse_conduct.1
  46.1 0.2 collective-permute-done.7.y_in
  46.3 1.4 %residual.1 = (f32[5,16,256]{2,1,0:T(8,128)S(1)}, f32[5,16,128]{2,1,0:T(8,128)S(1)}, f32[3,16,128]{2,1,0:T(8,128)S(1)}, f32[3,16,128]{2,1,0:T(8,128)S(1)}) custom-call(s32[128]{0:T(128)S(1)} %get-tuple-element.58.info.refs_0_, f32[5,24,640]{2,1,0:T(8,128)S(1)} %get-tuple-element.77.u_in, f32[5,6,24,640]{3,2,1,0:T(8,128)S(1)} %get-tuple-element.72.refs_2_.g, ...), custom_call_target="tpu_custom_call" | custom-call | flops 10000000 | bytes 4000000 | tf_op jit(solution)/shard_map/residual/pallas_call | solution.py:460
  47.7 6.6 %collective-permute-start.8 = (f32[3,16,128]{2,1,0:T(8,128)S(1)}, f32[3,16,128]{2,1,0:T(8,128)S(1)}, u32[]{:S(2)}, u32[]{:S(2)}) collective-permute-start(f32[3,16,128]{2,1,0:T(8,128)S(1)} %get-tuple-element.87), channel_id=1, source_target_pairs={{1,2},{3,4},{5,6},{7,8},{9,10},{11,12},{13,14},{15,16},{17,18},{19... | collective-permute-start | bytes 73736 | tf_op jit(solution)/shard_map/ppermute | solution.py:474
  54.4 1.9 %collective-permute-start.9 = (f32[3,16,128]{2,1,0:T(8,128)S(1)}, f32[3,16,128]{2,1,0:T(8,128)S(1)}, u32[]{:S(2)}, u32[]{:S(2)}) collective-permute-start(f32[3,16,128]{2,1,0:T(8,128)S(1)} %get-tuple-element.88), channel_id=1, source_target_pairs={{0,1},{2,3},{4,5},{6,7},{8,9},{10,11},{12,13},{14,15},{16,17},{18,... | collective-permute-start | bytes 73736 | tf_op jit(solution)/shard_map/ppermute | solution.py:474
  56.3 0.8 collective-permute-done.8.refs_5_
  57.1 0.3 collective-permute-done.9.refs_6_
  57.4 0.8 coarse_pre.1
  58.3 6.3 %collective-permute-start.10 = (f32[3,16,128]{2,1,0:T(8,128)S(1)}, f32[3,16,128]{2,1,0:T(8,128)S(1)}, u32[]{:S(2)}, u32[]{:S(2)}) collective-permute-start(f32[3,16,128]{2,1,0:T(8,128)S(1)} %get-tuple-element.93), channel_id=1, source_target_pairs={{1,2},{3,4},{5,6},{7,8},{9,10},{11,12},{13,14},{15,16},{17,18},{19... | collective-permute-start | bytes 73736 | tf_op jit(solution)/shard_map/ppermute | solution.py:474
  64.5 1.9 %collective-permute-start.11 = (f32[3,16,128]{2,1,0:T(8,128)S(1)}, f32[3,16,128]{2,1,0:T(8,128)S(1)}, u32[]{:S(2)}, u32[]{:S(2)}) collective-permute-start(f32[3,16,128]{2,1,0:T(8,128)S(1)} %get-tuple-element.94), channel_id=1, source_target_pairs={{0,1},{2,3},{4,5},{6,7},{8,9},{10,11},{12,13},{14,15},{16,17},{18,... | collective-permute-start | bytes 73736 | tf_op jit(solution)/shard_map/ppermute | solution.py:474
  66.5 1.2 collective-permute-done.10.x_in
  67.6 0.9 totals.1
  68.5 15.4 %all_to_all.11 = f32[32,1,128]{2,1,0:T(1,128)S(1)} all-to-all(f32[32,1,128]{2,1,0:T(1,128)S(1)} %bitcast.7), channel_id=1, replica_groups=mesh['group'=16,'curve'=32] {'curve'}, dimensions={0} | all-to-all | bytes 32768 | tf_op jit(solution)/shard_map/all_to_all | solution.py:563
  83.9 2.8 %solve.1 = (f32[5,16,256]{2,1,0:T(8,128)S(1)}, f32[5,16,128]{2,1,0:T(8,128)S(1)}, f32[3,16,128]{2,1,0:T(8,128)S(1)}, f32[3,16,128]{2,1,0:T(8,128)S(1)}) custom-call(s32[128]{0:T(128)S(1)} %get-tuple-element.58.info.refs_0_, f32[32,128]{1,0:T(8,128)S(1)} %bitcast.8, f32[5,16,256]{2,1,0:T(8,128)S(1)} %get-tuple-element.89.u_in), custom_call_target="tpu_custom_call" | custom-call | flops 10000000 | bytes 4000000 | tf_op jit(solution)/shard_map/solve/pallas_call | solution.py:460
  86.7 4.7 %collective-permute-start.12 = (f32[3,16,128]{2,1,0:T(8,128)S(1)}, f32[3,16,128]{2,1,0:T(8,128)S(1)}, u32[]{:S(2)}, u32[]{:S(2)}) collective-permute-start(f32[3,16,128]{2,1,0:T(8,128)S(1)} %get-tuple-element.97), channel_id=1, source_target_pairs={{1,2},{3,4},{5,6},{7,8},{9,10},{11,12},{13,14},{15,16},{17,18},{19... | collective-permute-start | bytes 73736 | tf_op jit(solution)/shard_map/ppermute | solution.py:474
  91.3 1.9 %collective-permute-start.13 = (f32[3,16,128]{2,1,0:T(8,128)S(1)}, f32[3,16,128]{2,1,0:T(8,128)S(1)}, u32[]{:S(2)}, u32[]{:S(2)}) collective-permute-start(f32[3,16,128]{2,1,0:T(8,128)S(1)} %get-tuple-element.98), channel_id=1, source_target_pairs={{0,1},{2,3},{4,5},{6,7},{8,9},{10,11},{12,13},{14,15},{16,17},{18,... | collective-permute-start | bytes 73736 | tf_op jit(solution)/shard_map/ppermute | solution.py:474
  93.3 2.8 %collective-permute-done.12.refs_5_ = f32[3,16,128]{2,1,0:T(8,128)S(1)} collective-permute-done((f32[3,16,128]{2,1,0:T(8,128)S(1)}, f32[3,16,128]{2,1,0:T(8,128)S(1)}, u32[]{:S(2)}, u32[]{:S(2)}) %collective-permute-start.12) | collective-permute-done | bytes 24608 | tf_op jit(solution)/shard_map/ppermute | solution.py:474
  96.0 0.8 coarse_post.1
  96.9 4.7 %collective-permute-start.14 = (f32[3,16,128]{2,1,0:T(8,128)S(1)}, f32[3,16,128]{2,1,0:T(8,128)S(1)}, u32[]{:S(2)}, u32[]{:S(2)}) collective-permute-start(f32[3,16,128]{2,1,0:T(8,128)S(1)} %get-tuple-element.101), channel_id=1, source_target_pairs={{1,2},{3,4},{5,6},{7,8},{9,10},{11,12},{13,14},{15,16},{17,18},{19... | collective-permute-start | bytes 73736 | tf_op jit(solution)/shard_map/ppermute | solution.py:474
  101.5 1.9 %collective-permute-start.15 = (f32[3,16,128]{2,1,0:T(8,128)S(1)}, f32[3,16,128]{2,1,0:T(8,128)S(1)}, u32[]{:S(2)}, u32[]{:S(2)}) collective-permute-start(f32[3,16,128]{2,1,0:T(8,128)S(1)} %get-tuple-element.102), channel_id=1, source_target_pairs={{0,1},{2,3},{4,5},{6,7},{8,9},{10,11},{12,13},{14,15},{16,17},{18,... | collective-permute-start | bytes 73736 | tf_op jit(solution)/shard_map/ppermute | solution.py:474
  103.5 2.8 %collective-permute-done.14.x_in = f32[3,16,128]{2,1,0:T(8,128)S(1)} collective-permute-done((f32[3,16,128]{2,1,0:T(8,128)S(1)}, f32[3,16,128]{2,1,0:T(8,128)S(1)}, u32[]{:S(2)}, u32[]{:S(2)}) %collective-permute-start.14) | collective-permute-done | bytes 24608 | tf_op jit(solution)/shard_map/ppermute | solution.py:474
  106.2 1.0 refine.1
  107.3 4.7 %collective-permute-start.16 = (f32[3,40,128]{2,1,0:T(8,128)S(1)}, f32[3,40,128]{2,1,0:T(8,128)S(1)}, u32[]{:S(2)}, u32[]{:S(2)}) collective-permute-start(f32[3,40,128]{2,1,0:T(8,128)S(1)} %get-tuple-element.105), channel_id=1, source_target_pairs={{1,2},{3,4},{5,6},{7,8},{9,10},{11,12},{13,14},{15,16},{17,18},{19... | collective-permute-start | bytes 184328 | tf_op jit(solution)/shard_map/ppermute | solution.py:474
  111.9 1.9 %collective-permute-start.17 = (f32[3,40,128]{2,1,0:T(8,128)S(1)}, f32[3,40,128]{2,1,0:T(8,128)S(1)}, u32[]{:S(2)}, u32[]{:S(2)}) collective-permute-start(f32[3,40,128]{2,1,0:T(8,128)S(1)} %get-tuple-element.106), channel_id=1, source_target_pairs={{0,1},{2,3},{4,5},{6,7},{8,9},{10,11},{12,13},{14,15},{16,17},{18,... | collective-permute-start | bytes 184328 | tf_op jit(solution)/shard_map/ppermute | solution.py:474
  113.9 3.2 %collective-permute-done.16.refs_5_ = f32[3,40,128]{2,1,0:T(8,128)S(1)} collective-permute-done((f32[3,40,128]{2,1,0:T(8,128)S(1)}, f32[3,40,128]{2,1,0:T(8,128)S(1)}, u32[]{:S(2)}, u32[]{:S(2)}) %collective-permute-start.16) | collective-permute-done | bytes 61472 | tf_op jit(solution)/shard_map/ppermute | solution.py:474
  117.0 1.0 post.1
  118.1 4.7 %collective-permute-start.18 = (f32[3,40,128]{2,1,0:T(8,128)S(1)}, f32[3,40,128]{2,1,0:T(8,128)S(1)}, u32[]{:S(2)}, u32[]{:S(2)}) collective-permute-start(f32[3,40,128]{2,1,0:T(8,128)S(1)} %get-tuple-element.109), channel_id=1, source_target_pairs={{1,2},{3,4},{5,6},{7,8},{9,10},{11,12},{13,14},{15,16},{17,18},{19... | collective-permute-start | bytes 184328 | tf_op jit(solution)/shard_map/ppermute | solution.py:474
  122.8 1.9 %collective-permute-start.19 = (f32[3,40,128]{2,1,0:T(8,128)S(1)}, f32[3,40,128]{2,1,0:T(8,128)S(1)}, u32[]{:S(2)}, u32[]{:S(2)}) collective-permute-start(f32[3,40,128]{2,1,0:T(8,128)S(1)} %get-tuple-element.110), channel_id=1, source_target_pairs={{0,1},{2,3},{4,5},{6,7},{8,9},{10,11},{12,13},{14,15},{16,17},{18,... | collective-permute-start | bytes 184328 | tf_op jit(solution)/shard_map/ppermute | solution.py:474
  124.7 3.2 %collective-permute-done.18.x_in = f32[3,40,128]{2,1,0:T(8,128)S(1)} collective-permute-done((f32[3,40,128]{2,1,0:T(8,128)S(1)}, f32[3,40,128]{2,1,0:T(8,128)S(1)}, u32[]{:S(2)}, u32[]{:S(2)}) %collective-permute-start.18) | collective-permute-done | bytes 61472 | tf_op jit(solution)/shard_map/ppermute | solution.py:474
  127.8 1.7 %last.1 = f32[5,24,576]{2,1,0:T(8,128)} custom-call(s32[128]{0:T(128)S(1)} %get-tuple-element.58.info.refs_0_, f32[5,24,640]{2,1,0:T(8,128)S(1)} %get-tuple-element.107.u_in, f32[5,6,24,640]{3,2,1,0:T(8,128)S(1)} %get-tuple-element.72.refs_2_.g, f32[5,24,640]{2,1,0:T(8,128)S(1)} %get-tuple-element.73.refs_3_.start, ...), custom_call_target="tpu_custom_call" | custom-call | flops 10000000 | bytes 4000000 | tf_op jit(solution)/shard_map/last/pallas_call | solution.py:460
  (8 shorter events, 0.0 us)
Async XLA Ops:
  2.0 3.2 %collective-permute-start = (f32[2,24,576]{2,1,0:T(8,128)S(1)}, f32[2,24,576]{2,1,0:T(8,128)S(1)}, u32[]{:S(2)}, u32[]{:S(2)}) collective-permute-start(f32[2,24,576]{2,1,0:T(8,128)S(1)} %get-tuple-element.62), channel_id=1, source_target_pairs={{0,1},{2,3},{4,5},{6,7},{8,9},{10,11},{12,13},{14,15},{16,17},{18,... | collective-permute-start | bytes 331784 | tf_op jit(solution)/shard_map/ppermute | solution.py:474
  4.0 1.3 %collective-permute-start.1 = (f32[2,24,576]{2,1,0:T(8,128)S(1)}, f32[2,24,576]{2,1,0:T(8,128)S(1)}, u32[]{:S(2)}, u32[]{:S(2)}) collective-permute-start(f32[2,24,576]{2,1,0:T(8,128)S(1)} %get-tuple-element.63), channel_id=1, source_target_pairs={{1,2},{3,4},{5,6},{7,8},{9,10},{11,12},{13,14},{15,16},{17,18},{19... | collective-permute-start | bytes 331784 | tf_op jit(solution)/shard_map/ppermute | solution.py:474
  5.9 16.9 %collective-permute-start.2 = (f32[3,40,128]{2,1,0:T(8,128)S(1)}, f32[3,40,128]{2,1,0:T(8,128)S(1)}, u32[]{:S(2)}, u32[]{:S(2)}) collective-permute-start(f32[3,40,128]{2,1,0:T(8,128)S(1)} %get-tuple-element.69), channel_id=1, source_target_pairs={{1,2},{3,4},{5,6},{7,8},{9,10},{11,12},{13,14},{15,16},{17,18},{19... | collective-permute-start | bytes 184328 | tf_op jit(solution)/shard_map/ppermute | solution.py:474
  19.8 3.1 %collective-permute-start.3 = (f32[3,40,128]{2,1,0:T(8,128)S(1)}, f32[3,40,128]{2,1,0:T(8,128)S(1)}, u32[]{:S(2)}, u32[]{:S(2)}) collective-permute-start(f32[3,40,128]{2,1,0:T(8,128)S(1)} %get-tuple-element.70), channel_id=1, source_target_pairs={{0,1},{2,3},{4,5},{6,7},{8,9},{10,11},{12,13},{14,15},{16,17},{18,... | collective-permute-start | bytes 184328 | tf_op jit(solution)/shard_map/ppermute | solution.py:474
  24.2 10.0 %collective-permute-start.4 = (f32[3,56,128]{2,1,0:T(8,128)S(1)}, f32[3,56,128]{2,1,0:T(8,128)S(1)}, u32[]{:S(2)}, u32[]{:S(2)}) collective-permute-start(f32[3,56,128]{2,1,0:T(8,128)S(1)} %get-tuple-element.75), channel_id=1, source_target_pairs={{1,2},{3,4},{5,6},{7,8},{9,10},{11,12},{13,14},{15,16},{17,18},{19... | collective-permute-start | bytes 258056 | tf_op jit(solution)/shard_map/ppermute | solution.py:474
  32.1 3.2 %collective-permute-start.5 = (f32[3,56,128]{2,1,0:T(8,128)S(1)}, f32[3,56,128]{2,1,0:T(8,128)S(1)}, u32[]{:S(2)}, u32[]{:S(2)}) collective-permute-start(f32[3,56,128]{2,1,0:T(8,128)S(1)} %get-tuple-element.76), channel_id=1, source_target_pairs={{0,1},{2,3},{4,5},{6,7},{8,9},{10,11},{12,13},{14,15},{16,17},{18,... | collective-permute-start | bytes 258056 | tf_op jit(solution)/shard_map/ppermute | solution.py:474
  36.3 9.8 %collective-permute-start.6 = (f32[3,40,128]{2,1,0:T(8,128)S(1)}, f32[3,40,128]{2,1,0:T(8,128)S(1)}, u32[]{:S(2)}, u32[]{:S(2)}) collective-permute-start(f32[3,40,128]{2,1,0:T(8,128)S(1)} %get-tuple-element.82), channel_id=1, source_target_pairs={{1,2},{3,4},{5,6},{7,8},{9,10},{11,12},{13,14},{15,16},{17,18},{19... | collective-permute-start | bytes 184328 | tf_op jit(solution)/shard_map/ppermute | solution.py:474
  43.2 3.1 %collective-permute-start.7 = (f32[3,40,128]{2,1,0:T(8,128)S(1)}, f32[3,40,128]{2,1,0:T(8,128)S(1)}, u32[]{:S(2)}, u32[]{:S(2)}) collective-permute-start(f32[3,40,128]{2,1,0:T(8,128)S(1)} %get-tuple-element.83), channel_id=1, source_target_pairs={{0,1},{2,3},{4,5},{6,7},{8,9},{10,11},{12,13},{14,15},{16,17},{18,... | collective-permute-start | bytes 184328 | tf_op jit(solution)/shard_map/ppermute | solution.py:474
  47.7 9.4 %collective-permute-start.8 = (f32[3,16,128]{2,1,0:T(8,128)S(1)}, f32[3,16,128]{2,1,0:T(8,128)S(1)}, u32[]{:S(2)}, u32[]{:S(2)}) collective-permute-start(f32[3,16,128]{2,1,0:T(8,128)S(1)} %get-tuple-element.87), channel_id=1, source_target_pairs={{1,2},{3,4},{5,6},{7,8},{9,10},{11,12},{13,14},{15,16},{17,18},{19... | collective-permute-start | bytes 73736 | tf_op jit(solution)/shard_map/ppermute | solution.py:474
  54.4 3.1 %collective-permute-start.9 = (f32[3,16,128]{2,1,0:T(8,128)S(1)}, f32[3,16,128]{2,1,0:T(8,128)S(1)}, u32[]{:S(2)}, u32[]{:S(2)}) collective-permute-start(f32[3,16,128]{2,1,0:T(8,128)S(1)} %get-tuple-element.88), channel_id=1, source_target_pairs={{0,1},{2,3},{4,5},{6,7},{8,9},{10,11},{12,13},{14,15},{16,17},{18,... | collective-permute-start | bytes 73736 | tf_op jit(solution)/shard_map/ppermute | solution.py:474
  58.3 9.4 %collective-permute-start.10 = (f32[3,16,128]{2,1,0:T(8,128)S(1)}, f32[3,16,128]{2,1,0:T(8,128)S(1)}, u32[]{:S(2)}, u32[]{:S(2)}) collective-permute-start(f32[3,16,128]{2,1,0:T(8,128)S(1)} %get-tuple-element.93), channel_id=1, source_target_pairs={{1,2},{3,4},{5,6},{7,8},{9,10},{11,12},{13,14},{15,16},{17,18},{19... | collective-permute-start | bytes 73736 | tf_op jit(solution)/shard_map/ppermute | solution.py:474
  64.5 3.1 %collective-permute-start.11 = (f32[3,16,128]{2,1,0:T(8,128)S(1)}, f32[3,16,128]{2,1,0:T(8,128)S(1)}, u32[]{:S(2)}, u32[]{:S(2)}) collective-permute-start(f32[3,16,128]{2,1,0:T(8,128)S(1)} %get-tuple-element.94), channel_id=1, source_target_pairs={{0,1},{2,3},{4,5},{6,7},{8,9},{10,11},{12,13},{14,15},{16,17},{18,... | collective-permute-start | bytes 73736 | tf_op jit(solution)/shard_map/ppermute | solution.py:474
  86.7 9.4 %collective-permute-start.12 = (f32[3,16,128]{2,1,0:T(8,128)S(1)}, f32[3,16,128]{2,1,0:T(8,128)S(1)}, u32[]{:S(2)}, u32[]{:S(2)}) collective-permute-start(f32[3,16,128]{2,1,0:T(8,128)S(1)} %get-tuple-element.97), channel_id=1, source_target_pairs={{1,2},{3,4},{5,6},{7,8},{9,10},{11,12},{13,14},{15,16},{17,18},{19... | collective-permute-start | bytes 73736 | tf_op jit(solution)/shard_map/ppermute | solution.py:474
  91.3 4.7 %collective-permute-start.13 = (f32[3,16,128]{2,1,0:T(8,128)S(1)}, f32[3,16,128]{2,1,0:T(8,128)S(1)}, u32[]{:S(2)}, u32[]{:S(2)}) collective-permute-start(f32[3,16,128]{2,1,0:T(8,128)S(1)} %get-tuple-element.98), channel_id=1, source_target_pairs={{0,1},{2,3},{4,5},{6,7},{8,9},{10,11},{12,13},{14,15},{16,17},{18,... | collective-permute-start | bytes 73736 | tf_op jit(solution)/shard_map/ppermute | solution.py:474
  96.9 9.4 %collective-permute-start.14 = (f32[3,16,128]{2,1,0:T(8,128)S(1)}, f32[3,16,128]{2,1,0:T(8,128)S(1)}, u32[]{:S(2)}, u32[]{:S(2)}) collective-permute-start(f32[3,16,128]{2,1,0:T(8,128)S(1)} %get-tuple-element.101), channel_id=1, source_target_pairs={{1,2},{3,4},{5,6},{7,8},{9,10},{11,12},{13,14},{15,16},{17,18},{19... | collective-permute-start | bytes 73736 | tf_op jit(solution)/shard_map/ppermute | solution.py:474
  101.5 4.7 %collective-permute-start.15 = (f32[3,16,128]{2,1,0:T(8,128)S(1)}, f32[3,16,128]{2,1,0:T(8,128)S(1)}, u32[]{:S(2)}, u32[]{:S(2)}) collective-permute-start(f32[3,16,128]{2,1,0:T(8,128)S(1)} %get-tuple-element.102), channel_id=1, source_target_pairs={{0,1},{2,3},{4,5},{6,7},{8,9},{10,11},{12,13},{14,15},{16,17},{18,... | collective-permute-start | bytes 73736 | tf_op jit(solution)/shard_map/ppermute | solution.py:474
  107.3 9.8 %collective-permute-start.16 = (f32[3,40,128]{2,1,0:T(8,128)S(1)}, f32[3,40,128]{2,1,0:T(8,128)S(1)}, u32[]{:S(2)}, u32[]{:S(2)}) collective-permute-start(f32[3,40,128]{2,1,0:T(8,128)S(1)} %get-tuple-element.105), channel_id=1, source_target_pairs={{1,2},{3,4},{5,6},{7,8},{9,10},{11,12},{13,14},{15,16},{17,18},{19... | collective-permute-start | bytes 184328 | tf_op jit(solution)/shard_map/ppermute | solution.py:474
  111.9 5.1 %collective-permute-start.17 = (f32[3,40,128]{2,1,0:T(8,128)S(1)}, f32[3,40,128]{2,1,0:T(8,128)S(1)}, u32[]{:S(2)}, u32[]{:S(2)}) collective-permute-start(f32[3,40,128]{2,1,0:T(8,128)S(1)} %get-tuple-element.106), channel_id=1, source_target_pairs={{0,1},{2,3},{4,5},{6,7},{8,9},{10,11},{12,13},{14,15},{16,17},{18,... | collective-permute-start | bytes 184328 | tf_op jit(solution)/shard_map/ppermute | solution.py:474
  118.1 9.8 %collective-permute-start.18 = (f32[3,40,128]{2,1,0:T(8,128)S(1)}, f32[3,40,128]{2,1,0:T(8,128)S(1)}, u32[]{:S(2)}, u32[]{:S(2)}) collective-permute-start(f32[3,40,128]{2,1,0:T(8,128)S(1)} %get-tuple-element.109), channel_id=1, source_target_pairs={{1,2},{3,4},{5,6},{7,8},{9,10},{11,12},{13,14},{15,16},{17,18},{19... | collective-permute-start | bytes 184328 | tf_op jit(solution)/shard_map/ppermute | solution.py:474
  122.8 5.1 %collective-permute-start.19 = (f32[3,40,128]{2,1,0:T(8,128)S(1)}, f32[3,40,128]{2,1,0:T(8,128)S(1)}, u32[]{:S(2)}, u32[]{:S(2)}) collective-permute-start(f32[3,40,128]{2,1,0:T(8,128)S(1)} %get-tuple-element.110), channel_id=1, source_target_pairs={{0,1},{2,3},{4,5},{6,7},{8,9},{10,11},{12,13},{14,15},{16,17},{18,... | collective-permute-start | bytes 184328 | tf_op jit(solution)/shard_map/ppermute | solution.py:474

commit v4 on v3

--- a/solution.py
+++ b/solution.py
@@ -18,6 +18,9 @@
 
 HELD, PICK, TABLE, CELL, BAND = 0, 1, 8, 32, 40
 SEND_X, SEND_Y, AT_X, AT_Y = 64, 65, 66, 67
+SPARE, OTHER, BESIDE, FACING = 7, 72, 96, 116
+OPPOSITE = (1, 0, 3, 2)
+LIFT_ROW = 13
 ABSENT = 2 * REACH + CAP_NEW
 
 
@@ -45,17 +48,23 @@
 
 
 def pack_faces(lev, field, faces, k, base):
+    pack_fields(lev, field, field, faces, k, base)
+
+
+def pack_fields(lev, y_field, x_field, faces, k, base, y_high=None, x_high=None):
+    y_high = y_field if y_high is None else y_high
+    x_high = x_field if x_high is None else x_high
     lane = iota((lev.rows, 128), 1)
-    tail = field[:, lev.width - 128 :]
+    tail = y_high[:, lev.width - 128 :]
     move = lev.high_at - lev.last
     if move:
         tail = pltpu.roll(tail, move, 1)
-    faces[k, base : base + lev.rows, :] = jnp.where(lane < lev.side, field[:, :128], tail)
+    faces[k, base : base + lev.rows, :] = jnp.where(lane < lev.side, y_field[:, :128], tail)
     for j in range(lev.tiles):
         part = slice(128 * j, 128 * j + 128)
         low, high = base + lev.x_low + j, base + lev.x_high + j
-        faces[k, low : low + 1, :] = field[0:1, part]
-        faces[k, high : high + 1, :] = field[lev.side - 1 : lev.side, part]
+        faces[k, low : low + 1, :] = x_field[0:1, part]
+        faces[k, high : high + 1, :] = x_high[lev.side - 1 : lev.side, part]
 
 
 def send_faces(info, faces, x_out, y_out):
@@ -68,20 +77,20 @@
 def fill_table(info, table, x_in, faces, y_in):
     x_first, y_first = info[AT_X], info[AT_Y]
     for j in range(REACH):
-        table[x_first + j] = x_in[j]
+        table[x_first + j] = x_in[j, 0 : table.shape[1]]
         table[y_first + j] = y_in[j]
     table[REACH : REACH + CAP_NEW] = faces[...]
     table[ABSENT] = jnp.zeros(table.shape[1:], F32)
 
 
+def x_line(lev, table, slot, first):
+    return jnp.concatenate([table[slot, pl.ds(first + j, 1), :] for j in range(lev.tiles)], axis=1)
+
+
 def ghosts_of(lev, info, table, k, base):
     row = [info[TABLE + 4 * k + f] for f in range(4)]
-    x_low = jnp.concatenate(
-        [table[row[0], pl.ds(base + lev.x_high + j, 1), :] for j in range(lev.tiles)], axis=1
-    )
-    x_high = jnp.concatenate(
-        [table[row[1], pl.ds(base + lev.x_low + j, 1), :] for j in range(lev.tiles)], axis=1
-    )
+    x_low = x_line(lev, table, row[0], base + lev.x_high)
+    x_high = x_line(lev, table, row[1], base + lev.x_low)
     y_low = pltpu.roll(table[row[2], pl.ds(base, lev.rows), :], 128 - lev.high_at, 1)
     y_high = pltpu.roll(table[row[3], pl.ds(base, lev.rows), :], lev.last, 1)
     return row, x_low, x_high, y_low, y_high
@@ -153,21 +162,21 @@
 
 
 def split_three(values):
+    high, rest = values.astype(jnp.bfloat16), values - values.astype(jnp.bfloat16).astype(F32)
+    mid = rest.astype(jnp.bfloat16)
+    return high, mid, (rest - mid.astype(F32)).astype(jnp.bfloat16)
+
+
+def split_two(values):
     high = values.astype(jnp.bfloat16)
-    rest = values - high.astype(F32)
-    mid = rest.astype(jnp.bfloat16)
-    low = (rest - mid.astype(F32)).astype(jnp.bfloat16)
-    return high, mid, low
-
-
-def coarsen_blocks(fine, scratch):
-    spread = spread_matrix()
-    total = None
-    for part in split_three(fine):
-        one = lax.dot_general(
-            part, spread, (((1,), (1,)), ((), ())), preferred_element_type=F32
-        )
-        total = one if total is None else total + one
+    return high, (values - high.astype(F32)).astype(jnp.bfloat16)
+
+
+def coarsen_blocks(fine, spread, scratch):
+    total = sum(
+        lax.dot_general(part, spread, (((1,), (1,)), ((), ())), preferred_element_type=F32)
+        for part in split_two(fine)
+    )
     scratch[0] = total[:, :128]
     scratch[1] = total[:, 128:]
 
@@ -214,6 +223,9 @@
     info[SEND_X], info[SEND_Y] = jnp.where(up, final, 0), jnp.where(up, 0, final)
     info[AT_X] = jnp.where(up, REACH + CAP_NEW, 0)
     info[AT_Y] = jnp.where(up, 0, REACH + CAP_NEW)
+    for i in range(4 * REACH):
+        info[FACING + i] = -1
+    x_at = jnp.where(up, REACH + CAP_NEW, 0)
     from_next, from_previous = jnp.where(up, 0, CAP_OLD + 1), jnp.where(up, CAP_OLD + 1, 0)
     first_id = group * NBG + new_first
     finish = first_id + held
@@ -236,6 +248,11 @@
             inside = present & (local >= 0) & (local < NBG)
             other = map_ref[0, jnp.clip(local, 0, NBG - 1)]
             info[BAND + 4 * k + f] = jnp.where(inside, 8 * k + 3 + other - cell, -1)
+            info[BESIDE + 4 * k + f] = jnp.where(inside, other, -1)
+            outside = present & jnp.logical_not(inside)
+            place = jnp.clip(slot - x_at, 0, REACH - 1)
+            info[OTHER + 4 * k + f] = jnp.where(outside, place, REACH)
+            info[jnp.where(outside, FACING + 4 * place + OPPOSITE[f], SPARE)] = cell
 
 
 def place_kernel(info, rhs_ref, coef_ref, source, coef):
@@ -263,11 +280,12 @@
     send_faces(info, faces, x_out, y_out)
 
 
-def level_kernel(info, kept, y_in, x_in, coef, source, level, faces, scratch):
+def level_kernel(info, kept, y_in, x_in, coef, source, level, faces, spread, scratch):
     source[...] = kept[...]
     for k in range(CAP_NEW):
         source[k, :, 0:576] = patched(info, kept, 0, k, x_in, y_in)
-    coarsen_blocks(coef[...].reshape(CAP_NEW * 24, FINE.width), scratch)
+    spread[...] = spread_matrix()
+    coarsen_blocks(coef[...].reshape(CAP_NEW * 24, FINE.width), spread[...], scratch)
     row, lane = iota((16, 256), 0), iota((16, 256), 1)
     for k in range(CAP_NEW):
         level[k] = jnp.ones((16, 256), F32)
@@ -296,7 +314,7 @@
 
 
 def coarse_conduct_kernel(
-    info, level, faces_in, x_in, y_in, coarse_g, coarse_w, coarse_d, row_out, table
+    info, level, faces_in, x_in, y_in, coarse_g, coarse_w, coarse_d, g_faces, row_out, table
 ):
     fill_table(info, table, x_in, faces_in, y_in)
     lane_row = iota((1, 128), 1)
@@ -308,6 +326,11 @@
         for i in range(6):
             coarse_g[k, i] = g[i]
         coarse_w[k] = weight
+        pack_fields(COARSE, g[2], g[4], g_faces, k, 0, g[3], g[5])
+        low_y = jnp.where(lane < 12, g[2], 0.0)
+        x_edge = jnp.where(lane >= 132, g[3], low_y)
+        y_edge = jnp.where(row == 0, g[4], jnp.where(row == 11, g[5], 0.0))
+        pack_fields(COARSE, y_edge, x_edge, g_faces, k, 16)
         coarse_d[k] = (1.0 / OMEGA) * diagonal
         face = [
             both_totals(jnp.where(inside & (row == 0), q[4], 0.0)),
@@ -338,7 +361,7 @@
 
 
 def residual_kernel(
-    info, u_in, g, start, diagonal, weight, faces_in, x_in, y_in,
+    info, u_in, g, start, diagonal, weight, spread, g_faces, faces_in, x_in, y_in,
     coarse_s, faces, x_out, y_out, table, rest, scratch,
 ):
     fill_table(info, table, x_in, faces_in, y_in)
@@ -347,12 +370,16 @@
         ghosts = ghosts_of(FINE, info, table, k, 0)
         inner = start[k] + neighbour_sum(FINE, field, g.at[k], ghosts)
         rest[k] = diagonal[k] * (inner - OMEGA * field)
-    coarsen_blocks(rest[...].reshape(CAP_NEW * 24, FINE.width), scratch)
+    coarsen_blocks(rest[...].reshape(CAP_NEW * 24, FINE.width), spread[...], scratch)
     for k in range(CAP_NEW):
         coarse_s[k] = jnp.zeros((16, 256), F32)
         coarse_s[k, 0:12, :] = weight[k, 0:12, :] * coarse_rows(scratch, k)
         pack_faces(COARSE, coarse_s[k], faces, k, 0)
-    send_faces(info, faces, x_out, y_out)
+    x_first, y_first = info[SEND_X], info[SEND_Y]
+    for j in range(REACH):
+        x_out[j, 0:16] = faces[x_first + j]
+        x_out[j, 16:48] = g_faces[x_first + j]
+        y_out[j] = faces[y_first + j]
 
 
 def total_kernel(info, u_in, g, start, diagonal, row_in, faces_in, x_in, y_in, rows_out, table):
@@ -371,20 +398,27 @@
     rows_out[...] = jnp.broadcast_to(band, rows_out.shape)
 
 
-def solve_kernel(info, rows_in, u_in, u, faces, x_out, y_out):
+def lifted(answer, cell):
+    at = iota((NCOARSE, 1), 0)
+    return jnp.sum(jnp.where(at == cell, answer, 0.0), axis=0, keepdims=True)
+
+
+def solve_kernel(
+    info, rows_in, u_in, g, start, faces_in, x_in, y_in, u, answer_out, faces, x_out, table
+):
+    fill_table(info, table, x_in, faces_in, y_in)
     rows = rows_in[...]
     shape = (NCOARSE, 128)
     row, lane = iota(shape, 0), iota(shape, 1)
     cells = iota((NCOARSE, NCOARSE), 1).astype(F32)
-    band = jnp.zeros(shape, F32)
-    for k in range(CAP_NEW):
-        member = (rows[:, 64 + k : 65 + k] == cells).astype(F32)
-        part = rows if k == 0 else pltpu.roll(rows, 128 - 8 * k, 1)
-        part = jnp.where(lane < 8, part, 0.0)
-        band += lax.dot_general(
-            member, part, (((0,), (0,)), ((), ())),
-            precision=lax.Precision.HIGHEST, preferred_element_type=F32,
-        )
+    member = jnp.concatenate(
+        [(rows[:, 64 + k : 65 + k] == cells).astype(F32) for k in range(CAP_NEW)], axis=0
+    ).astype(jnp.bfloat16)
+    shifts = [rows] + [pltpu.roll(rows, 128 - 8 * k, 1) for k in range(1, CAP_NEW)]
+    band = sum(
+        lax.dot_general(member, part, (((0,), (0,)), ((), ())), preferred_element_type=F32)
+        for part in split_three(jnp.concatenate(shifts, axis=0))
+    )
     matrix = jnp.where(lane == 64, band[:, 7:8], 0.0)
     for o in range(7):
         matrix += jnp.where(lane == row + (o - REACH), band[:, o : o + 1], 0.0)
@@ -401,30 +435,63 @@
         matrix = matrix - drop(matrix, j)
     pivots = jnp.sum(jnp.where(lane == row, matrix, 0.0), axis=1, keepdims=True)
     answer = matrix[:, 64:65] / pivots
-    at = iota((NCOARSE, 1), 0)
+    answer_out[...] = jnp.broadcast_to(answer, shape)
     row, lane = iota((16, 256), 0), iota((16, 256), 1)
     inside = (row < 12) & (lane < 144)
     for k in range(CAP_NEW):
-        lift = jnp.sum(jnp.where(at == info[CELL + k], answer, 0.0), axis=0, keepdims=True)
-        new = u_in[k] + jnp.where(inside, lift, 0.0)
+        lift = lifted(answer, info[CELL + k])
+        slots, *sides = ghosts_of(COARSE, info, table, k, 0)
+        sides = [v + lifted(answer, info[BESIDE + 4 * k + f]) for f, v in enumerate(sides)]
+        field = u_in[k] + jnp.where(inside, lift, 0.0)
+        new = KEEP * field + (start[k] + neighbour_sum(COARSE, field, g.at[k], (slots, *sides)))
         u[k] = new
         pack_faces(COARSE, new, faces, k, 0)
-    send_faces(info, faces, x_out, y_out)
+        faces[k, LIFT_ROW : LIFT_ROW + 1, 64:128] = jnp.broadcast_to(lift, (1, 64))
+    for j in range(REACH):
+        x_out[j] = faces[info[SEND_X] + j]
+
+
+def across_kernel(
+    info, u_in, g, answer_in, x_in, g_in, u, faces, ghosts, y_out, table
+):
+    table[0:REACH] = x_in[...]
+    table[REACH] = jnp.zeros((16, 128), F32)
+    row, lane = iota((16, 256), 0), iota((16, 256), 1)
+    answer = answer_in[...][:, 0:1]
+    for k in range(CAP_NEW):
+        lift = [
+            table[info[OTHER + 4 * k + f], LIFT_ROW : LIFT_ROW + 1, 64:65] for f in range(4)
+        ]
+        new = u_in[k] + jnp.where(row == 0, g[k, 4] * lift[0], 0.0)
+        new += jnp.where(row == 11, g[k, 5] * lift[1], 0.0)
+        new += jnp.where(lane < 12, g[k, 2] * lift[2], 0.0)
+        new += jnp.where((lane >= 132) & (lane < 144), g[k, 3] * lift[3], 0.0)
+        u[k] = new
+        pack_faces(COARSE, new, faces, k, 0)
+    row, lane = iota((16, 128), 0), iota((16, 128), 1)
+    for j in range(REACH):
+        lift = [lifted(answer, info[FACING + 4 * j + f]) for f in range(4)]
+        face = jnp.where(lane < 64, lift[2], lift[3])
+        face = jnp.where(row >= 14, lift[1], jnp.where(row >= 12, lift[0], face))
+        edge = jnp.where(row == 0, lift[0], jnp.where(row == 11, lift[1], 0.0))
+        edge = jnp.where((row == 12) | (row == 14), lift[2], edge)
+        edge = jnp.where((row == 13) | (row == 15), lift[3], edge)
+        ghosts[j] = x_in[j] + face * g_in[j, 16:32] + edge * g_in[j, 32:48]
+        y_out[j] = faces[info[SEND_Y] + j]
 
 
 def refine_kernel(
-    info, e_in, g, start, faces_in, x_in, y_in, u_in, u, faces, x_out, y_out, table, coarse, rest
+    info, e_in, g, start, faces_in, x_in, y_in, u_in, spread, u, faces, x_out, y_out, table, coarse, rest
 ):
     fill_table(info, table, x_in, faces_in, y_in)
     for k in range(CAP_NEW):
         field = e_in[k]
         ghosts = ghosts_of(COARSE, info, table, k, 0)
         coarse[k] = KEEP * field + (start[k] + neighbour_sum(COARSE, field, g.at[k], ghosts))
-    spread = spread_matrix()
-    total = None
-    for part in split_three(coarse[...].reshape(CAP_NEW * 16, 256)):
-        one = jnp.dot(part, spread, preferred_element_type=F32)
-        total = one if total is None else total + one
+    total = sum(
+        jnp.dot(part, spread[...], preferred_element_type=F32)
+        for part in split_two(coarse[...].reshape(CAP_NEW * 16, 256))
+    )
     for k in range(CAP_NEW):
         twelve = total[16 * k : 16 * k + 12, :]
         for t in range(FINE.tiles):
@@ -514,8 +581,10 @@
     coef, faces, x_out, y_out = call(
         collect_kernel, "collect", [fine] + fine_faces, [], (info, coef, y_in, x_in)
     )
-    source, level, coarse_own = call(
-        level_kernel, "level", [fine, coarse, coarse_faces[0]], [sums],
+    source, level, coarse_own, spread = call(
+        level_kernel, "level",
+        [fine, coarse, coarse_faces[0], jax.ShapeDtypeStruct((256, FINE.width), jnp.bfloat16)],
+        [sums],
         (info, source, y_in, x_in, coef),
     )
     x_in, y_in = exchange(x_out, y_out)
@@ -525,9 +594,9 @@
         (info, source, coef, faces, coarse_own, x_in, y_in),
     )
     x_in, y_in = exchange(x_out, y_out)
-    coarse_g, coarse_w, coarse_d, row = call(
+    coarse_g, coarse_w, coarse_d, g_faces, row = call(
         coarse_conduct_kernel, "coarse_conduct",
-        [sds(CAP_NEW, 6, 16, 256), coarse, coarse, sds(1, 128)],
+        [sds(CAP_NEW, 6, 16, 256), coarse, coarse, sds(CAP_NEW, 32, 128), sds(1, 128)],
         [(ABSENT + 1, BOTH_ROWS, 128)],
         (info, level, faces, x_in, y_in),
     )
@@ -548,12 +617,15 @@
 
     x_in, y_in = exchange(x_out, y_out)
     coarse_s, faces, x_out, y_out = call(
-        residual_kernel, "residual", [coarse, *coarse_faces],
+        residual_kernel, "residual",
+        [coarse, coarse_faces[0], sds(REACH, 48, 128), coarse_faces[2]],
         fine_table + [(CAP_NEW, 24, FINE.width), sums],
-        (info, u0, fine_g, fine_s, fine_d, coarse_w, faces, x_in, y_in),
-    )
-    e, faces, x_out, y_out = sweep(
-        COARSE, coarse_s, coarse_g, coarse_s, faces, x_out, y_out, "coarse_pre"
+        (info, u0, fine_g, fine_s, fine_d, coarse_w, spread, g_faces, faces, x_in, y_in),
+    )
+    g_in, y_in = exchange(x_out, y_out)
+    e, faces, x_out, y_out = call(
+        lambda *refs: sweep_kernel(COARSE, *refs), "coarse_pre", [coarse, *coarse_faces],
+        coarse_table, (info, coarse_s, coarse_g, coarse_s, faces, g_in, y_in),
     )
     x_in, y_in = exchange(x_out, y_out)
     rows = call(
@@ -561,15 +633,20 @@
         (info, e, coarse_g, coarse_s, coarse_d, row, faces, x_in, y_in),
     )
     rows = lax.all_to_all(rows, "curve", 0, 0, tiled=True)
-    e, faces, x_out, y_out = call(
-        solve_kernel, "solve", [coarse, *coarse_faces], [], (info, rows, e)
-    )
-    e, faces, x_out, y_out = sweep(COARSE, e, coarse_g, coarse_s, faces, x_out, y_out, "coarse_post")
-    x_in, y_in = exchange(x_out, y_out)
+    e, answer, faces, x_out = call(
+        solve_kernel, "solve", [coarse, sds(NCOARSE, 128), *coarse_faces[:2]], coarse_table,
+        (info, rows, e, coarse_g, coarse_s, faces, x_in, y_in),
+    )
+    x_in = swap(x_out, AXES, 1)
+    e, faces, x_in, y_out = call(
+        across_kernel, "across", [coarse, *coarse_faces], [(REACH + 1, 16, 128)],
+        (info, e, coarse_g, answer, x_in, g_in),
+    )
+    y_in = swap(y_out, AXES, 0)
     u, faces, x_out, y_out = call(
         refine_kernel, "refine", [fine, *fine_faces],
         coarse_table + [(CAP_NEW, 16, 256), (FINE.tiles, 24, 128)],
-        (info, e, coarse_g, coarse_s, faces, x_in, y_in, u0),
+        (info, e, coarse_g, coarse_s, faces, x_in, y_in, u0, spread),
     )
     u, faces, x_out, y_out = sweep(FINE, u, fine_g, fine_s, faces, x_out, y_out, "post")
     x_in, y_in = exchange(x_out, y_out)

time: 130 us -> 125 us (0.962)
  starting transfers between devices: 80 us -> 73.6 us
    ppermute x20 -> x18, starting transfers between devices: 80 us -> 73.6 us  [swap(): lax.ppermute(block, axis, [(i, i + 1) for i in starts] + [(i + 1, i) for...]
    ppermute x20 -> x18, waiting for transfers between devices: 15.7 us -> 16.3 us  [swap(): lax.ppermute(block, axis, [(i, i + 1) for i in starts] + [(i + 1, i) for...]
  transfers between devices with their start and end apart: 20 -> 18, of which waited for: 11 -> 12; matrix products, arithmetic and copies ran while one was open for 0% -> 0% of each run, Pallas kernels for 2% -> 2%
where the time goes in v4:
time: 125 us; the launch traced here: 124 us
  starting transfers between devices  73.6 us (59%)
  Pallas kernels  18.7 us (15%)
  waiting for transfers between devices  16.3 us (13%)
  blocking collectives  15.4 us (12%)
    ppermute x18, starting transfers between devices, swap(): lax.ppermute(block, axis, [(i, i + 1) for i in starts] + [(i + 1, i) for...  73.6 us
    pallas_call x15, Pallas kernels, call(): pl.pallas_call(kernel, out_shape=outs if many else outs[0], in_specs=in_s...  18.7 us
    ppermute x18, waiting for transfers between devices, swap(): lax.ppermute(block, axis, [(i, i + 1) for i in starts] + [(i + 1, i) for...  16.3 us
    all_to_all x1, blocking collectives, body(): rows = lax.all_to_all(rows, 'curve', 0, 0, tiled=True)  15.4 us
  transfers between devices with their start and end apart: 18, of which 12 were waited for; matrix products, arithmetic and copies ran while one was open for 0% of the time, Pallas kernels for 2%

profile of v4, /device:TPU:24, one launch (start us, length us, event | category | flops | bytes accessed | tf_op | source)
XLA Modules:
  0.0 124.3 jit_solution(10702312903725052349)
XLA Ops:
  0.0 2.1 %owners.1 = (f32[2,24,576]{2,1,0:T(8,128)S(1)}, f32[2,24,576]{2,1,0:T(8,128)S(1)}, s32[128]{0:T(128)S(1)}, f32[7,24,576]{2,1,0:T(8,128)S(1)}, f32[7,24,576]{2,1,0:T(8,128)S(1)}) custom-call(s32[1,128]{1,0:T(1,128)} %new_in.1, s32[1,128]{1,0:T(1,128)} %old_in.1, s32[4,128]{1,0:T(4,128)} %bitcast.9, s32[1,128]{1,0:T(1,128)} %map_in.1, f32[7,24,576]{2,1,0:T(8,128)} %rhs_in.1, ...), custom_call_target="tpu_custom_call" | custom-call | flops 10000000 | bytes 4000000 | tf_op jit(solution)/shard_map/owners/pallas_call | solution.py:527
  2.1 1.9 %collective-permute-start = (f32[2,24,576]{2,1,0:T(8,128)S(1)}, f32[2,24,576]{2,1,0:T(8,128)S(1)}, u32[]{:S(2)}, u32[]{:S(2)}) collective-permute-start(f32[2,24,576]{2,1,0:T(8,128)S(1)} %get-tuple-element.63), channel_id=1, source_target_pairs={{0,1},{2,3},{4,5},{6,7},{8,9},{10,11},{12,13},{14,15},{16,17},{18,... | collective-permute-start | bytes 331784 | tf_op jit(solution)/shard_map/ppermute | solution.py:541
  4.0 0.7 collective-permute-start.1
  4.7 0.6 place.1
  5.3 0.0 collective-permute-done.y_in
  5.3 0.6 collect.1
  6.0 13.9 %collective-permute-start.2 = (f32[3,40,128]{2,1,0:T(8,128)S(1)}, f32[3,40,128]{2,1,0:T(8,128)S(1)}, u32[]{:S(2)}, u32[]{:S(2)}) collective-permute-start(f32[3,40,128]{2,1,0:T(8,128)S(1)} %get-tuple-element.70), channel_id=1, source_target_pairs={{1,2},{3,4},{5,6},{7,8},{9,10},{11,12},{13,14},{15,16},{17,18},{19... | collective-permute-start | bytes 184328 | tf_op jit(solution)/shard_map/ppermute | solution.py:541
  19.9 1.9 %collective-permute-start.3 = (f32[3,40,128]{2,1,0:T(8,128)S(1)}, f32[3,40,128]{2,1,0:T(8,128)S(1)}, u32[]{:S(2)}, u32[]{:S(2)}) collective-permute-start(f32[3,40,128]{2,1,0:T(8,128)S(1)} %get-tuple-element.71), channel_id=1, source_target_pairs={{0,1},{2,3},{4,5},{6,7},{8,9},{10,11},{12,13},{14,15},{16,17},{18,... | collective-permute-start | bytes 184328 | tf_op jit(solution)/shard_map/ppermute | solution.py:541
  21.8 1.0 level.1
  22.8 0.0 collective-permute-done.2.x_in
  22.8 0.2 collective-permute-done.3.y_in
  23.0 1.3 %conduct.1 = (f32[5,6,24,640]{3,2,1,0:T(8,128)S(1)}, f32[5,24,640]{2,1,0:T(8,128)S(1)}, f32[5,24,640]{2,1,0:T(8,128)S(1)}, f32[5,24,640]{2,1,0:T(8,128)S(1)}, f3...) custom-call(s32[128]{0:T(128)S(1)} %get-tuple-element.59.info.refs_0_, ...), custom_call_target="tpu_custom_call" | custom-call | flops 10000000 | bytes 4000000 | tf_op jit(solution)/shard_map/conduct/pallas_call | solution.py:527
  24.3 7.8 %collective-permute-start.4 = (f32[3,56,128]{2,1,0:T(8,128)S(1)}, f32[3,56,128]{2,1,0:T(8,128)S(1)}, u32[]{:S(2)}, u32[]{:S(2)}) collective-permute-start(f32[3,56,128]{2,1,0:T(8,128)S(1)} %get-tuple-element.76), channel_id=1, source_target_pairs={{1,2},{3,4},{5,6},{7,8},{9,10},{11,12},{13,14},{15,16},{17,18},{19... | collective-permute-start | bytes 258056 | tf_op jit(solution)/shard_map/ppermute | solution.py:541
  32.1 1.9 %collective-permute-start.5 = (f32[3,56,128]{2,1,0:T(8,128)S(1)}, f32[3,56,128]{2,1,0:T(8,128)S(1)}, u32[]{:S(2)}, u32[]{:S(2)}) collective-permute-start(f32[3,56,128]{2,1,0:T(8,128)S(1)} %get-tuple-element.77), channel_id=1, source_target_pairs={{0,1},{2,3},{4,5},{6,7},{8,9},{10,11},{12,13},{14,15},{16,17},{18,... | collective-permute-start | bytes 258056 | tf_op jit(solution)/shard_map/ppermute | solution.py:541
  34.0 0.3 collective-permute-done.4.refs_5_.x_in
  34.4 0.9 collective-permute-done.5.refs_6_.y_in
  35.3 1.0 pre.1
  36.3 6.8 %collective-permute-start.6 = (f32[3,40,128]{2,1,0:T(8,128)S(1)}, f32[3,40,128]{2,1,0:T(8,128)S(1)}, u32[]{:S(2)}, u32[]{:S(2)}) collective-permute-start(f32[3,40,128]{2,1,0:T(8,128)S(1)} %get-tuple-element.85), channel_id=1, source_target_pairs={{1,2},{3,4},{5,6},{7,8},{9,10},{11,12},{13,14},{15,16},{17,18},{19... | collective-permute-start | bytes 184328 | tf_op jit(solution)/shard_map/ppermute | solution.py:541
  43.2 1.9 %collective-permute-start.7 = (f32[3,40,128]{2,1,0:T(8,128)S(1)}, f32[3,40,128]{2,1,0:T(8,128)S(1)}, u32[]{:S(2)}, u32[]{:S(2)}) collective-permute-start(f32[3,40,128]{2,1,0:T(8,128)S(1)} %get-tuple-element.86), channel_id=1, source_target_pairs={{0,1},{2,3},{4,5},{6,7},{8,9},{10,11},{12,13},{14,15},{16,17},{18,... | collective-permute-start | bytes 184328 | tf_op jit(solution)/shard_map/ppermute | solution.py:541
  45.1 1.0 coarse_conduct.1
  46.1 0.2 collective-permute-done.7.y_in
  46.3 1.3 %residual.1 = (f32[5,16,256]{2,1,0:T(8,128)S(1)}, f32[5,16,128]{2,1,0:T(8,128)S(1)}, f32[3,48,128]{2,1,0:T(8,128)S(1)}, f32[3,16,128]{2,1,0:T(8,128)S(1)}) custom-call(s32[128]{0:T(128)S(1)} %get-tuple-element.59.info.refs_0_, f32[5,24,640]{2,1,0:T(8,128)S(1)} %get-tuple-element.78.u_in, f32[5,6,24,640]{3,2,1,0:T(8,128)S(1)} %get-tuple-element.73.refs_2_.g, ...), custom_call_target="tpu_custom_call" | custom-call | flops 10000000 | bytes 4000000 | tf_op jit(solution)/shard_map/residual/pallas_call | solution.py:527
  47.6 6.6 %collective-permute-start.8 = (f32[3,48,128]{2,1,0:T(8,128)S(1)}, f32[3,48,128]{2,1,0:T(8,128)S(1)}, u32[]{:S(2)}, u32[]{:S(2)}) collective-permute-start(f32[3,48,128]{2,1,0:T(8,128)S(1)} %get-tuple-element.90), channel_id=1, source_target_pairs={{1,2},{3,4},{5,6},{7,8},{9,10},{11,12},{13,14},{15,16},{17,18},{19... | collective-permute-start | bytes 221192 | tf_op jit(solution)/shard_map/ppermute | solution.py:541
  54.2 1.9 %collective-permute-start.9 = (f32[3,16,128]{2,1,0:T(8,128)S(1)}, f32[3,16,128]{2,1,0:T(8,128)S(1)}, u32[]{:S(2)}, u32[]{:S(2)}) collective-permute-start(f32[3,16,128]{2,1,0:T(8,128)S(1)} %get-tuple-element.91), channel_id=1, source_target_pairs={{0,1},{2,3},{4,5},{6,7},{8,9},{10,11},{12,13},{14,15},{16,17},{18,... | collective-permute-start | bytes 73736 | tf_op jit(solution)/shard_map/ppermute | solution.py:541
  56.2 1.2 collective-permute-done.9.refs_6_
  57.3 0.2 collective-permute-done.8.refs_5_.g_in
  57.5 0.8 coarse_pre.1
  58.3 6.6 %collective-permute-start.10 = (f32[3,16,128]{2,1,0:T(8,128)S(1)}, f32[3,16,128]{2,1,0:T(8,128)S(1)}, u32[]{:S(2)}, u32[]{:S(2)}) collective-permute-start(f32[3,16,128]{2,1,0:T(8,128)S(1)} %get-tuple-element.96), channel_id=1, source_target_pairs={{1,2},{3,4},{5,6},{7,8},{9,10},{11,12},{13,14},{15,16},{17,18},{19... | collective-permute-start | bytes 73736 | tf_op jit(solution)/shard_map/ppermute | solution.py:541
  65.0 1.9 %collective-permute-start.11 = (f32[3,16,128]{2,1,0:T(8,128)S(1)}, f32[3,16,128]{2,1,0:T(8,128)S(1)}, u32[]{:S(2)}, u32[]{:S(2)}) collective-permute-start(f32[3,16,128]{2,1,0:T(8,128)S(1)} %get-tuple-element.97), channel_id=1, source_target_pairs={{0,1},{2,3},{4,5},{6,7},{8,9},{10,11},{12,13},{14,15},{16,17},{18,... | collective-permute-start | bytes 73736 | tf_op jit(solution)/shard_map/ppermute | solution.py:541
  66.9 0.8 collective-permute-done.10.x_in
  67.7 0.3 collective-permute-done.11.y_in
  68.0 0.9 totals.1
  68.9 15.4 %all_to_all.11 = f32[32,1,128]{2,1,0:T(1,128)S(1)} all-to-all(f32[32,1,128]{2,1,0:T(1,128)S(1)} %bitcast.7), channel_id=1, replica_groups=mesh['group'=16,'curve'=32] {'curve'}, dimensions={0} | all-to-all | bytes 32768 | tf_op jit(solution)/shard_map/all_to_all | solution.py:635
  84.3 3.5 %solve.1 = (f32[5,16,256]{2,1,0:T(8,128)S(1)}, f32[32,128]{1,0:T(8,128)S(1)}, f32[5,16,128]{2,1,0:T(8,128)}, f32[3,16,128]{2,1,0:T(8,128)S(1)}) custom-call(s32[128]{0:T(128)S(1)} %get-tuple-element.59.info.refs_0_, f32[32,128]{1,0:T(8,128)S(1)} %bitcast.8, f32[5,16,256]{2,1,0:T(8,128)S(1)} %get-tuple-element.92.u_in, ...), custom_call_target="tpu_custom_call" | custom-call | flops 10000000 | bytes 4000000 | tf_op jit(solution)/shard_map/solve/pallas_call | solution.py:527
  87.8 4.6 %collective-permute-start.12 = (f32[3,16,128]{2,1,0:T(8,128)S(1)}, f32[3,16,128]{2,1,0:T(8,128)S(1)}, u32[]{:S(2)}, u32[]{:S(2)}) collective-permute-start(f32[3,16,128]{2,1,0:T(8,128)S(1)} %get-tuple-element.100), channel_id=1, source_target_pairs={{1,2},{3,4},{5,6},{7,8},{9,10},{11,12},{13,14},{15,16},{17,18},{19... | collective-permute-start | bytes 73736 | tf_op jit(solution)/shard_map/ppermute | solution.py:541
  92.5 4.7 %collective-permute-done.12.x_in = f32[3,16,128]{2,1,0:T(8,128)S(1)} collective-permute-done((f32[3,16,128]{2,1,0:T(8,128)S(1)}, f32[3,16,128]{2,1,0:T(8,128)S(1)}, u32[]{:S(2)}, u32[]{:S(2)}) %collective-permute-start.12) | collective-permute-done | bytes 24608 | tf_op jit(solution)/shard_map/ppermute | solution.py:541
  97.2 0.8 across.1
  97.9 1.9 %collective-permute-start.13 = (f32[3,16,128]{2,1,0:T(8,128)S(1)}, f32[3,16,128]{2,1,0:T(8,128)S(1)}, u32[]{:S(2)}, u32[]{:S(2)}) collective-permute-start(f32[3,16,128]{2,1,0:T(8,128)S(1)} %get-tuple-element.104), channel_id=1, source_target_pairs={{0,1},{2,3},{4,5},{6,7},{8,9},{10,11},{12,13},{14,15},{16,17},{18,... | collective-permute-start | bytes 73736 | tf_op jit(solution)/shard_map/ppermute | solution.py:541
  99.8 1.2 collective-permute-done.13.y_in
  101.0 1.0 refine.1
  102.0 4.7 %collective-permute-start.14 = (f32[3,40,128]{2,1,0:T(8,128)S(1)}, f32[3,40,128]{2,1,0:T(8,128)S(1)}, u32[]{:S(2)}, u32[]{:S(2)}) collective-permute-start(f32[3,40,128]{2,1,0:T(8,128)S(1)} %get-tuple-element.107), channel_id=1, source_target_pairs={{1,2},{3,4},{5,6},{7,8},{9,10},{11,12},{13,14},{15,16},{17,18},{19... | collective-permute-start | bytes 184328 | tf_op jit(solution)/shard_map/ppermute | solution.py:541
  106.6 1.9 %collective-permute-start.15 = (f32[3,40,128]{2,1,0:T(8,128)S(1)}, f32[3,40,128]{2,1,0:T(8,128)S(1)}, u32[]{:S(2)}, u32[]{:S(2)}) collective-permute-start(f32[3,40,128]{2,1,0:T(8,128)S(1)} %get-tuple-element.108), channel_id=1, source_target_pairs={{0,1},{2,3},{4,5},{6,7},{8,9},{10,11},{12,13},{14,15},{16,17},{18,... | collective-permute-start | bytes 184328 | tf_op jit(solution)/shard_map/ppermute | solution.py:541
  108.6 3.2 %collective-permute-done.14.refs_5_ = f32[3,40,128]{2,1,0:T(8,128)S(1)} collective-permute-done((f32[3,40,128]{2,1,0:T(8,128)S(1)}, f32[3,40,128]{2,1,0:T(8,128)S(1)}, u32[]{:S(2)}, u32[]{:S(2)}) %collective-permute-start.14) | collective-permute-done | bytes 61472 | tf_op jit(solution)/shard_map/ppermute | solution.py:541
  111.7 1.0 post.1
  112.8 4.7 %collective-permute-start.16 = (f32[3,40,128]{2,1,0:T(8,128)S(1)}, f32[3,40,128]{2,1,0:T(8,128)S(1)}, u32[]{:S(2)}, u32[]{:S(2)}) collective-permute-start(f32[3,40,128]{2,1,0:T(8,128)S(1)} %get-tuple-element.111), channel_id=1, source_target_pairs={{1,2},{3,4},{5,6},{7,8},{9,10},{11,12},{13,14},{15,16},{17,18},{19... | collective-permute-start | bytes 184328 | tf_op jit(solution)/shard_map/ppermute | solution.py:541
  117.4 1.9 %collective-permute-start.17 = (f32[3,40,128]{2,1,0:T(8,128)S(1)}, f32[3,40,128]{2,1,0:T(8,128)S(1)}, u32[]{:S(2)}, u32[]{:S(2)}) collective-permute-start(f32[3,40,128]{2,1,0:T(8,128)S(1)} %get-tuple-element.112), channel_id=1, source_target_pairs={{0,1},{2,3},{4,5},{6,7},{8,9},{10,11},{12,13},{14,15},{16,17},{18,... | collective-permute-start | bytes 184328 | tf_op jit(solution)/shard_map/ppermute | solution.py:541
  119.4 3.2 %collective-permute-done.16.x_in = f32[3,40,128]{2,1,0:T(8,128)S(1)} collective-permute-done((f32[3,40,128]{2,1,0:T(8,128)S(1)}, f32[3,40,128]{2,1,0:T(8,128)S(1)}, u32[]{:S(2)}, u32[]{:S(2)}) %collective-permute-start.16) | collective-permute-done | bytes 61472 | tf_op jit(solution)/shard_map/ppermute | solution.py:541
  122.5 1.7 %last.1 = f32[5,24,576]{2,1,0:T(8,128)} custom-call(s32[128]{0:T(128)S(1)} %get-tuple-element.59.info.refs_0_, f32[5,24,640]{2,1,0:T(8,128)S(1)} %get-tuple-element.109.u_in, f32[5,6,24,640]{3,2,1,0:T(8,128)S(1)} %get-tuple-element.73.refs_2_.g, f32[5,24,640]{2,1,0:T(8,128)S(1)} %get-tuple-element.74.refs_3_.start, ...), custom_call_target="tpu_custom_call" | custom-call | flops 10000000 | bytes 4000000 | tf_op jit(solution)/shard_map/last/pallas_call | solution.py:527
  (4 shorter events, 0.0 us)
Async XLA Ops:
  2.1 3.2 %collective-permute-start = (f32[2,24,576]{2,1,0:T(8,128)S(1)}, f32[2,24,576]{2,1,0:T(8,128)S(1)}, u32[]{:S(2)}, u32[]{:S(2)}) collective-permute-start(f32[2,24,576]{2,1,0:T(8,128)S(1)} %get-tuple-element.63), channel_id=1, source_target_pairs={{0,1},{2,3},{4,5},{6,7},{8,9},{10,11},{12,13},{14,15},{16,17},{18,... | collective-permute-start | bytes 331784 | tf_op jit(solution)/shard_map/ppermute | solution.py:541
  4.0 1.3 %collective-permute-start.1 = (f32[2,24,576]{2,1,0:T(8,128)S(1)}, f32[2,24,576]{2,1,0:T(8,128)S(1)}, u32[]{:S(2)}, u32[]{:S(2)}) collective-permute-start(f32[2,24,576]{2,1,0:T(8,128)S(1)} %get-tuple-element.64), channel_id=1, source_target_pairs={{1,2},{3,4},{5,6},{7,8},{9,10},{11,12},{13,14},{15,16},{17,18},{19... | collective-permute-start | bytes 331784 | tf_op jit(solution)/shard_map/ppermute | solution.py:541
  6.0 16.9 %collective-permute-start.2 = (f32[3,40,128]{2,1,0:T(8,128)S(1)}, f32[3,40,128]{2,1,0:T(8,128)S(1)}, u32[]{:S(2)}, u32[]{:S(2)}) collective-permute-start(f32[3,40,128]{2,1,0:T(8,128)S(1)} %get-tuple-element.70), channel_id=1, source_target_pairs={{1,2},{3,4},{5,6},{7,8},{9,10},{11,12},{13,14},{15,16},{17,18},{19... | collective-permute-start | bytes 184328 | tf_op jit(solution)/shard_map/ppermute | solution.py:541
  19.9 3.1 %collective-permute-start.3 = (f32[3,40,128]{2,1,0:T(8,128)S(1)}, f32[3,40,128]{2,1,0:T(8,128)S(1)}, u32[]{:S(2)}, u32[]{:S(2)}) collective-permute-start(f32[3,40,128]{2,1,0:T(8,128)S(1)} %get-tuple-element.71), channel_id=1, source_target_pairs={{0,1},{2,3},{4,5},{6,7},{8,9},{10,11},{12,13},{14,15},{16,17},{18,... | collective-permute-start | bytes 184328 | tf_op jit(solution)/shard_map/ppermute | solution.py:541
  24.3 10.0 %collective-permute-start.4 = (f32[3,56,128]{2,1,0:T(8,128)S(1)}, f32[3,56,128]{2,1,0:T(8,128)S(1)}, u32[]{:S(2)}, u32[]{:S(2)}) collective-permute-start(f32[3,56,128]{2,1,0:T(8,128)S(1)} %get-tuple-element.76), channel_id=1, source_target_pairs={{1,2},{3,4},{5,6},{7,8},{9,10},{11,12},{13,14},{15,16},{17,18},{19... | collective-permute-start | bytes 258056 | tf_op jit(solution)/shard_map/ppermute | solution.py:541
  32.1 3.2 %collective-permute-start.5 = (f32[3,56,128]{2,1,0:T(8,128)S(1)}, f32[3,56,128]{2,1,0:T(8,128)S(1)}, u32[]{:S(2)}, u32[]{:S(2)}) collective-permute-start(f32[3,56,128]{2,1,0:T(8,128)S(1)} %get-tuple-element.77), channel_id=1, source_target_pairs={{0,1},{2,3},{4,5},{6,7},{8,9},{10,11},{12,13},{14,15},{16,17},{18,... | collective-permute-start | bytes 258056 | tf_op jit(solution)/shard_map/ppermute | solution.py:541
  36.3 9.8 %collective-permute-start.6 = (f32[3,40,128]{2,1,0:T(8,128)S(1)}, f32[3,40,128]{2,1,0:T(8,128)S(1)}, u32[]{:S(2)}, u32[]{:S(2)}) collective-permute-start(f32[3,40,128]{2,1,0:T(8,128)S(1)} %get-tuple-element.85), channel_id=1, source_target_pairs={{1,2},{3,4},{5,6},{7,8},{9,10},{11,12},{13,14},{15,16},{17,18},{19... | collective-permute-start | bytes 184328 | tf_op jit(solution)/shard_map/ppermute | solution.py:541
  43.2 3.1 %collective-permute-start.7 = (f32[3,40,128]{2,1,0:T(8,128)S(1)}, f32[3,40,128]{2,1,0:T(8,128)S(1)}, u32[]{:S(2)}, u32[]{:S(2)}) collective-permute-start(f32[3,40,128]{2,1,0:T(8,128)S(1)} %get-tuple-element.86), channel_id=1, source_target_pairs={{0,1},{2,3},{4,5},{6,7},{8,9},{10,11},{12,13},{14,15},{16,17},{18,... | collective-permute-start | bytes 184328 | tf_op jit(solution)/shard_map/ppermute | solution.py:541
  47.6 9.9 %collective-permute-start.8 = (f32[3,48,128]{2,1,0:T(8,128)S(1)}, f32[3,48,128]{2,1,0:T(8,128)S(1)}, u32[]{:S(2)}, u32[]{:S(2)}) collective-permute-start(f32[3,48,128]{2,1,0:T(8,128)S(1)} %get-tuple-element.90), channel_id=1, source_target_pairs={{1,2},{3,4},{5,6},{7,8},{9,10},{11,12},{13,14},{15,16},{17,18},{19... | collective-permute-start | bytes 221192 | tf_op jit(solution)/shard_map/ppermute | solution.py:541
  54.2 3.1 %collective-permute-start.9 = (f32[3,16,128]{2,1,0:T(8,128)S(1)}, f32[3,16,128]{2,1,0:T(8,128)S(1)}, u32[]{:S(2)}, u32[]{:S(2)}) collective-permute-start(f32[3,16,128]{2,1,0:T(8,128)S(1)} %get-tuple-element.91), channel_id=1, source_target_pairs={{0,1},{2,3},{4,5},{6,7},{8,9},{10,11},{12,13},{14,15},{16,17},{18,... | collective-permute-start | bytes 73736 | tf_op jit(solution)/shard_map/ppermute | solution.py:541
  58.3 9.4 %collective-permute-start.10 = (f32[3,16,128]{2,1,0:T(8,128)S(1)}, f32[3,16,128]{2,1,0:T(8,128)S(1)}, u32[]{:S(2)}, u32[]{:S(2)}) collective-permute-start(f32[3,16,128]{2,1,0:T(8,128)S(1)} %get-tuple-element.96), channel_id=1, source_target_pairs={{1,2},{3,4},{5,6},{7,8},{9,10},{11,12},{13,14},{15,16},{17,18},{19... | collective-permute-start | bytes 73736 | tf_op jit(solution)/shard_map/ppermute | solution.py:541
  65.0 3.1 %collective-permute-start.11 = (f32[3,16,128]{2,1,0:T(8,128)S(1)}, f32[3,16,128]{2,1,0:T(8,128)S(1)}, u32[]{:S(2)}, u32[]{:S(2)}) collective-permute-start(f32[3,16,128]{2,1,0:T(8,128)S(1)} %get-tuple-element.97), channel_id=1, source_target_pairs={{0,1},{2,3},{4,5},{6,7},{8,9},{10,11},{12,13},{14,15},{16,17},{18,... | collective-permute-start | bytes 73736 | tf_op jit(solution)/shard_map/ppermute | solution.py:541
  87.8 9.4 %collective-permute-start.12 = (f32[3,16,128]{2,1,0:T(8,128)S(1)}, f32[3,16,128]{2,1,0:T(8,128)S(1)}, u32[]{:S(2)}, u32[]{:S(2)}) collective-permute-start(f32[3,16,128]{2,1,0:T(8,128)S(1)} %get-tuple-element.100), channel_id=1, source_target_pairs={{1,2},{3,4},{5,6},{7,8},{9,10},{11,12},{13,14},{15,16},{17,18},{19... | collective-permute-start | bytes 73736 | tf_op jit(solution)/shard_map/ppermute | solution.py:541
  97.9 3.1 %collective-permute-start.13 = (f32[3,16,128]{2,1,0:T(8,128)S(1)}, f32[3,16,128]{2,1,0:T(8,128)S(1)}, u32[]{:S(2)}, u32[]{:S(2)}) collective-permute-start(f32[3,16,128]{2,1,0:T(8,128)S(1)} %get-tuple-element.104), channel_id=1, source_target_pairs={{0,1},{2,3},{4,5},{6,7},{8,9},{10,11},{12,13},{14,15},{16,17},{18,... | collective-permute-start | bytes 73736 | tf_op jit(solution)/shard_map/ppermute | solution.py:541
  102.0 9.8 %collective-permute-start.14 = (f32[3,40,128]{2,1,0:T(8,128)S(1)}, f32[3,40,128]{2,1,0:T(8,128)S(1)}, u32[]{:S(2)}, u32[]{:S(2)}) collective-permute-start(f32[3,40,128]{2,1,0:T(8,128)S(1)} %get-tuple-element.107), channel_id=1, source_target_pairs={{1,2},{3,4},{5,6},{7,8},{9,10},{11,12},{13,14},{15,16},{17,18},{19... | collective-permute-start | bytes 184328 | tf_op jit(solution)/shard_map/ppermute | solution.py:541
  106.6 5.1 %collective-permute-start.15 = (f32[3,40,128]{2,1,0:T(8,128)S(1)}, f32[3,40,128]{2,1,0:T(8,128)S(1)}, u32[]{:S(2)}, u32[]{:S(2)}) collective-permute-start(f32[3,40,128]{2,1,0:T(8,128)S(1)} %get-tuple-element.108), channel_id=1, source_target_pairs={{0,1},{2,3},{4,5},{6,7},{8,9},{10,11},{12,13},{14,15},{16,17},{18,... | collective-permute-start | bytes 184328 | tf_op jit(solution)/shard_map/ppermute | solution.py:541
  112.8 9.8 %collective-permute-start.16 = (f32[3,40,128]{2,1,0:T(8,128)S(1)}, f32[3,40,128]{2,1,0:T(8,128)S(1)}, u32[]{:S(2)}, u32[]{:S(2)}) collective-permute-start(f32[3,40,128]{2,1,0:T(8,128)S(1)} %get-tuple-element.111), channel_id=1, source_target_pairs={{1,2},{3,4},{5,6},{7,8},{9,10},{11,12},{13,14},{15,16},{17,18},{19... | collective-permute-start | bytes 184328 | tf_op jit(solution)/shard_map/ppermute | solution.py:541
  117.4 5.1 %collective-permute-start.17 = (f32[3,40,128]{2,1,0:T(8,128)S(1)}, f32[3,40,128]{2,1,0:T(8,128)S(1)}, u32[]{:S(2)}, u32[]{:S(2)}) collective-permute-start(f32[3,40,128]{2,1,0:T(8,128)S(1)} %get-tuple-element.112), channel_id=1, source_target_pairs={{0,1},{2,3},{4,5},{6,7},{8,9},{10,11},{12,13},{14,15},{16,17},{18,... | collective-permute-start | bytes 184328 | tf_op jit(solution)/shard_map/ppermute | solution.py:541

commit v5 on v4

--- a/solution.py
+++ b/solution.py
@@ -94,6 +94,32 @@
     y_low = pltpu.roll(table[row[2], pl.ds(base, lev.rows), :], 128 - lev.high_at, 1)
     y_high = pltpu.roll(table[row[3], pl.ds(base, lev.rows), :], lev.last, 1)
     return row, x_low, x_high, y_low, y_high
+
+
+def interior_sum(lev, field, g):
+    rows, width, side = lev.rows, lev.width, lev.side
+    row = iota((rows, width), 0)
+    total = g[0] * pltpu.roll(field, 1, 1) + g[1] * pltpu.roll(field, width - 1, 1)
+    total += g[2] * pltpu.roll(field, side, 1) + g[3] * pltpu.roll(field, width - side, 1)
+    total += g[4] * jnp.where(row == 0, 0.0, pltpu.roll(field, 1, 0))
+    return total + g[5] * jnp.where(row == side - 1, 0.0, pltpu.roll(field, rows - 1, 0))
+
+
+def add_ghosts(lev, out, g, ghosts):
+    _, x_low, x_high, y_low, y_high = ghosts
+    last, tail = lev.side - 1, lev.width - 128
+    lane = iota((lev.rows, 128), 1)
+    on_high = (lane >= lev.last) & (lane < lev.last + lev.side)
+    out[0:1, :] += g[4, 0:1, :] * x_low
+    out[last : last + 1, :] += g[5, last : last + 1, :] * x_high
+    out[:, 0:128] += jnp.where(lane < lev.side, g[2, :, 0:128] * y_low, 0.0)
+    out[:, tail:] += jnp.where(on_high, g[3, :, tail:] * y_high, 0.0)
+
+
+def inner_kernel(u_in, g, start, part):
+    for k in range(CAP_NEW):
+        field = u_in[k]
+        part[k] = KEEP * field + (start[k] + interior_sum(FINE, field, g.at[k]))
 
 
 def neighbour_sum(lev, field, g, ghosts):
@@ -314,7 +340,7 @@
 
 
 def coarse_conduct_kernel(
-    info, level, faces_in, x_in, y_in, coarse_g, coarse_w, coarse_d, g_faces, row_out, table
+    info, level, faces_in, x_in, y_in, coarse_g, coarse_w, coarse_d, alpha, g_faces, row_out, table
 ):
     fill_table(info, table, x_in, faces_in, y_in)
     lane_row = iota((1, 128), 1)
@@ -326,6 +352,10 @@
         for i in range(6):
             coarse_g[k, i] = g[i]
         coarse_w[k] = weight
+        one = g[0] + g[1]
+        one += jnp.where(lane < 12, 0.0, g[2]) + jnp.where(high_y, 0.0, g[3])
+        one += jnp.where(row == 0, 0.0, g[4]) + jnp.where(row == 11, 0.0, g[5])
+        alpha[k] = jnp.where(inside, KEEP + one, 0.0)
         pack_fields(COARSE, g[2], g[4], g_faces, k, 0, g[3], g[5])
         low_y = jnp.where(lane < 12, g[2], 0.0)
         x_edge = jnp.where(lane >= 132, g[3], low_y)
@@ -349,27 +379,35 @@
     row_out[...] = band
 
 
-def sweep_kernel(lev, info, u_in, g, start, faces_in, x_in, y_in, u, faces, x_out, y_out, table):
+def sweep_kernel(info, u_in, g, start, faces_in, x_in, y_in, u, faces, x_out, y_out, table):
     fill_table(info, table, x_in, faces_in, y_in)
     for k in range(CAP_NEW):
         field = u_in[k]
-        ghosts = ghosts_of(lev, info, table, k, 0)
-        new = KEEP * field + (start[k] + neighbour_sum(lev, field, g.at[k], ghosts))
+        ghosts = ghosts_of(COARSE, info, table, k, 0)
+        new = KEEP * field + (start[k] + neighbour_sum(COARSE, field, g.at[k], ghosts))
         u[k] = new
-        pack_faces(lev, new, faces, k, 0)
+        pack_faces(COARSE, new, faces, k, 0)
     send_faces(info, faces, x_out, y_out)
 
 
+def finish_kernel(info, part, g, faces_in, x_in, y_in, u, faces, x_out, y_out, table):
+    fill_table(info, table, x_in, faces_in, y_in)
+    for k in range(CAP_NEW):
+        u[k] = part[k]
+        add_ghosts(FINE, u.at[k], g.at[k], ghosts_of(FINE, info, table, k, 0))
+        pack_faces(FINE, u[k], faces, k, 0)
+    send_faces(info, faces, x_out, y_out)
+
+
 def residual_kernel(
-    info, u_in, g, start, diagonal, weight, spread, g_faces, faces_in, x_in, y_in,
+    info, u_in, part, g, diagonal, weight, spread, g_faces, faces_in, x_in, y_in,
     coarse_s, faces, x_out, y_out, table, rest, scratch,
 ):
     fill_table(info, table, x_in, faces_in, y_in)
     for k in range(CAP_NEW):
-        field = u_in[k]
-        ghosts = ghosts_of(FINE, info, table, k, 0)
-        inner = start[k] + neighbour_sum(FINE, field, g.at[k], ghosts)
-        rest[k] = diagonal[k] * (inner - OMEGA * field)
+        rest[k] = part[k]
+        add_ghosts(FINE, rest.at[k], g.at[k], ghosts_of(FINE, info, table, k, 0))
+        rest[k] = diagonal[k] * (rest[k] - u_in[k])
     coarsen_blocks(rest[...].reshape(CAP_NEW * 24, FINE.width), spread[...], scratch)
     for k in range(CAP_NEW):
         coarse_s[k] = jnp.zeros((16, 256), F32)
@@ -382,7 +420,9 @@
         y_out[j] = faces[y_first + j]
 
 
-def total_kernel(info, u_in, g, start, diagonal, row_in, faces_in, x_in, y_in, rows_out, table):
+def total_kernel(
+    info, u_in, g, start, diagonal, row_in, faces_in, x_in, y_in, rows_out, swept, table
+):
     fill_table(info, table, x_in, faces_in, y_in)
     lane_row = iota((1, 128), 1)
     row, lane = iota((16, 256), 0), iota((16, 256), 1)
@@ -392,6 +432,7 @@
         field = u_in[k]
         ghosts = ghosts_of(COARSE, info, table, k, 0)
         inner = start[k] + neighbour_sum(COARSE, field, g.at[k], ghosts)
+        swept[k] = KEEP * field + inner
         rest = jnp.where(inside, diagonal[k] * (inner - OMEGA * field), 0.0)
         occupied = k < info[HELD]
         band += jnp.where((lane_row == 8 * k + 7) & occupied, both_totals(rest), 0.0)
@@ -399,14 +440,25 @@
 
 
 def lifted(answer, cell):
-    at = iota((NCOARSE, 1), 0)
+    at = iota((NCOARSE, 128), 0)
     return jnp.sum(jnp.where(at == cell, answer, 0.0), axis=0, keepdims=True)
 
 
+def wide(line):
+    return jnp.concatenate([line, line], axis=1)
+
+
+def surface_lift(g, lift):
+    row, lane = iota((16, 256), 0), iota((16, 256), 1)
+    total = jnp.where(row == 0, g[4] * lift[0], 0.0)
+    total += jnp.where(row == 11, g[5] * lift[1], 0.0)
+    total += jnp.where(lane < 12, g[2] * lift[2], 0.0)
+    return total + jnp.where((lane >= 132) & (lane < 144), g[3] * lift[3], 0.0)
+
+
 def solve_kernel(
-    info, rows_in, u_in, g, start, faces_in, x_in, y_in, u, answer_out, faces, x_out, table
+    info, rows_in, swept, g, alpha, u, answer_out, faces, x_out
 ):
-    fill_table(info, table, x_in, faces_in, y_in)
     rows = rows_in[...]
     shape = (NCOARSE, 128)
     row, lane = iota(shape, 0), iota(shape, 1)
@@ -423,30 +475,26 @@
     for o in range(7):
         matrix += jnp.where(lane == row + (o - REACH), band[:, o : o + 1], 0.0)
 
-    def drop(current, j):
-        pivot = current[j : j + 1, :]
-        share = current[:, j : j + 1] / pivot[:, j : j + 1]
-        return jnp.where(iota((NCOARSE, 1), 0) == j, 0.0, share) * pivot
-
-    apart = (NCOARSE - REACH - 1) // 2
-    for j in range(apart):
-        matrix = matrix - (drop(matrix, j) + drop(matrix, NCOARSE - 1 - j))
-    for j in range(apart, NCOARSE - apart):
-        matrix = matrix - drop(matrix, j)
+    lists = [[i for i in (t, 9 + t, 18 + t, 27 + t) if i < NCOARSE] for t in range(6)]
+    lists += [[6 + t, 24 + t] for t in range(REACH)] + [[15 + t] for t in range(REACH)]
+    for pivots in lists:
+        drop = None
+        for j in pivots:
+            column = jnp.broadcast_to(matrix[:, j : j + 1], shape)
+            scaled = matrix[j : j + 1, :] / column[j : j + 1, :]
+            one = jnp.where(row == j, 0.0, column) * scaled
+            drop = one if drop is None else drop + one
+        matrix = matrix - drop
     pivots = jnp.sum(jnp.where(lane == row, matrix, 0.0), axis=1, keepdims=True)
-    answer = matrix[:, 64:65] / pivots
-    answer_out[...] = jnp.broadcast_to(answer, shape)
-    row, lane = iota((16, 256), 0), iota((16, 256), 1)
-    inside = (row < 12) & (lane < 144)
+    answer = jnp.broadcast_to(matrix[:, 64:65], shape) / jnp.broadcast_to(pivots, shape)
+    answer_out[...] = answer
     for k in range(CAP_NEW):
         lift = lifted(answer, info[CELL + k])
-        slots, *sides = ghosts_of(COARSE, info, table, k, 0)
-        sides = [v + lifted(answer, info[BESIDE + 4 * k + f]) for f, v in enumerate(sides)]
-        field = u_in[k] + jnp.where(inside, lift, 0.0)
-        new = KEEP * field + (start[k] + neighbour_sum(COARSE, field, g.at[k], (slots, *sides)))
+        beside = [wide(lifted(answer, info[BESIDE + 4 * k + f])) for f in range(4)]
+        new = swept[k] + wide(lift) * alpha[k] + surface_lift(g.at[k], beside)
         u[k] = new
         pack_faces(COARSE, new, faces, k, 0)
-        faces[k, LIFT_ROW : LIFT_ROW + 1, 64:128] = jnp.broadcast_to(lift, (1, 64))
+        faces[k, LIFT_ROW : LIFT_ROW + 1, 64:128] = lift[:, 64:128]
     for j in range(REACH):
         x_out[j] = faces[info[SEND_X] + j]
 
@@ -456,16 +504,12 @@
 ):
     table[0:REACH] = x_in[...]
     table[REACH] = jnp.zeros((16, 128), F32)
-    row, lane = iota((16, 256), 0), iota((16, 256), 1)
-    answer = answer_in[...][:, 0:1]
-    for k in range(CAP_NEW):
-        lift = [
-            table[info[OTHER + 4 * k + f], LIFT_ROW : LIFT_ROW + 1, 64:65] for f in range(4)
-        ]
-        new = u_in[k] + jnp.where(row == 0, g[k, 4] * lift[0], 0.0)
-        new += jnp.where(row == 11, g[k, 5] * lift[1], 0.0)
-        new += jnp.where(lane < 12, g[k, 2] * lift[2], 0.0)
-        new += jnp.where((lane >= 132) & (lane < 144), g[k, 3] * lift[3], 0.0)
+    answer = answer_in[...]
+    upper = iota((1, 128), 1) >= 64
+    for k in range(CAP_NEW):
+        lift = [table[info[OTHER + 4 * k + f], pl.ds(LIFT_ROW, 1), :] for f in range(4)]
+        lift = [wide(jnp.where(upper, line, pltpu.roll(line, 64, 1))) for line in lift]
+        new = u_in[k] + surface_lift(g.at[k], lift)
         u[k] = new
         pack_faces(COARSE, new, faces, k, 0)
     row, lane = iota((16, 128), 0), iota((16, 128), 1)
@@ -504,13 +548,18 @@
     send_faces(info, faces, x_out, y_out)
 
 
-def last_kernel(info, u_in, g, start, faces_in, x_in, y_in, out, table):
+def last_kernel(info, part, g, faces_in, x_in, y_in, out, table, u, block, sems):
     fill_table(info, table, x_in, faces_in, y_in)
-    for k in range(CAP_NEW):
-        field = u_in[k]
-        ghosts = ghosts_of(FINE, info, table, k, 0)
-        new = KEEP * field + (start[k] + neighbour_sum(FINE, field, g.at[k], ghosts))
-        out[k] = jnp.where(k < info[HELD], new[:, 0:576], 0.0)
+    copies = [
+        pltpu.make_async_copy(block.at[k], out.at[k], sems.at[k]) for k in range(CAP_NEW)
+    ]
+    for k in range(CAP_NEW):
+        u[...] = part[k]
+        add_ghosts(FINE, u, g.at[k], ghosts_of(FINE, info, table, k, 0))
+        block[k] = jnp.where(k < info[HELD], u[:, 0:576], 0.0)
+        copies[k].start()
+    for copy in copies:
+        copy.wait()
 
 
 def sds(*shape):
@@ -594,48 +643,43 @@
         (info, source, coef, faces, coarse_own, x_in, y_in),
     )
     x_in, y_in = exchange(x_out, y_out)
-    coarse_g, coarse_w, coarse_d, g_faces, row = call(
+    coarse_g, coarse_w, coarse_d, alpha, g_faces, row = call(
         coarse_conduct_kernel, "coarse_conduct",
-        [sds(CAP_NEW, 6, 16, 256), coarse, coarse, sds(CAP_NEW, 32, 128), sds(1, 128)],
+        [sds(CAP_NEW, 6, 16, 256), coarse, coarse, coarse, sds(CAP_NEW, 32, 128), sds(1, 128)],
         [(ABSENT + 1, BOTH_ROWS, 128)],
         (info, level, faces, x_in, y_in),
     )
+
+    def inner(u, name):
+        return call(inner_kernel, name, [fine], [], (u, fine_g, fine_s), [VMEM] * 3)
+
+    part = inner(u, "pre_inner")
     u0, faces, x_out, y_out = call(
-        lambda *refs: sweep_kernel(FINE, *refs), "pre", [fine, *fine_faces],
-        [(ABSENT + 1, BOTH_ROWS, 128)],
-        (info, u, fine_g, fine_s, faces, x_in, y_in),
-    )
-
-    def sweep(lev, u, g, start, faces, x_out, y_out, name):
-        x_in, y_in = exchange(x_out, y_out)
-        return call(
-            lambda *refs: sweep_kernel(lev, *refs), name,
-            [fine, *fine_faces] if lev is FINE else [coarse, *coarse_faces],
-            fine_table if lev is FINE else coarse_table,
-            (info, u, g, start, faces, x_in, y_in),
-        )
-
+        finish_kernel, "pre", [fine, *fine_faces], [(ABSENT + 1, BOTH_ROWS, 128)],
+        (info, part, fine_g, faces, x_in, y_in),
+    )
     x_in, y_in = exchange(x_out, y_out)
+    part = inner(u0, "residual_inner")
     coarse_s, faces, x_out, y_out = call(
         residual_kernel, "residual",
         [coarse, coarse_faces[0], sds(REACH, 48, 128), coarse_faces[2]],
         fine_table + [(CAP_NEW, 24, FINE.width), sums],
-        (info, u0, fine_g, fine_s, fine_d, coarse_w, spread, g_faces, faces, x_in, y_in),
+        (info, u0, part, fine_g, fine_d, coarse_w, spread, g_faces, faces, x_in, y_in),
     )
     g_in, y_in = exchange(x_out, y_out)
     e, faces, x_out, y_out = call(
-        lambda *refs: sweep_kernel(COARSE, *refs), "coarse_pre", [coarse, *coarse_faces],
+        sweep_kernel, "coarse_pre", [coarse, *coarse_faces],
         coarse_table, (info, coarse_s, coarse_g, coarse_s, faces, g_in, y_in),
     )
     x_in, y_in = exchange(x_out, y_out)
-    rows = call(
-        total_kernel, "totals", [sds(NCOARSE, 128)], coarse_table,
+    rows, swept = call(
+        total_kernel, "totals", [sds(NCOARSE, 128), coarse], coarse_table,
         (info, e, coarse_g, coarse_s, coarse_d, row, faces, x_in, y_in),
     )
     rows = lax.all_to_all(rows, "curve", 0, 0, tiled=True)
     e, answer, faces, x_out = call(
-        solve_kernel, "solve", [coarse, sds(NCOARSE, 128), *coarse_faces[:2]], coarse_table,
-        (info, rows, e, coarse_g, coarse_s, faces, x_in, y_in),
+        solve_kernel, "solve", [coarse, sds(NCOARSE, 128), *coarse_faces[:2]], [],
+        (info, rows, swept, coarse_g, alpha),
     )
     x_in = swap(x_out, AXES, 1)
     e, faces, x_in, y_out = call(
@@ -648,11 +692,19 @@
         coarse_table + [(CAP_NEW, 16, 256), (FINE.tiles, 24, 128)],
         (info, e, coarse_g, coarse_s, faces, x_in, y_in, u0, spread),
     )
-    u, faces, x_out, y_out = sweep(FINE, u, fine_g, fine_s, faces, x_out, y_out, "post")
     x_in, y_in = exchange(x_out, y_out)
+    part = inner(u, "post_inner")
+    u, faces, x_out, y_out = call(
+        finish_kernel, "post", [fine, *fine_faces], fine_table,
+        (info, part, fine_g, faces, x_in, y_in),
+    )
+    x_in, y_in = exchange(x_out, y_out)
+    part = inner(u, "last_inner")
     return call(
-        last_kernel, "last", [sds(CAP_NEW, 24, 576)], fine_table,
-        (info, u, fine_g, fine_s, faces, x_in, y_in),
+        last_kernel, "last", [sds(CAP_NEW, 24, 576)],
+        fine_table
+        + [(24, FINE.width), (CAP_NEW, 24, 576), pltpu.SemaphoreType.DMA((CAP_NEW,))],
+        (info, part, fine_g, faces, x_in, y_in), None, pl.BlockSpec(memory_space=pl.ANY),
     )
 
 

time: 125 us -> 123 us (0.984)
    pallas_call x15 -> x19, Pallas kernels: 18.7 us -> 18.5 us  [call(): pl.pallas_call(kernel, out_shape=outs if many else outs[0], in_specs=in_s...]
  transfers between devices with their start and end apart: 18 -> 18, of which waited for: 12 -> 9; matrix products, arithmetic and copies ran while one was open for 0% -> 0% of each run, Pallas kernels for 2% -> 4%
where the time goes in v5:
time: 123 us; the launch traced here: 122 us
  starting transfers between devices  73 us (59%)
  Pallas kernels  18.5 us (15%)
  blocking collectives  15.4 us (13%)
  waiting for transfers between devices  15.1 us (12%)
    ppermute x18, starting transfers between devices, swap(): lax.ppermute(block, axis, [(i, i + 1) for i in starts] + [(i + 1, i) for...  73 us
    pallas_call x19, Pallas kernels, call(): pl.pallas_call(kernel, out_shape=outs if many else outs[0], in_specs=in_s...  18.5 us
    all_to_all x1, blocking collectives, body(): rows = lax.all_to_all(rows, 'curve', 0, 0, tiled=True)  15.4 us
    ppermute x18, waiting for transfers between devices, swap(): lax.ppermute(block, axis, [(i, i + 1) for i in starts] + [(i + 1, i) for...  15.1 us
  transfers between devices with their start and end apart: 18, of which 9 were waited for; matrix products, arithmetic and copies ran while one was open for 0% of the time, Pallas kernels for 4%

profile of v5, /device:TPU:24, one launch (start us, length us, event | category | flops | bytes accessed | tf_op | source)
XLA Modules:
  0.0 122.3 jit_solution(16234687450408108253)
XLA Ops:
  0.0 2.1 %owners.1 = (f32[2,24,576]{2,1,0:T(8,128)S(1)}, f32[2,24,576]{2,1,0:T(8,128)S(1)}, s32[128]{0:T(128)S(1)}, f32[7,24,576]{2,1,0:T(8,128)S(1)}, f32[7,24,576]{2,1,0:T(8,128)S(1)}) custom-call(s32[1,128]{1,0:T(1,128)} %new_in.1, s32[1,128]{1,0:T(1,128)} %old_in.1, s32[4,128]{1,0:T(4,128)} %bitcast.9, s32[1,128]{1,0:T(1,128)} %map_in.1, f32[7,24,576]{2,1,0:T(8,128)} %rhs_in.1, ...), custom_call_target="tpu_custom_call" | custom-call | flops 10000000 | bytes 4000000 | tf_op jit(solution)/shard_map/owners/pallas_call | solution.py:576
  2.1 1.9 %collective-permute-start = (f32[2,24,576]{2,1,0:T(8,128)S(1)}, f32[2,24,576]{2,1,0:T(8,128)S(1)}, u32[]{:S(2)}, u32[]{:S(2)}) collective-permute-start(f32[2,24,576]{2,1,0:T(8,128)S(1)} %get-tuple-element.66), channel_id=1, source_target_pairs={{0,1},{2,3},{4,5},{6,7},{8,9},{10,11},{12,13},{14,15},{16,17},{18,... | collective-permute-start | bytes 331784 | tf_op jit(solution)/shard_map/ppermute | solution.py:590
  4.0 0.7 collective-permute-start.1
  4.7 0.6 place.1
  5.3 0.6 collect.1
  6.0 13.9 %collective-permute-start.2 = (f32[3,40,128]{2,1,0:T(8,128)S(1)}, f32[3,40,128]{2,1,0:T(8,128)S(1)}, u32[]{:S(2)}, u32[]{:S(2)}) collective-permute-start(f32[3,40,128]{2,1,0:T(8,128)S(1)} %get-tuple-element.73), channel_id=1, source_target_pairs={{1,2},{3,4},{5,6},{7,8},{9,10},{11,12},{13,14},{15,16},{17,18},{19... | collective-permute-start | bytes 184328 | tf_op jit(solution)/shard_map/ppermute | solution.py:590
  19.9 1.9 %collective-permute-start.3 = (f32[3,40,128]{2,1,0:T(8,128)S(1)}, f32[3,40,128]{2,1,0:T(8,128)S(1)}, u32[]{:S(2)}, u32[]{:S(2)}) collective-permute-start(f32[3,40,128]{2,1,0:T(8,128)S(1)} %get-tuple-element.74), channel_id=1, source_target_pairs={{0,1},{2,3},{4,5},{6,7},{8,9},{10,11},{12,13},{14,15},{16,17},{18,... | collective-permute-start | bytes 184328 | tf_op jit(solution)/shard_map/ppermute | solution.py:590
  21.8 1.0 level.1
  22.8 0.2 collective-permute-done.3.y_in
  23.0 1.3 %conduct.1 = (f32[5,6,24,640]{3,2,1,0:T(8,128)S(1)}, f32[5,24,640]{2,1,0:T(8,128)S(1)}, f32[5,24,640]{2,1,0:T(8,128)S(1)}, f32[5,24,640]{2,1,0:T(8,128)S(1)}, f3...) custom-call(s32[128]{0:T(128)S(1)} %get-tuple-element.62.info, ...), custom_call_target="tpu_custom_call" | custom-call | flops 10000000 | bytes 4000000 | tf_op jit(solution)/shard_map/conduct/pallas_call | solution.py:576
  24.3 7.8 %collective-permute-start.4 = (f32[3,56,128]{2,1,0:T(8,128)S(1)}, f32[3,56,128]{2,1,0:T(8,128)S(1)}, u32[]{:S(2)}, u32[]{:S(2)}) collective-permute-start(f32[3,56,128]{2,1,0:T(8,128)S(1)} %get-tuple-element.79), channel_id=1, source_target_pairs={{1,2},{3,4},{5,6},{7,8},{9,10},{11,12},{13,14},{15,16},{17,18},{19... | collective-permute-start | bytes 258056 | tf_op jit(solution)/shard_map/ppermute | solution.py:590
  32.1 1.9 %collective-permute-start.5 = (f32[3,56,128]{2,1,0:T(8,128)S(1)}, f32[3,56,128]{2,1,0:T(8,128)S(1)}, u32[]{:S(2)}, u32[]{:S(2)}) collective-permute-start(f32[3,56,128]{2,1,0:T(8,128)S(1)} %get-tuple-element.80), channel_id=1, source_target_pairs={{0,1},{2,3},{4,5},{6,7},{8,9},{10,11},{12,13},{14,15},{16,17},{18,... | collective-permute-start | bytes 258056 | tf_op jit(solution)/shard_map/ppermute | solution.py:590
  34.0 0.4 pre_inner.1.part
  34.5 0.8 collective-permute-done.5.y_in
  35.3 0.7 pre.1
  36.0 6.8 %collective-permute-start.6 = (f32[3,40,128]{2,1,0:T(8,128)S(1)}, f32[3,40,128]{2,1,0:T(8,128)S(1)}, u32[]{:S(2)}, u32[]{:S(2)}) collective-permute-start(f32[3,40,128]{2,1,0:T(8,128)S(1)} %get-tuple-element.88), channel_id=1, source_target_pairs={{1,2},{3,4},{5,6},{7,8},{9,10},{11,12},{13,14},{15,16},{17,18},{19... | collective-permute-start | bytes 184328 | tf_op jit(solution)/shard_map/ppermute | solution.py:590
  42.8 1.9 %collective-permute-start.7 = (f32[3,40,128]{2,1,0:T(8,128)S(1)}, f32[3,40,128]{2,1,0:T(8,128)S(1)}, u32[]{:S(2)}, u32[]{:S(2)}) collective-permute-start(f32[3,40,128]{2,1,0:T(8,128)S(1)} %get-tuple-element.89), channel_id=1, source_target_pairs={{0,1},{2,3},{4,5},{6,7},{8,9},{10,11},{12,13},{14,15},{16,17},{18,... | collective-permute-start | bytes 184328 | tf_op jit(solution)/shard_map/ppermute | solution.py:590
  44.8 0.4 residual_inner.1.part
  45.2 1.0 coarse_conduct.1
  46.3 1.1 residual.1
  47.3 6.3 %collective-permute-start.8 = (f32[3,48,128]{2,1,0:T(8,128)S(1)}, f32[3,48,128]{2,1,0:T(8,128)S(1)}, u32[]{:S(2)}, u32[]{:S(2)}) collective-permute-start(f32[3,48,128]{2,1,0:T(8,128)S(1)} %get-tuple-element.93), channel_id=1, source_target_pairs={{1,2},{3,4},{5,6},{7,8},{9,10},{11,12},{13,14},{15,16},{17,18},{19... | collective-permute-start | bytes 221192 | tf_op jit(solution)/shard_map/ppermute | solution.py:590
  53.7 1.9 %collective-permute-start.9 = (f32[3,16,128]{2,1,0:T(8,128)S(1)}, f32[3,16,128]{2,1,0:T(8,128)S(1)}, u32[]{:S(2)}, u32[]{:S(2)}) collective-permute-start(f32[3,16,128]{2,1,0:T(8,128)S(1)} %get-tuple-element.94), channel_id=1, source_target_pairs={{0,1},{2,3},{4,5},{6,7},{8,9},{10,11},{12,13},{14,15},{16,17},{18,... | collective-permute-start | bytes 73736 | tf_op jit(solution)/shard_map/ppermute | solution.py:590
  55.6 1.2 collective-permute-done.9.y_in
  56.7 0.5 collective-permute-done.8.x_in.g_in
  57.2 0.8 coarse_pre.1
  58.0 6.3 %collective-permute-start.10 = (f32[3,16,128]{2,1,0:T(8,128)S(1)}, f32[3,16,128]{2,1,0:T(8,128)S(1)}, u32[]{:S(2)}, u32[]{:S(2)}) collective-permute-start(f32[3,16,128]{2,1,0:T(8,128)S(1)} %get-tuple-element.99), channel_id=1, source_target_pairs={{1,2},{3,4},{5,6},{7,8},{9,10},{11,12},{13,14},{15,16},{17,18},{19... | collective-permute-start | bytes 73736 | tf_op jit(solution)/shard_map/ppermute | solution.py:590
  64.4 1.9 %collective-permute-start.11 = (f32[3,16,128]{2,1,0:T(8,128)S(1)}, f32[3,16,128]{2,1,0:T(8,128)S(1)}, u32[]{:S(2)}, u32[]{:S(2)}) collective-permute-start(f32[3,16,128]{2,1,0:T(8,128)S(1)} %get-tuple-element.100), channel_id=1, source_target_pairs={{0,1},{2,3},{4,5},{6,7},{8,9},{10,11},{12,13},{14,15},{16,17},{18,... | collective-permute-start | bytes 73736 | tf_op jit(solution)/shard_map/ppermute | solution.py:590
  66.3 1.1 collective-permute-done.10.x_in
  67.4 0.0 collective-permute-done.11.y_in
  67.4 0.9 totals.1
  68.3 15.4 %all_to_all.11 = f32[32,1,128]{2,1,0:T(1,128)S(1)} all-to-all(f32[32,1,128]{2,1,0:T(1,128)S(1)} %bitcast.8), channel_id=1, replica_groups=mesh['group'=16,'curve'=32] {'curve'}, dimensions={0} | all-to-all | bytes 32768 | tf_op jit(solution)/shard_map/all_to_all | solution.py:679
  83.7 2.8 %solve.1 = (f32[5,16,256]{2,1,0:T(8,128)S(1)}, f32[32,128]{1,0:T(8,128)S(1)}, f32[5,16,128]{2,1,0:T(8,128)}, f32[3,16,128]{2,1,0:T(8,128)S(1)}) custom-call(s32[128]{0:T(128)S(1)} %get-tuple-element.62.info, f32[32,128]{1,0:T(8,128)S(1)} %bitcast.7, f32[5,16,256]{2,1,0:T(8,128)S(1)} %get-tuple-element.102.swept, f32[5,6,16,256]{3,2,1,0:T(8,128)S(1)} %get-tuple-element.91.g, ...), custom_call_target="tpu_custom_call" | custom-call | flops 10000000 | bytes 4000000 | tf_op jit(solution)/shard_map/solve/pallas_call | solution.py:576
  86.5 4.6 %collective-permute-start.12 = (f32[3,16,128]{2,1,0:T(8,128)S(1)}, f32[3,16,128]{2,1,0:T(8,128)S(1)}, u32[]{:S(2)}, u32[]{:S(2)}) collective-permute-start(f32[3,16,128]{2,1,0:T(8,128)S(1)} %get-tuple-element.106), channel_id=1, source_target_pairs={{1,2},{3,4},{5,6},{7,8},{9,10},{11,12},{13,14},{15,16},{17,18},{19... | collective-permute-start | bytes 73736 | tf_op jit(solution)/shard_map/ppermute | solution.py:590
  91.2 4.7 %collective-permute-done.12.x_in = f32[3,16,128]{2,1,0:T(8,128)S(1)} collective-permute-done((f32[3,16,128]{2,1,0:T(8,128)S(1)}, f32[3,16,128]{2,1,0:T(8,128)S(1)}, u32[]{:S(2)}, u32[]{:S(2)}) %collective-permute-start.12) | collective-permute-done | bytes 24608 | tf_op jit(solution)/shard_map/ppermute | solution.py:590
  95.9 0.7 across.1
  96.6 1.9 %collective-permute-start.13 = (f32[3,16,128]{2,1,0:T(8,128)S(1)}, f32[3,16,128]{2,1,0:T(8,128)S(1)}, u32[]{:S(2)}, u32[]{:S(2)}) collective-permute-start(f32[3,16,128]{2,1,0:T(8,128)S(1)} %get-tuple-element.110), channel_id=1, source_target_pairs={{0,1},{2,3},{4,5},{6,7},{8,9},{10,11},{12,13},{14,15},{16,17},{18,... | collective-permute-start | bytes 73736 | tf_op jit(solution)/shard_map/ppermute | solution.py:590
  98.5 1.2 collective-permute-done.13.y_in
  99.7 1.0 refine.1
  100.6 4.7 %collective-permute-start.14 = (f32[3,40,128]{2,1,0:T(8,128)S(1)}, f32[3,40,128]{2,1,0:T(8,128)S(1)}, u32[]{:S(2)}, u32[]{:S(2)}) collective-permute-start(f32[3,40,128]{2,1,0:T(8,128)S(1)} %get-tuple-element.113), channel_id=1, source_target_pairs={{1,2},{3,4},{5,6},{7,8},{9,10},{11,12},{13,14},{15,16},{17,18},{19... | collective-permute-start | bytes 184328 | tf_op jit(solution)/shard_map/ppermute | solution.py:590
  105.3 1.9 %collective-permute-start.15 = (f32[3,40,128]{2,1,0:T(8,128)S(1)}, f32[3,40,128]{2,1,0:T(8,128)S(1)}, u32[]{:S(2)}, u32[]{:S(2)}) collective-permute-start(f32[3,40,128]{2,1,0:T(8,128)S(1)} %get-tuple-element.114), channel_id=1, source_target_pairs={{0,1},{2,3},{4,5},{6,7},{8,9},{10,11},{12,13},{14,15},{16,17},{18,... | collective-permute-start | bytes 184328 | tf_op jit(solution)/shard_map/ppermute | solution.py:590
  107.2 0.4 post_inner.1.part
  107.7 2.7 %collective-permute-done.14.x_in = f32[3,40,128]{2,1,0:T(8,128)S(1)} collective-permute-done((f32[3,40,128]{2,1,0:T(8,128)S(1)}, f32[3,40,128]{2,1,0:T(8,128)S(1)}, u32[]{:S(2)}, u32[]{:S(2)}) %collective-permute-start.14) | collective-permute-done | bytes 61472 | tf_op jit(solution)/shard_map/ppermute | solution.py:590
  110.4 0.7 post.1
  111.1 4.7 %collective-permute-start.16 = (f32[3,40,128]{2,1,0:T(8,128)S(1)}, f32[3,40,128]{2,1,0:T(8,128)S(1)}, u32[]{:S(2)}, u32[]{:S(2)}) collective-permute-start(f32[3,40,128]{2,1,0:T(8,128)S(1)} %get-tuple-element.117), channel_id=1, source_target_pairs={{1,2},{3,4},{5,6},{7,8},{9,10},{11,12},{13,14},{15,16},{17,18},{19... | collective-permute-start | bytes 184328 | tf_op jit(solution)/shard_map/ppermute | solution.py:590
  115.8 1.9 %collective-permute-start.17 = (f32[3,40,128]{2,1,0:T(8,128)S(1)}, f32[3,40,128]{2,1,0:T(8,128)S(1)}, u32[]{:S(2)}, u32[]{:S(2)}) collective-permute-start(f32[3,40,128]{2,1,0:T(8,128)S(1)} %get-tuple-element.118), channel_id=1, source_target_pairs={{0,1},{2,3},{4,5},{6,7},{8,9},{10,11},{12,13},{14,15},{16,17},{18,... | collective-permute-start | bytes 184328 | tf_op jit(solution)/shard_map/ppermute | solution.py:590
  117.7 0.4 last_inner.1.part
  118.1 2.7 %collective-permute-done.16.x_in = f32[3,40,128]{2,1,0:T(8,128)S(1)} collective-permute-done((f32[3,40,128]{2,1,0:T(8,128)S(1)}, f32[3,40,128]{2,1,0:T(8,128)S(1)}, u32[]{:S(2)}, u32[]{:S(2)}) %collective-permute-start.16) | collective-permute-done | bytes 61472 | tf_op jit(solution)/shard_map/ppermute | solution.py:590
  120.9 1.4 %last.1 = f32[5,24,576]{2,1,0:T(8,128)} custom-call(s32[128]{0:T(128)S(1)} %get-tuple-element.62.info, f32[5,24,640]{2,1,0:T(8,128)S(1)} %last_inner.1.part, f32[5,6,24,640]{3,2,1,0:T(8,128)S(1)} %get-tuple-element.76.g, f32[5,40,128]{2,1,0:T(8,128)S(1)} %get-tuple-element.116.faces_in, f32[3,40,128]{2,1,0:T(8,128)S(1)} %collective-permute-done.16.x_in, ...), custom_call_target="tpu_custom_call" | custom-call | flops 10000000 | bytes 4000000 | tf_op jit(solution)/shard_map/last/pallas_call | solution.py:576
  (8 shorter events, 0.0 us)
Async XLA Ops:
  2.1 3.2 %collective-permute-start = (f32[2,24,576]{2,1,0:T(8,128)S(1)}, f32[2,24,576]{2,1,0:T(8,128)S(1)}, u32[]{:S(2)}, u32[]{:S(2)}) collective-permute-start(f32[2,24,576]{2,1,0:T(8,128)S(1)} %get-tuple-element.66), channel_id=1, source_target_pairs={{0,1},{2,3},{4,5},{6,7},{8,9},{10,11},{12,13},{14,15},{16,17},{18,... | collective-permute-start | bytes 331784 | tf_op jit(solution)/shard_map/ppermute | solution.py:590
  4.0 1.3 %collective-permute-start.1 = (f32[2,24,576]{2,1,0:T(8,128)S(1)}, f32[2,24,576]{2,1,0:T(8,128)S(1)}, u32[]{:S(2)}, u32[]{:S(2)}) collective-permute-start(f32[2,24,576]{2,1,0:T(8,128)S(1)} %get-tuple-element.67), channel_id=1, source_target_pairs={{1,2},{3,4},{5,6},{7,8},{9,10},{11,12},{13,14},{15,16},{17,18},{19... | collective-permute-start | bytes 331784 | tf_op jit(solution)/shard_map/ppermute | solution.py:590
  6.0 16.9 %collective-permute-start.2 = (f32[3,40,128]{2,1,0:T(8,128)S(1)}, f32[3,40,128]{2,1,0:T(8,128)S(1)}, u32[]{:S(2)}, u32[]{:S(2)}) collective-permute-start(f32[3,40,128]{2,1,0:T(8,128)S(1)} %get-tuple-element.73), channel_id=1, source_target_pairs={{1,2},{3,4},{5,6},{7,8},{9,10},{11,12},{13,14},{15,16},{17,18},{19... | collective-permute-start | bytes 184328 | tf_op jit(solution)/shard_map/ppermute | solution.py:590
  19.9 3.1 %collective-permute-start.3 = (f32[3,40,128]{2,1,0:T(8,128)S(1)}, f32[3,40,128]{2,1,0:T(8,128)S(1)}, u32[]{:S(2)}, u32[]{:S(2)}) collective-permute-start(f32[3,40,128]{2,1,0:T(8,128)S(1)} %get-tuple-element.74), channel_id=1, source_target_pairs={{0,1},{2,3},{4,5},{6,7},{8,9},{10,11},{12,13},{14,15},{16,17},{18,... | collective-permute-start | bytes 184328 | tf_op jit(solution)/shard_map/ppermute | solution.py:590
  24.3 10.1 %collective-permute-start.4 = (f32[3,56,128]{2,1,0:T(8,128)S(1)}, f32[3,56,128]{2,1,0:T(8,128)S(1)}, u32[]{:S(2)}, u32[]{:S(2)}) collective-permute-start(f32[3,56,128]{2,1,0:T(8,128)S(1)} %get-tuple-element.79), channel_id=1, source_target_pairs={{1,2},{3,4},{5,6},{7,8},{9,10},{11,12},{13,14},{15,16},{17,18},{19... | collective-permute-start | bytes 258056 | tf_op jit(solution)/shard_map/ppermute | solution.py:590
  32.1 3.2 %collective-permute-start.5 = (f32[3,56,128]{2,1,0:T(8,128)S(1)}, f32[3,56,128]{2,1,0:T(8,128)S(1)}, u32[]{:S(2)}, u32[]{:S(2)}) collective-permute-start(f32[3,56,128]{2,1,0:T(8,128)S(1)} %get-tuple-element.80), channel_id=1, source_target_pairs={{0,1},{2,3},{4,5},{6,7},{8,9},{10,11},{12,13},{14,15},{16,17},{18,... | collective-permute-start | bytes 258056 | tf_op jit(solution)/shard_map/ppermute | solution.py:590
  36.0 10.3 %collective-permute-start.6 = (f32[3,40,128]{2,1,0:T(8,128)S(1)}, f32[3,40,128]{2,1,0:T(8,128)S(1)}, u32[]{:S(2)}, u32[]{:S(2)}) collective-permute-start(f32[3,40,128]{2,1,0:T(8,128)S(1)} %get-tuple-element.88), channel_id=1, source_target_pairs={{1,2},{3,4},{5,6},{7,8},{9,10},{11,12},{13,14},{15,16},{17,18},{19... | collective-permute-start | bytes 184328 | tf_op jit(solution)/shard_map/ppermute | solution.py:590
  42.8 3.4 %collective-permute-start.7 = (f32[3,40,128]{2,1,0:T(8,128)S(1)}, f32[3,40,128]{2,1,0:T(8,128)S(1)}, u32[]{:S(2)}, u32[]{:S(2)}) collective-permute-start(f32[3,40,128]{2,1,0:T(8,128)S(1)} %get-tuple-element.89), channel_id=1, source_target_pairs={{0,1},{2,3},{4,5},{6,7},{8,9},{10,11},{12,13},{14,15},{16,17},{18,... | collective-permute-start | bytes 184328 | tf_op jit(solution)/shard_map/ppermute | solution.py:590
  47.3 9.9 %collective-permute-start.8 = (f32[3,48,128]{2,1,0:T(8,128)S(1)}, f32[3,48,128]{2,1,0:T(8,128)S(1)}, u32[]{:S(2)}, u32[]{:S(2)}) collective-permute-start(f32[3,48,128]{2,1,0:T(8,128)S(1)} %get-tuple-element.93), channel_id=1, source_target_pairs={{1,2},{3,4},{5,6},{7,8},{9,10},{11,12},{13,14},{15,16},{17,18},{19... | collective-permute-start | bytes 221192 | tf_op jit(solution)/shard_map/ppermute | solution.py:590
  53.7 3.1 %collective-permute-start.9 = (f32[3,16,128]{2,1,0:T(8,128)S(1)}, f32[3,16,128]{2,1,0:T(8,128)S(1)}, u32[]{:S(2)}, u32[]{:S(2)}) collective-permute-start(f32[3,16,128]{2,1,0:T(8,128)S(1)} %get-tuple-element.94), channel_id=1, source_target_pairs={{0,1},{2,3},{4,5},{6,7},{8,9},{10,11},{12,13},{14,15},{16,17},{18,... | collective-permute-start | bytes 73736 | tf_op jit(solution)/shard_map/ppermute | solution.py:590
  58.0 9.4 %collective-permute-start.10 = (f32[3,16,128]{2,1,0:T(8,128)S(1)}, f32[3,16,128]{2,1,0:T(8,128)S(1)}, u32[]{:S(2)}, u32[]{:S(2)}) collective-permute-start(f32[3,16,128]{2,1,0:T(8,128)S(1)} %get-tuple-element.99), channel_id=1, source_target_pairs={{1,2},{3,4},{5,6},{7,8},{9,10},{11,12},{13,14},{15,16},{17,18},{19... | collective-permute-start | bytes 73736 | tf_op jit(solution)/shard_map/ppermute | solution.py:590
  64.4 3.1 %collective-permute-start.11 = (f32[3,16,128]{2,1,0:T(8,128)S(1)}, f32[3,16,128]{2,1,0:T(8,128)S(1)}, u32[]{:S(2)}, u32[]{:S(2)}) collective-permute-start(f32[3,16,128]{2,1,0:T(8,128)S(1)} %get-tuple-element.100), channel_id=1, source_target_pairs={{0,1},{2,3},{4,5},{6,7},{8,9},{10,11},{12,13},{14,15},{16,17},{18,... | collective-permute-start | bytes 73736 | tf_op jit(solution)/shard_map/ppermute | solution.py:590
  86.5 9.4 %collective-permute-start.12 = (f32[3,16,128]{2,1,0:T(8,128)S(1)}, f32[3,16,128]{2,1,0:T(8,128)S(1)}, u32[]{:S(2)}, u32[]{:S(2)}) collective-permute-start(f32[3,16,128]{2,1,0:T(8,128)S(1)} %get-tuple-element.106), channel_id=1, source_target_pairs={{1,2},{3,4},{5,6},{7,8},{9,10},{11,12},{13,14},{15,16},{17,18},{19... | collective-permute-start | bytes 73736 | tf_op jit(solution)/shard_map/ppermute | solution.py:590
  96.6 3.1 %collective-permute-start.13 = (f32[3,16,128]{2,1,0:T(8,128)S(1)}, f32[3,16,128]{2,1,0:T(8,128)S(1)}, u32[]{:S(2)}, u32[]{:S(2)}) collective-permute-start(f32[3,16,128]{2,1,0:T(8,128)S(1)} %get-tuple-element.110), channel_id=1, source_target_pairs={{0,1},{2,3},{4,5},{6,7},{8,9},{10,11},{12,13},{14,15},{16,17},{18,... | collective-permute-start | bytes 73736 | tf_op jit(solution)/shard_map/ppermute | solution.py:590
  100.6 9.8 %collective-permute-start.14 = (f32[3,40,128]{2,1,0:T(8,128)S(1)}, f32[3,40,128]{2,1,0:T(8,128)S(1)}, u32[]{:S(2)}, u32[]{:S(2)}) collective-permute-start(f32[3,40,128]{2,1,0:T(8,128)S(1)} %get-tuple-element.113), channel_id=1, source_target_pairs={{1,2},{3,4},{5,6},{7,8},{9,10},{11,12},{13,14},{15,16},{17,18},{19... | collective-permute-start | bytes 184328 | tf_op jit(solution)/shard_map/ppermute | solution.py:590
  105.3 5.1 %collective-permute-start.15 = (f32[3,40,128]{2,1,0:T(8,128)S(1)}, f32[3,40,128]{2,1,0:T(8,128)S(1)}, u32[]{:S(2)}, u32[]{:S(2)}) collective-permute-start(f32[3,40,128]{2,1,0:T(8,128)S(1)} %get-tuple-element.114), channel_id=1, source_target_pairs={{0,1},{2,3},{4,5},{6,7},{8,9},{10,11},{12,13},{14,15},{16,17},{18,... | collective-permute-start | bytes 184328 | tf_op jit(solution)/shard_map/ppermute | solution.py:590
  111.1 9.8 %collective-permute-start.16 = (f32[3,40,128]{2,1,0:T(8,128)S(1)}, f32[3,40,128]{2,1,0:T(8,128)S(1)}, u32[]{:S(2)}, u32[]{:S(2)}) collective-permute-start(f32[3,40,128]{2,1,0:T(8,128)S(1)} %get-tuple-element.117), channel_id=1, source_target_pairs={{1,2},{3,4},{5,6},{7,8},{9,10},{11,12},{13,14},{15,16},{17,18},{19... | collective-permute-start | bytes 184328 | tf_op jit(solution)/shard_map/ppermute | solution.py:590
  115.8 5.1 %collective-permute-start.17 = (f32[3,40,128]{2,1,0:T(8,128)S(1)}, f32[3,40,128]{2,1,0:T(8,128)S(1)}, u32[]{:S(2)}, u32[]{:S(2)}) collective-permute-start(f32[3,40,128]{2,1,0:T(8,128)S(1)} %get-tuple-element.118), channel_id=1, source_target_pairs={{0,1},{2,3},{4,5},{6,7},{8,9},{10,11},{12,13},{14,15},{16,17},{18,... | collective-permute-start | bytes 184328 | tf_op jit(solution)/shard_map/ppermute | solution.py:590

commit v6 on v5

--- a/solution.py
+++ b/solution.py
@@ -320,23 +320,28 @@
         pack_faces(COARSE, level[k], faces, k, 0)
 
 
-def conduct_kernel(
-    info, source, coef, faces_in, coarse_faces, x_in, y_in,
-    fine_g, fine_s, fine_d, u, faces, x_out, y_out, table,
+def start_kernel(
+    info, source, coef, faces_in, coarse_faces, x_in, y_in, u, faces, x_out, y_out, table
 ):
     fill_table(info, table, x_in, faces_in, y_in)
     for k in range(CAP_NEW):
         ghosts = ghosts_of(FINE, info, table, k, 0)
-        _, g, weight, diagonal, _ = conductances(FINE, coef[k], ghosts)
-        for i in range(6):
-            fine_g[k, i] = g[i]
-        fine_d[k] = (1.0 / OMEGA) * diagonal
+        _, _, weight, _, _ = conductances(FINE, coef[k], ghosts)
         start = weight * source[k]
-        fine_s[k] = start
         u[k] = start
         pack_faces(FINE, start, faces, k, 0)
     faces[:, FINE.face_rows : BOTH_ROWS, :] = coarse_faces[...]
     send_faces(info, faces, x_out, y_out)
+
+
+def conduct_kernel(info, coef, faces_in, x_in, y_in, fine_g, fine_d, table):
+    fill_table(info, table, x_in, faces_in, y_in)
+    for k in range(CAP_NEW):
+        ghosts = ghosts_of(FINE, info, table, k, 0)
+        _, g, _, diagonal, _ = conductances(FINE, coef[k], ghosts)
+        for i in range(6):
+            fine_g[k, i] = g[i]
+        fine_d[k] = (1.0 / OMEGA) * diagonal
 
 
 def coarse_conduct_kernel(
@@ -637,11 +642,16 @@
         (info, source, y_in, x_in, coef),
     )
     x_in, y_in = exchange(x_out, y_out)
-    fine_g, fine_s, fine_d, u, faces, x_out, y_out = call(
-        conduct_kernel, "conduct",
-        [sds(CAP_NEW, 6, 24, FINE.width), fine, fine, fine] + face_outs(BOTH_ROWS), fine_table,
+    u, new_faces, x_out, y_out = call(
+        start_kernel, "start", [fine] + face_outs(BOTH_ROWS), fine_table,
         (info, source, coef, faces, coarse_own, x_in, y_in),
     )
+    fine_s = u
+    fine_g, fine_d = call(
+        conduct_kernel, "conduct", [sds(CAP_NEW, 6, 24, FINE.width), fine], fine_table,
+        (info, coef, faces, x_in, y_in),
+    )
+    faces = new_faces
     x_in, y_in = exchange(x_out, y_out)
     coarse_g, coarse_w, coarse_d, alpha, g_faces, row = call(
         coarse_conduct_kernel, "coarse_conduct",

time: 123 us -> 123 us (level)
    pallas_call x19 -> x20, Pallas kernels: 18.5 us -> 19.7 us  [call(): pl.pallas_call(kernel, out_shape=outs if many else outs[0], in_specs=in_s...]
  transfers between devices with their start and end apart: 18 -> 18, of which waited for: 9 -> 8; matrix products, arithmetic and copies ran while one was open for 0% -> 0% of each run, Pallas kernels for 4% -> 5%
where the time goes in v6:
time: 123 us; the launch traced here: 122 us
  starting transfers between devices  72.5 us (59%)
  Pallas kernels  19.7 us (16%)
  blocking collectives  15.4 us (13%)
  waiting for transfers between devices  14.3 us (12%)
    ppermute x18, starting transfers between devices, swap(): lax.ppermute(block, axis, [(i, i + 1) for i in starts] + [(i + 1, i) for...  72.5 us
    pallas_call x20, Pallas kernels, call(): pl.pallas_call(kernel, out_shape=outs if many else outs[0], in_specs=in_s...  19.7 us
    all_to_all x1, blocking collectives, body(): rows = lax.all_to_all(rows, 'curve', 0, 0, tiled=True)  15.4 us
    ppermute x18, waiting for transfers between devices, swap(): lax.ppermute(block, axis, [(i, i + 1) for i in starts] + [(i + 1, i) for...  14.3 us
  transfers between devices with their start and end apart: 18, of which 8 were waited for; matrix products, arithmetic and copies ran while one was open for 0% of the time, Pallas kernels for 5%

profile of v6, /device:TPU:24, one launch (start us, length us, event | category | flops | bytes accessed | tf_op | source)
XLA Modules:
  0.0 122.1 jit_solution(4847960322705620928)
XLA Ops:
  0.0 2.1 %owners.1 = (f32[2,24,576]{2,1,0:T(8,128)S(1)}, f32[2,24,576]{2,1,0:T(8,128)S(1)}, s32[128]{0:T(128)S(1)}, f32[7,24,576]{2,1,0:T(8,128)S(1)}, f32[7,24,576]{2,1,0:T(8,128)S(1)}) custom-call(s32[1,128]{1,0:T(1,128)} %new_in.1, s32[1,128]{1,0:T(1,128)} %old_in.1, s32[4,128]{1,0:T(4,128)} %bitcast.9, s32[1,128]{1,0:T(1,128)} %map_in.1, f32[7,24,576]{2,1,0:T(8,128)} %rhs_in.1, ...), custom_call_target="tpu_custom_call" | custom-call | flops 10000000 | bytes 4000000 | tf_op jit(solution)/shard_map/owners/pallas_call | solution.py:581
  2.1 1.9 %collective-permute-start = (f32[2,24,576]{2,1,0:T(8,128)S(1)}, f32[2,24,576]{2,1,0:T(8,128)S(1)}, u32[]{:S(2)}, u32[]{:S(2)}) collective-permute-start(f32[2,24,576]{2,1,0:T(8,128)S(1)} %get-tuple-element.65), channel_id=1, source_target_pairs={{0,1},{2,3},{4,5},{6,7},{8,9},{10,11},{12,13},{14,15},{16,17},{18,... | collective-permute-start | bytes 331784 | tf_op jit(solution)/shard_map/ppermute | solution.py:595
  4.0 0.7 collective-permute-start.1
  4.7 0.6 place.1
  5.3 0.6 collect.1
  6.0 13.9 %collective-permute-start.2 = (f32[3,40,128]{2,1,0:T(8,128)S(1)}, f32[3,40,128]{2,1,0:T(8,128)S(1)}, u32[]{:S(2)}, u32[]{:S(2)}) collective-permute-start(f32[3,40,128]{2,1,0:T(8,128)S(1)} %get-tuple-element.72), channel_id=1, source_target_pairs={{1,2},{3,4},{5,6},{7,8},{9,10},{11,12},{13,14},{15,16},{17,18},{19... | collective-permute-start | bytes 184328 | tf_op jit(solution)/shard_map/ppermute | solution.py:595
  19.9 1.9 %collective-permute-start.3 = (f32[3,40,128]{2,1,0:T(8,128)S(1)}, f32[3,40,128]{2,1,0:T(8,128)S(1)}, u32[]{:S(2)}, u32[]{:S(2)}) collective-permute-start(f32[3,40,128]{2,1,0:T(8,128)S(1)} %get-tuple-element.73), channel_id=1, source_target_pairs={{0,1},{2,3},{4,5},{6,7},{8,9},{10,11},{12,13},{14,15},{16,17},{18,... | collective-permute-start | bytes 184328 | tf_op jit(solution)/shard_map/ppermute | solution.py:595
  21.8 1.0 level.1
  22.8 0.2 collective-permute-done.3.y_in
  23.0 1.2 start.1
  24.2 7.8 %collective-permute-start.4 = (f32[3,56,128]{2,1,0:T(8,128)S(1)}, f32[3,56,128]{2,1,0:T(8,128)S(1)}, u32[]{:S(2)}, u32[]{:S(2)}) collective-permute-start(f32[3,56,128]{2,1,0:T(8,128)S(1)} %get-tuple-element.77), channel_id=1, source_target_pairs={{1,2},{3,4},{5,6},{7,8},{9,10},{11,12},{13,14},{15,16},{17,18},{19... | collective-permute-start | bytes 258056 | tf_op jit(solution)/shard_map/ppermute | solution.py:595
  32.0 1.9 %collective-permute-start.5 = (f32[3,56,128]{2,1,0:T(8,128)S(1)}, f32[3,56,128]{2,1,0:T(8,128)S(1)}, u32[]{:S(2)}, u32[]{:S(2)}) collective-permute-start(f32[3,56,128]{2,1,0:T(8,128)S(1)} %get-tuple-element.78), channel_id=1, source_target_pairs={{0,1},{2,3},{4,5},{6,7},{8,9},{10,11},{12,13},{14,15},{16,17},{18,... | collective-permute-start | bytes 258056 | tf_op jit(solution)/shard_map/ppermute | solution.py:595
  33.9 1.3 %conduct.1 = (f32[5,6,24,640]{3,2,1,0:T(8,128)S(1)}, f32[5,24,640]{2,1,0:T(8,128)S(1)}) custom-call(s32[128]{0:T(128)S(1)} %get-tuple-element.61.info, f32[5,24,640]{2,1,0:T(8,128)S(1)} %get-tuple-element.68.coef, f32[5,40,128]{2,1,0:T(8,128)S(1)} %get-tuple-element.70.faces_in, f32[3,40,128]{2,1,0:T(8,128)S(1)} %collective-permute-done.2.x_in, ...), custom_call_target="tpu_custom_call" | custom-call | flops 10000000 | bytes 4000000 | tf_op jit(solution)/shard_map/conduct/pallas_call | solution.py:581
  35.2 0.5 pre_inner.1.part
  35.6 0.7 pre.1
  36.3 6.3 %collective-permute-start.6 = (f32[3,40,128]{2,1,0:T(8,128)S(1)}, f32[3,40,128]{2,1,0:T(8,128)S(1)}, u32[]{:S(2)}, u32[]{:S(2)}) collective-permute-start(f32[3,40,128]{2,1,0:T(8,128)S(1)} %get-tuple-element.86), channel_id=1, source_target_pairs={{1,2},{3,4},{5,6},{7,8},{9,10},{11,12},{13,14},{15,16},{17,18},{19... | collective-permute-start | bytes 184328 | tf_op jit(solution)/shard_map/ppermute | solution.py:595
  42.7 1.9 %collective-permute-start.7 = (f32[3,40,128]{2,1,0:T(8,128)S(1)}, f32[3,40,128]{2,1,0:T(8,128)S(1)}, u32[]{:S(2)}, u32[]{:S(2)}) collective-permute-start(f32[3,40,128]{2,1,0:T(8,128)S(1)} %get-tuple-element.87), channel_id=1, source_target_pairs={{0,1},{2,3},{4,5},{6,7},{8,9},{10,11},{12,13},{14,15},{16,17},{18,... | collective-permute-start | bytes 184328 | tf_op jit(solution)/shard_map/ppermute | solution.py:595
  44.6 0.5 residual_inner.1.part
  45.1 1.0 coarse_conduct.1
  46.1 1.1 residual.1
  47.2 6.3 %collective-permute-start.8 = (f32[3,48,128]{2,1,0:T(8,128)S(1)}, f32[3,48,128]{2,1,0:T(8,128)S(1)}, u32[]{:S(2)}, u32[]{:S(2)}) collective-permute-start(f32[3,48,128]{2,1,0:T(8,128)S(1)} %get-tuple-element.91), channel_id=1, source_target_pairs={{1,2},{3,4},{5,6},{7,8},{9,10},{11,12},{13,14},{15,16},{17,18},{19... | collective-permute-start | bytes 221192 | tf_op jit(solution)/shard_map/ppermute | solution.py:595
  53.5 1.9 %collective-permute-start.9 = (f32[3,16,128]{2,1,0:T(8,128)S(1)}, f32[3,16,128]{2,1,0:T(8,128)S(1)}, u32[]{:S(2)}, u32[]{:S(2)}) collective-permute-start(f32[3,16,128]{2,1,0:T(8,128)S(1)} %get-tuple-element.92), channel_id=1, source_target_pairs={{0,1},{2,3},{4,5},{6,7},{8,9},{10,11},{12,13},{14,15},{16,17},{18,... | collective-permute-start | bytes 73736 | tf_op jit(solution)/shard_map/ppermute | solution.py:595
  55.4 1.2 collective-permute-done.9.y_in
  56.6 0.5 collective-permute-done.8.x_in.g_in
  57.1 0.8 coarse_pre.1
  57.9 6.3 %collective-permute-start.10 = (f32[3,16,128]{2,1,0:T(8,128)S(1)}, f32[3,16,128]{2,1,0:T(8,128)S(1)}, u32[]{:S(2)}, u32[]{:S(2)}) collective-permute-start(f32[3,16,128]{2,1,0:T(8,128)S(1)} %get-tuple-element.97), channel_id=1, source_target_pairs={{1,2},{3,4},{5,6},{7,8},{9,10},{11,12},{13,14},{15,16},{17,18},{19... | collective-permute-start | bytes 73736 | tf_op jit(solution)/shard_map/ppermute | solution.py:595
  64.2 1.9 %collective-permute-start.11 = (f32[3,16,128]{2,1,0:T(8,128)S(1)}, f32[3,16,128]{2,1,0:T(8,128)S(1)}, u32[]{:S(2)}, u32[]{:S(2)}) collective-permute-start(f32[3,16,128]{2,1,0:T(8,128)S(1)} %get-tuple-element.98), channel_id=1, source_target_pairs={{0,1},{2,3},{4,5},{6,7},{8,9},{10,11},{12,13},{14,15},{16,17},{18,... | collective-permute-start | bytes 73736 | tf_op jit(solution)/shard_map/ppermute | solution.py:595
  66.1 1.1 collective-permute-done.10.x_in
  67.3 0.0 collective-permute-done.11.y_in
  67.3 0.9 totals.1
  68.2 15.4 %all_to_all.11 = f32[32,1,128]{2,1,0:T(1,128)S(1)} all-to-all(f32[32,1,128]{2,1,0:T(1,128)S(1)} %bitcast.8), channel_id=1, replica_groups=mesh['group'=16,'curve'=32] {'curve'}, dimensions={0} | all-to-all | bytes 32768 | tf_op jit(solution)/shard_map/all_to_all | solution.py:689
  83.6 2.8 %solve.1 = (f32[5,16,256]{2,1,0:T(8,128)S(1)}, f32[32,128]{1,0:T(8,128)S(1)}, f32[5,16,128]{2,1,0:T(8,128)}, f32[3,16,128]{2,1,0:T(8,128)S(1)}) custom-call(s32[128]{0:T(128)S(1)} %get-tuple-element.61.info, f32[32,128]{1,0:T(8,128)S(1)} %bitcast.7, f32[5,16,256]{2,1,0:T(8,128)S(1)} %get-tuple-element.100.swept, f32[5,6,16,256]{3,2,1,0:T(8,128)S(1)} %get-tuple-element.89.g, ...), custom_call_target="tpu_custom_call" | custom-call | flops 10000000 | bytes 4000000 | tf_op jit(solution)/shard_map/solve/pallas_call | solution.py:581
  86.4 4.6 %collective-permute-start.12 = (f32[3,16,128]{2,1,0:T(8,128)S(1)}, f32[3,16,128]{2,1,0:T(8,128)S(1)}, u32[]{:S(2)}, u32[]{:S(2)}) collective-permute-start(f32[3,16,128]{2,1,0:T(8,128)S(1)} %get-tuple-element.104), channel_id=1, source_target_pairs={{1,2},{3,4},{5,6},{7,8},{9,10},{11,12},{13,14},{15,16},{17,18},{19... | collective-permute-start | bytes 73736 | tf_op jit(solution)/shard_map/ppermute | solution.py:595
  91.0 4.7 %collective-permute-done.12.x_in = f32[3,16,128]{2,1,0:T(8,128)S(1)} collective-permute-done((f32[3,16,128]{2,1,0:T(8,128)S(1)}, f32[3,16,128]{2,1,0:T(8,128)S(1)}, u32[]{:S(2)}, u32[]{:S(2)}) %collective-permute-start.12) | collective-permute-done | bytes 24608 | tf_op jit(solution)/shard_map/ppermute | solution.py:595
  95.7 0.7 across.1
  96.4 1.9 %collective-permute-start.13 = (f32[3,16,128]{2,1,0:T(8,128)S(1)}, f32[3,16,128]{2,1,0:T(8,128)S(1)}, u32[]{:S(2)}, u32[]{:S(2)}) collective-permute-start(f32[3,16,128]{2,1,0:T(8,128)S(1)} %get-tuple-element.108), channel_id=1, source_target_pairs={{0,1},{2,3},{4,5},{6,7},{8,9},{10,11},{12,13},{14,15},{16,17},{18,... | collective-permute-start | bytes 73736 | tf_op jit(solution)/shard_map/ppermute | solution.py:595
  98.4 1.2 collective-permute-done.13.y_in
  99.5 1.0 refine.1
  100.5 4.7 %collective-permute-start.14 = (f32[3,40,128]{2,1,0:T(8,128)S(1)}, f32[3,40,128]{2,1,0:T(8,128)S(1)}, u32[]{:S(2)}, u32[]{:S(2)}) collective-permute-start(f32[3,40,128]{2,1,0:T(8,128)S(1)} %get-tuple-element.111), channel_id=1, source_target_pairs={{1,2},{3,4},{5,6},{7,8},{9,10},{11,12},{13,14},{15,16},{17,18},{19... | collective-permute-start | bytes 184328 | tf_op jit(solution)/shard_map/ppermute | solution.py:595
  105.2 1.9 %collective-permute-start.15 = (f32[3,40,128]{2,1,0:T(8,128)S(1)}, f32[3,40,128]{2,1,0:T(8,128)S(1)}, u32[]{:S(2)}, u32[]{:S(2)}) collective-permute-start(f32[3,40,128]{2,1,0:T(8,128)S(1)} %get-tuple-element.112), channel_id=1, source_target_pairs={{0,1},{2,3},{4,5},{6,7},{8,9},{10,11},{12,13},{14,15},{16,17},{18,... | collective-permute-start | bytes 184328 | tf_op jit(solution)/shard_map/ppermute | solution.py:595
  107.1 0.5 post_inner.1.part
  107.6 2.7 %collective-permute-done.14.x_in = f32[3,40,128]{2,1,0:T(8,128)S(1)} collective-permute-done((f32[3,40,128]{2,1,0:T(8,128)S(1)}, f32[3,40,128]{2,1,0:T(8,128)S(1)}, u32[]{:S(2)}, u32[]{:S(2)}) %collective-permute-start.14) | collective-permute-done | bytes 61472 | tf_op jit(solution)/shard_map/ppermute | solution.py:595
  110.3 0.7 post.1
  110.9 4.7 %collective-permute-start.16 = (f32[3,40,128]{2,1,0:T(8,128)S(1)}, f32[3,40,128]{2,1,0:T(8,128)S(1)}, u32[]{:S(2)}, u32[]{:S(2)}) collective-permute-start(f32[3,40,128]{2,1,0:T(8,128)S(1)} %get-tuple-element.115), channel_id=1, source_target_pairs={{1,2},{3,4},{5,6},{7,8},{9,10},{11,12},{13,14},{15,16},{17,18},{19... | collective-permute-start | bytes 184328 | tf_op jit(solution)/shard_map/ppermute | solution.py:595
  115.6 1.9 %collective-permute-start.17 = (f32[3,40,128]{2,1,0:T(8,128)S(1)}, f32[3,40,128]{2,1,0:T(8,128)S(1)}, u32[]{:S(2)}, u32[]{:S(2)}) collective-permute-start(f32[3,40,128]{2,1,0:T(8,128)S(1)} %get-tuple-element.116), channel_id=1, source_target_pairs={{0,1},{2,3},{4,5},{6,7},{8,9},{10,11},{12,13},{14,15},{16,17},{18,... | collective-permute-start | bytes 184328 | tf_op jit(solution)/shard_map/ppermute | solution.py:595
  117.5 0.5 last_inner.1.part
  118.0 2.7 %collective-permute-done.16.x_in = f32[3,40,128]{2,1,0:T(8,128)S(1)} collective-permute-done((f32[3,40,128]{2,1,0:T(8,128)S(1)}, f32[3,40,128]{2,1,0:T(8,128)S(1)}, u32[]{:S(2)}, u32[]{:S(2)}) %collective-permute-start.16) | collective-permute-done | bytes 61472 | tf_op jit(solution)/shard_map/ppermute | solution.py:595
  120.7 1.4 %last.1 = f32[5,24,576]{2,1,0:T(8,128)} custom-call(s32[128]{0:T(128)S(1)} %get-tuple-element.61.info, f32[5,24,640]{2,1,0:T(8,128)S(1)} %last_inner.1.part, f32[5,6,24,640]{3,2,1,0:T(8,128)S(1)} %get-tuple-element.75.g, f32[5,40,128]{2,1,0:T(8,128)S(1)} %get-tuple-element.114.faces_in, f32[3,40,128]{2,1,0:T(8,128)S(1)} %collective-permute-done.16.x_in, ...), custom_call_target="tpu_custom_call" | custom-call | flops 10000000 | bytes 4000000 | tf_op jit(solution)/shard_map/last/pallas_call | solution.py:581
  (9 shorter events, 0.0 us)
Async XLA Ops:
  2.1 3.2 %collective-permute-start = (f32[2,24,576]{2,1,0:T(8,128)S(1)}, f32[2,24,576]{2,1,0:T(8,128)S(1)}, u32[]{:S(2)}, u32[]{:S(2)}) collective-permute-start(f32[2,24,576]{2,1,0:T(8,128)S(1)} %get-tuple-element.65), channel_id=1, source_target_pairs={{0,1},{2,3},{4,5},{6,7},{8,9},{10,11},{12,13},{14,15},{16,17},{18,... | collective-permute-start | bytes 331784 | tf_op jit(solution)/shard_map/ppermute | solution.py:595
  4.0 1.3 %collective-permute-start.1 = (f32[2,24,576]{2,1,0:T(8,128)S(1)}, f32[2,24,576]{2,1,0:T(8,128)S(1)}, u32[]{:S(2)}, u32[]{:S(2)}) collective-permute-start(f32[2,24,576]{2,1,0:T(8,128)S(1)} %get-tuple-element.66), channel_id=1, source_target_pairs={{1,2},{3,4},{5,6},{7,8},{9,10},{11,12},{13,14},{15,16},{17,18},{19... | collective-permute-start | bytes 331784 | tf_op jit(solution)/shard_map/ppermute | solution.py:595
  6.0 16.9 %collective-permute-start.2 = (f32[3,40,128]{2,1,0:T(8,128)S(1)}, f32[3,40,128]{2,1,0:T(8,128)S(1)}, u32[]{:S(2)}, u32[]{:S(2)}) collective-permute-start(f32[3,40,128]{2,1,0:T(8,128)S(1)} %get-tuple-element.72), channel_id=1, source_target_pairs={{1,2},{3,4},{5,6},{7,8},{9,10},{11,12},{13,14},{15,16},{17,18},{19... | collective-permute-start | bytes 184328 | tf_op jit(solution)/shard_map/ppermute | solution.py:595
  19.9 3.1 %collective-permute-start.3 = (f32[3,40,128]{2,1,0:T(8,128)S(1)}, f32[3,40,128]{2,1,0:T(8,128)S(1)}, u32[]{:S(2)}, u32[]{:S(2)}) collective-permute-start(f32[3,40,128]{2,1,0:T(8,128)S(1)} %get-tuple-element.73), channel_id=1, source_target_pairs={{0,1},{2,3},{4,5},{6,7},{8,9},{10,11},{12,13},{14,15},{16,17},{18,... | collective-permute-start | bytes 184328 | tf_op jit(solution)/shard_map/ppermute | solution.py:595
  24.2 11.4 %collective-permute-start.4 = (f32[3,56,128]{2,1,0:T(8,128)S(1)}, f32[3,56,128]{2,1,0:T(8,128)S(1)}, u32[]{:S(2)}, u32[]{:S(2)}) collective-permute-start(f32[3,56,128]{2,1,0:T(8,128)S(1)} %get-tuple-element.77), channel_id=1, source_target_pairs={{1,2},{3,4},{5,6},{7,8},{9,10},{11,12},{13,14},{15,16},{17,18},{19... | collective-permute-start | bytes 258056 | tf_op jit(solution)/shard_map/ppermute | solution.py:595
  32.0 3.7 %collective-permute-start.5 = (f32[3,56,128]{2,1,0:T(8,128)S(1)}, f32[3,56,128]{2,1,0:T(8,128)S(1)}, u32[]{:S(2)}, u32[]{:S(2)}) collective-permute-start(f32[3,56,128]{2,1,0:T(8,128)S(1)} %get-tuple-element.78), channel_id=1, source_target_pairs={{0,1},{2,3},{4,5},{6,7},{8,9},{10,11},{12,13},{14,15},{16,17},{18,... | collective-permute-start | bytes 258056 | tf_op jit(solution)/shard_map/ppermute | solution.py:595
  36.3 9.8 %collective-permute-start.6 = (f32[3,40,128]{2,1,0:T(8,128)S(1)}, f32[3,40,128]{2,1,0:T(8,128)S(1)}, u32[]{:S(2)}, u32[]{:S(2)}) collective-permute-start(f32[3,40,128]{2,1,0:T(8,128)S(1)} %get-tuple-element.86), channel_id=1, source_target_pairs={{1,2},{3,4},{5,6},{7,8},{9,10},{11,12},{13,14},{15,16},{17,18},{19... | collective-permute-start | bytes 184328 | tf_op jit(solution)/shard_map/ppermute | solution.py:595
  42.7 3.5 %collective-permute-start.7 = (f32[3,40,128]{2,1,0:T(8,128)S(1)}, f32[3,40,128]{2,1,0:T(8,128)S(1)}, u32[]{:S(2)}, u32[]{:S(2)}) collective-permute-start(f32[3,40,128]{2,1,0:T(8,128)S(1)} %get-tuple-element.87), channel_id=1, source_target_pairs={{0,1},{2,3},{4,5},{6,7},{8,9},{10,11},{12,13},{14,15},{16,17},{18,... | collective-permute-start | bytes 184328 | tf_op jit(solution)/shard_map/ppermute | solution.py:595
  47.2 9.9 %collective-permute-start.8 = (f32[3,48,128]{2,1,0:T(8,128)S(1)}, f32[3,48,128]{2,1,0:T(8,128)S(1)}, u32[]{:S(2)}, u32[]{:S(2)}) collective-permute-start(f32[3,48,128]{2,1,0:T(8,128)S(1)} %get-tuple-element.91), channel_id=1, source_target_pairs={{1,2},{3,4},{5,6},{7,8},{9,10},{11,12},{13,14},{15,16},{17,18},{19... | collective-permute-start | bytes 221192 | tf_op jit(solution)/shard_map/ppermute | solution.py:595
  53.5 3.1 %collective-permute-start.9 = (f32[3,16,128]{2,1,0:T(8,128)S(1)}, f32[3,16,128]{2,1,0:T(8,128)S(1)}, u32[]{:S(2)}, u32[]{:S(2)}) collective-permute-start(f32[3,16,128]{2,1,0:T(8,128)S(1)} %get-tuple-element.92), channel_id=1, source_target_pairs={{0,1},{2,3},{4,5},{6,7},{8,9},{10,11},{12,13},{14,15},{16,17},{18,... | collective-permute-start | bytes 73736 | tf_op jit(solution)/shard_map/ppermute | solution.py:595
  57.9 9.4 %collective-permute-start.10 = (f32[3,16,128]{2,1,0:T(8,128)S(1)}, f32[3,16,128]{2,1,0:T(8,128)S(1)}, u32[]{:S(2)}, u32[]{:S(2)}) collective-permute-start(f32[3,16,128]{2,1,0:T(8,128)S(1)} %get-tuple-element.97), channel_id=1, source_target_pairs={{1,2},{3,4},{5,6},{7,8},{9,10},{11,12},{13,14},{15,16},{17,18},{19... | collective-permute-start | bytes 73736 | tf_op jit(solution)/shard_map/ppermute | solution.py:595
  64.2 3.1 %collective-permute-start.11 = (f32[3,16,128]{2,1,0:T(8,128)S(1)}, f32[3,16,128]{2,1,0:T(8,128)S(1)}, u32[]{:S(2)}, u32[]{:S(2)}) collective-permute-start(f32[3,16,128]{2,1,0:T(8,128)S(1)} %get-tuple-element.98), channel_id=1, source_target_pairs={{0,1},{2,3},{4,5},{6,7},{8,9},{10,11},{12,13},{14,15},{16,17},{18,... | collective-permute-start | bytes 73736 | tf_op jit(solution)/shard_map/ppermute | solution.py:595
  86.4 9.4 %collective-permute-start.12 = (f32[3,16,128]{2,1,0:T(8,128)S(1)}, f32[3,16,128]{2,1,0:T(8,128)S(1)}, u32[]{:S(2)}, u32[]{:S(2)}) collective-permute-start(f32[3,16,128]{2,1,0:T(8,128)S(1)} %get-tuple-element.104), channel_id=1, source_target_pairs={{1,2},{3,4},{5,6},{7,8},{9,10},{11,12},{13,14},{15,16},{17,18},{19... | collective-permute-start | bytes 73736 | tf_op jit(solution)/shard_map/ppermute | solution.py:595
  96.4 3.1 %collective-permute-start.13 = (f32[3,16,128]{2,1,0:T(8,128)S(1)}, f32[3,16,128]{2,1,0:T(8,128)S(1)}, u32[]{:S(2)}, u32[]{:S(2)}) collective-permute-start(f32[3,16,128]{2,1,0:T(8,128)S(1)} %get-tuple-element.108), channel_id=1, source_target_pairs={{0,1},{2,3},{4,5},{6,7},{8,9},{10,11},{12,13},{14,15},{16,17},{18,... | collective-permute-start | bytes 73736 | tf_op jit(solution)/shard_map/ppermute | solution.py:595
  100.5 9.8 %collective-permute-start.14 = (f32[3,40,128]{2,1,0:T(8,128)S(1)}, f32[3,40,128]{2,1,0:T(8,128)S(1)}, u32[]{:S(2)}, u32[]{:S(2)}) collective-permute-start(f32[3,40,128]{2,1,0:T(8,128)S(1)} %get-tuple-element.111), channel_id=1, source_target_pairs={{1,2},{3,4},{5,6},{7,8},{9,10},{11,12},{13,14},{15,16},{17,18},{19... | collective-permute-start | bytes 184328 | tf_op jit(solution)/shard_map/ppermute | solution.py:595
  105.2 5.1 %collective-permute-start.15 = (f32[3,40,128]{2,1,0:T(8,128)S(1)}, f32[3,40,128]{2,1,0:T(8,128)S(1)}, u32[]{:S(2)}, u32[]{:S(2)}) collective-permute-start(f32[3,40,128]{2,1,0:T(8,128)S(1)} %get-tuple-element.112), channel_id=1, source_target_pairs={{0,1},{2,3},{4,5},{6,7},{8,9},{10,11},{12,13},{14,15},{16,17},{18,... | collective-permute-start | bytes 184328 | tf_op jit(solution)/shard_map/ppermute | solution.py:595
  110.9 9.8 %collective-permute-start.16 = (f32[3,40,128]{2,1,0:T(8,128)S(1)}, f32[3,40,128]{2,1,0:T(8,128)S(1)}, u32[]{:S(2)}, u32[]{:S(2)}) collective-permute-start(f32[3,40,128]{2,1,0:T(8,128)S(1)} %get-tuple-element.115), channel_id=1, source_target_pairs={{1,2},{3,4},{5,6},{7,8},{9,10},{11,12},{13,14},{15,16},{17,18},{19... | collective-permute-start | bytes 184328 | tf_op jit(solution)/shard_map/ppermute | solution.py:595
  115.6 5.1 %collective-permute-start.17 = (f32[3,40,128]{2,1,0:T(8,128)S(1)}, f32[3,40,128]{2,1,0:T(8,128)S(1)}, u32[]{:S(2)}, u32[]{:S(2)}) collective-permute-start(f32[3,40,128]{2,1,0:T(8,128)S(1)} %get-tuple-element.116), channel_id=1, source_target_pairs={{0,1},{2,3},{4,5},{6,7},{8,9},{10,11},{12,13},{14,15},{16,17},{18,... | collective-permute-start | bytes 184328 | tf_op jit(solution)/shard_map/ppermute | solution.py:595

commit v7 on v5

--- a/solution.py
+++ b/solution.py
@@ -34,7 +34,7 @@
         self.factor = factor
 
 
-FINE = Level(24, 24, 640, 40, 24, 32, 40, 1.0)
+FINE = Level(24, 24, 640, 40, 16, 24, 32, 1.0)
 COARSE = Level(12, 16, 256, 68, 12, 14, 16, 0.25)
 BOTH_ROWS = FINE.face_rows + COARSE.face_rows
 
@@ -59,7 +59,13 @@
     move = lev.high_at - lev.last
     if move:
         tail = pltpu.roll(tail, move, 1)
-    faces[k, base : base + lev.rows, :] = jnp.where(lane < lev.side, y_field[:, :128], tail)
+    slab = jnp.where(lane < lev.side, y_field[:, :128], tail)
+    if lev is FINE:
+        pair = jnp.where(lane[0:8] < 64, slab[0:8], pltpu.roll(slab[8:16], 64, 1))
+        faces[k, base : base + 8, :] = pair
+        faces[k, base + 8 : base + 16, :] = slab[16:24]
+    else:
+        faces[k, base : base + lev.rows, :] = slab
     for j in range(lev.tiles):
         part = slice(128 * j, 128 * j + 128)
         low, high = base + lev.x_low + j, base + lev.x_high + j
@@ -87,12 +93,20 @@
     return jnp.concatenate([table[slot, pl.ds(first + j, 1), :] for j in range(lev.tiles)], axis=1)
 
 
+def y_slab(lev, table, slot, base):
+    if lev is not FINE:
+        return table[slot, pl.ds(base, lev.rows), :]
+    pair = table[slot, pl.ds(base, 8), :]
+    third = table[slot, pl.ds(base + 8, 8), :]
+    return jnp.concatenate([pair, pltpu.roll(pair, 64, 1), third], axis=0)
+
+
 def ghosts_of(lev, info, table, k, base):
     row = [info[TABLE + 4 * k + f] for f in range(4)]
     x_low = x_line(lev, table, row[0], base + lev.x_high)
     x_high = x_line(lev, table, row[1], base + lev.x_low)
-    y_low = pltpu.roll(table[row[2], pl.ds(base, lev.rows), :], 128 - lev.high_at, 1)
-    y_high = pltpu.roll(table[row[3], pl.ds(base, lev.rows), :], lev.last, 1)
+    y_low = pltpu.roll(y_slab(lev, table, row[2], base), 128 - lev.high_at, 1)
+    y_high = pltpu.roll(y_slab(lev, table, row[3], base), lev.last, 1)
     return row, x_low, x_high, y_low, y_high
 
 

time: 123 us -> 123 us (level)
  no operation moved by 1% of the time
where the time goes in v7:
time: 123 us; the launch traced here: 122 us
  starting transfers between devices  72.3 us (59%)
  Pallas kernels  19.1 us (16%)
  blocking collectives  15.4 us (13%)
  waiting for transfers between devices  15.3 us (12%)
    ppermute x18, starting transfers between devices, swap(): lax.ppermute(block, axis, [(i, i + 1) for i in starts] + [(i + 1, i) for...  72.3 us
    pallas_call x19, Pallas kernels, call(): pl.pallas_call(kernel, out_shape=outs if many else outs[0], in_specs=in_s...  19.1 us
    all_to_all x1, blocking collectives, body(): rows = lax.all_to_all(rows, 'curve', 0, 0, tiled=True)  15.4 us
    ppermute x18, waiting for transfers between devices, swap(): lax.ppermute(block, axis, [(i, i + 1) for i in starts] + [(i + 1, i) for...  15.3 us
  transfers between devices with their start and end apart: 18, of which 9 were waited for; matrix products, arithmetic and copies ran while one was open for 0% of the time, Pallas kernels for 4%

profile of v7, /device:TPU:24, one launch (start us, length us, event | category | flops | bytes accessed | tf_op | source)
XLA Modules:
  0.0 122.4 jit_solution(6799604761206990946)
XLA Ops:
  0.0 2.1 %owners.1 = (f32[2,24,576]{2,1,0:T(8,128)S(1)}, f32[2,24,576]{2,1,0:T(8,128)S(1)}, s32[128]{0:T(128)S(1)}, f32[7,24,576]{2,1,0:T(8,128)S(1)}, f32[7,24,576]{2,1,0:T(8,128)S(1)}) custom-call(s32[1,128]{1,0:T(1,128)} %new_in.1, s32[1,128]{1,0:T(1,128)} %old_in.1, s32[4,128]{1,0:T(4,128)} %bitcast.9, s32[1,128]{1,0:T(1,128)} %map_in.1, f32[7,24,576]{2,1,0:T(8,128)} %rhs_in.1, ...), custom_call_target="tpu_custom_call" | custom-call | flops 10000000 | bytes 4000000 | tf_op jit(solution)/shard_map/owners/pallas_call | solution.py:590
  2.1 1.9 %collective-permute-start = (f32[2,24,576]{2,1,0:T(8,128)S(1)}, f32[2,24,576]{2,1,0:T(8,128)S(1)}, u32[]{:S(2)}, u32[]{:S(2)}) collective-permute-start(f32[2,24,576]{2,1,0:T(8,128)S(1)} %get-tuple-element.66), channel_id=1, source_target_pairs={{0,1},{2,3},{4,5},{6,7},{8,9},{10,11},{12,13},{14,15},{16,17},{18,... | collective-permute-start | bytes 331784 | tf_op jit(solution)/shard_map/ppermute | solution.py:604
  4.0 0.7 collective-permute-start.1
  4.7 0.6 place.1
  5.3 0.0 collective-permute-done.y_in
  5.3 0.6 collect.1
  6.0 13.9 %collective-permute-start.2 = (f32[3,32,128]{2,1,0:T(8,128)S(1)}, f32[3,32,128]{2,1,0:T(8,128)S(1)}, u32[]{:S(2)}, u32[]{:S(2)}) collective-permute-start(f32[3,32,128]{2,1,0:T(8,128)S(1)} %get-tuple-element.73), channel_id=1, source_target_pairs={{1,2},{3,4},{5,6},{7,8},{9,10},{11,12},{13,14},{15,16},{17,18},{19... | collective-permute-start | bytes 147464 | tf_op jit(solution)/shard_map/ppermute | solution.py:604
  19.9 1.9 %collective-permute-start.3 = (f32[3,32,128]{2,1,0:T(8,128)S(1)}, f32[3,32,128]{2,1,0:T(8,128)S(1)}, u32[]{:S(2)}, u32[]{:S(2)}) collective-permute-start(f32[3,32,128]{2,1,0:T(8,128)S(1)} %get-tuple-element.74), channel_id=1, source_target_pairs={{0,1},{2,3},{4,5},{6,7},{8,9},{10,11},{12,13},{14,15},{16,17},{18,... | collective-permute-start | bytes 147464 | tf_op jit(solution)/shard_map/ppermute | solution.py:604
  21.8 1.0 level.1
  22.9 0.1 collective-permute-done.3.y_in
  23.0 1.5 %conduct.1 = (f32[5,6,24,640]{3,2,1,0:T(8,128)S(1)}, f32[5,24,640]{2,1,0:T(8,128)S(1)}, f32[5,24,640]{2,1,0:T(8,128)S(1)}, f32[5,24,640]{2,1,0:T(8,128)S(1)}, f3...) custom-call(s32[128]{0:T(128)S(1)} %get-tuple-element.62.info, ...), custom_call_target="tpu_custom_call" | custom-call | flops 10000000 | bytes 4000000 | tf_op jit(solution)/shard_map/conduct/pallas_call | solution.py:590
  24.5 7.8 %collective-permute-start.4 = (f32[3,48,128]{2,1,0:T(8,128)S(1)}, f32[3,48,128]{2,1,0:T(8,128)S(1)}, u32[]{:S(2)}, u32[]{:S(2)}) collective-permute-start(f32[3,48,128]{2,1,0:T(8,128)S(1)} %get-tuple-element.79), channel_id=1, source_target_pairs={{1,2},{3,4},{5,6},{7,8},{9,10},{11,12},{13,14},{15,16},{17,18},{19... | collective-permute-start | bytes 221192 | tf_op jit(solution)/shard_map/ppermute | solution.py:604
  32.3 1.9 %collective-permute-start.5 = (f32[3,48,128]{2,1,0:T(8,128)S(1)}, f32[3,48,128]{2,1,0:T(8,128)S(1)}, u32[]{:S(2)}, u32[]{:S(2)}) collective-permute-start(f32[3,48,128]{2,1,0:T(8,128)S(1)} %get-tuple-element.80), channel_id=1, source_target_pairs={{0,1},{2,3},{4,5},{6,7},{8,9},{10,11},{12,13},{14,15},{16,17},{18,... | collective-permute-start | bytes 221192 | tf_op jit(solution)/shard_map/ppermute | solution.py:604
  34.2 0.4 pre_inner.1.part
  34.7 0.8 collective-permute-done.5.y_in
  35.5 0.8 pre.1
  36.3 6.7 %collective-permute-start.6 = (f32[3,32,128]{2,1,0:T(8,128)S(1)}, f32[3,32,128]{2,1,0:T(8,128)S(1)}, u32[]{:S(2)}, u32[]{:S(2)}) collective-permute-start(f32[3,32,128]{2,1,0:T(8,128)S(1)} %get-tuple-element.88), channel_id=1, source_target_pairs={{1,2},{3,4},{5,6},{7,8},{9,10},{11,12},{13,14},{15,16},{17,18},{19... | collective-permute-start | bytes 147464 | tf_op jit(solution)/shard_map/ppermute | solution.py:604
  43.0 1.9 %collective-permute-start.7 = (f32[3,32,128]{2,1,0:T(8,128)S(1)}, f32[3,32,128]{2,1,0:T(8,128)S(1)}, u32[]{:S(2)}, u32[]{:S(2)}) collective-permute-start(f32[3,32,128]{2,1,0:T(8,128)S(1)} %get-tuple-element.89), channel_id=1, source_target_pairs={{0,1},{2,3},{4,5},{6,7},{8,9},{10,11},{12,13},{14,15},{16,17},{18,... | collective-permute-start | bytes 147464 | tf_op jit(solution)/shard_map/ppermute | solution.py:604
  44.9 0.5 residual_inner.1.part
  45.4 1.0 coarse_conduct.1
  46.5 1.1 residual.1
  47.6 6.2 %collective-permute-start.8 = (f32[3,48,128]{2,1,0:T(8,128)S(1)}, f32[3,48,128]{2,1,0:T(8,128)S(1)}, u32[]{:S(2)}, u32[]{:S(2)}) collective-permute-start(f32[3,48,128]{2,1,0:T(8,128)S(1)} %get-tuple-element.93), channel_id=1, source_target_pairs={{1,2},{3,4},{5,6},{7,8},{9,10},{11,12},{13,14},{15,16},{17,18},{19... | collective-permute-start | bytes 221192 | tf_op jit(solution)/shard_map/ppermute | solution.py:604
  53.8 1.9 %collective-permute-start.9 = (f32[3,16,128]{2,1,0:T(8,128)S(1)}, f32[3,16,128]{2,1,0:T(8,128)S(1)}, u32[]{:S(2)}, u32[]{:S(2)}) collective-permute-start(f32[3,16,128]{2,1,0:T(8,128)S(1)} %get-tuple-element.94), channel_id=1, source_target_pairs={{0,1},{2,3},{4,5},{6,7},{8,9},{10,11},{12,13},{14,15},{16,17},{18,... | collective-permute-start | bytes 73736 | tf_op jit(solution)/shard_map/ppermute | solution.py:604
  55.7 1.2 collective-permute-done.9.y_in
  56.9 0.6 collective-permute-done.8.x_in.g_in
  57.5 0.8 coarse_pre.1
  58.3 6.2 %collective-permute-start.10 = (f32[3,16,128]{2,1,0:T(8,128)S(1)}, f32[3,16,128]{2,1,0:T(8,128)S(1)}, u32[]{:S(2)}, u32[]{:S(2)}) collective-permute-start(f32[3,16,128]{2,1,0:T(8,128)S(1)} %get-tuple-element.99), channel_id=1, source_target_pairs={{1,2},{3,4},{5,6},{7,8},{9,10},{11,12},{13,14},{15,16},{17,18},{19... | collective-permute-start | bytes 73736 | tf_op jit(solution)/shard_map/ppermute | solution.py:604
  64.5 1.9 %collective-permute-start.11 = (f32[3,16,128]{2,1,0:T(8,128)S(1)}, f32[3,16,128]{2,1,0:T(8,128)S(1)}, u32[]{:S(2)}, u32[]{:S(2)}) collective-permute-start(f32[3,16,128]{2,1,0:T(8,128)S(1)} %get-tuple-element.100), channel_id=1, source_target_pairs={{0,1},{2,3},{4,5},{6,7},{8,9},{10,11},{12,13},{14,15},{16,17},{18,... | collective-permute-start | bytes 73736 | tf_op jit(solution)/shard_map/ppermute | solution.py:604
  66.4 1.3 %collective-permute-done.10.x_in = f32[3,16,128]{2,1,0:T(8,128)S(1)} collective-permute-done((f32[3,16,128]{2,1,0:T(8,128)S(1)}, f32[3,16,128]{2,1,0:T(8,128)S(1)}, u32[]{:S(2)}, u32[]{:S(2)}) %collective-permute-start.10) | collective-permute-done | bytes 24608 | tf_op jit(solution)/shard_map/ppermute | solution.py:604
  67.7 0.9 totals.1
  68.6 15.4 %all_to_all.11 = f32[32,1,128]{2,1,0:T(1,128)S(1)} all-to-all(f32[32,1,128]{2,1,0:T(1,128)S(1)} %bitcast.8), channel_id=1, replica_groups=mesh['group'=16,'curve'=32] {'curve'}, dimensions={0} | all-to-all | bytes 32768 | tf_op jit(solution)/shard_map/all_to_all | solution.py:693
  83.9 2.8 %solve.1 = (f32[5,16,256]{2,1,0:T(8,128)S(1)}, f32[32,128]{1,0:T(8,128)S(1)}, f32[5,16,128]{2,1,0:T(8,128)}, f32[3,16,128]{2,1,0:T(8,128)S(1)}) custom-call(s32[128]{0:T(128)S(1)} %get-tuple-element.62.info, f32[32,128]{1,0:T(8,128)S(1)} %bitcast.7, f32[5,16,256]{2,1,0:T(8,128)S(1)} %get-tuple-element.102.swept, f32[5,6,16,256]{3,2,1,0:T(8,128)S(1)} %get-tuple-element.91.g, ...), custom_call_target="tpu_custom_call" | custom-call | flops 10000000 | bytes 4000000 | tf_op jit(solution)/shard_map/solve/pallas_call | solution.py:590
  86.7 4.5 %collective-permute-start.12 = (f32[3,16,128]{2,1,0:T(8,128)S(1)}, f32[3,16,128]{2,1,0:T(8,128)S(1)}, u32[]{:S(2)}, u32[]{:S(2)}) collective-permute-start(f32[3,16,128]{2,1,0:T(8,128)S(1)} %get-tuple-element.106), channel_id=1, source_target_pairs={{1,2},{3,4},{5,6},{7,8},{9,10},{11,12},{13,14},{15,16},{17,18},{19... | collective-permute-start | bytes 73736 | tf_op jit(solution)/shard_map/ppermute | solution.py:604
  91.3 4.8 %collective-permute-done.12.x_in = f32[3,16,128]{2,1,0:T(8,128)S(1)} collective-permute-done((f32[3,16,128]{2,1,0:T(8,128)S(1)}, f32[3,16,128]{2,1,0:T(8,128)S(1)}, u32[]{:S(2)}, u32[]{:S(2)}) %collective-permute-start.12) | collective-permute-done | bytes 24608 | tf_op jit(solution)/shard_map/ppermute | solution.py:604
  96.1 0.7 across.1
  96.8 1.9 %collective-permute-start.13 = (f32[3,16,128]{2,1,0:T(8,128)S(1)}, f32[3,16,128]{2,1,0:T(8,128)S(1)}, u32[]{:S(2)}, u32[]{:S(2)}) collective-permute-start(f32[3,16,128]{2,1,0:T(8,128)S(1)} %get-tuple-element.110), channel_id=1, source_target_pairs={{0,1},{2,3},{4,5},{6,7},{8,9},{10,11},{12,13},{14,15},{16,17},{18,... | collective-permute-start | bytes 73736 | tf_op jit(solution)/shard_map/ppermute | solution.py:604
  98.7 1.2 collective-permute-done.13.y_in
  99.9 1.0 refine.1
  100.9 4.6 %collective-permute-start.14 = (f32[3,32,128]{2,1,0:T(8,128)S(1)}, f32[3,32,128]{2,1,0:T(8,128)S(1)}, u32[]{:S(2)}, u32[]{:S(2)}) collective-permute-start(f32[3,32,128]{2,1,0:T(8,128)S(1)} %get-tuple-element.113), channel_id=1, source_target_pairs={{1,2},{3,4},{5,6},{7,8},{9,10},{11,12},{13,14},{15,16},{17,18},{19... | collective-permute-start | bytes 147464 | tf_op jit(solution)/shard_map/ppermute | solution.py:604
  105.5 1.9 %collective-permute-start.15 = (f32[3,32,128]{2,1,0:T(8,128)S(1)}, f32[3,32,128]{2,1,0:T(8,128)S(1)}, u32[]{:S(2)}, u32[]{:S(2)}) collective-permute-start(f32[3,32,128]{2,1,0:T(8,128)S(1)} %get-tuple-element.114), channel_id=1, source_target_pairs={{0,1},{2,3},{4,5},{6,7},{8,9},{10,11},{12,13},{14,15},{16,17},{18,... | collective-permute-start | bytes 147464 | tf_op jit(solution)/shard_map/ppermute | solution.py:604
  107.4 0.4 post_inner.1.part
  107.9 2.7 %collective-permute-done.14.x_in = f32[3,32,128]{2,1,0:T(8,128)S(1)} collective-permute-done((f32[3,32,128]{2,1,0:T(8,128)S(1)}, f32[3,32,128]{2,1,0:T(8,128)S(1)}, u32[]{:S(2)}, u32[]{:S(2)}) %collective-permute-start.14) | collective-permute-done | bytes 49184 | tf_op jit(solution)/shard_map/ppermute | solution.py:604
  110.5 0.8 post.1
  111.3 4.6 %collective-permute-start.16 = (f32[3,32,128]{2,1,0:T(8,128)S(1)}, f32[3,32,128]{2,1,0:T(8,128)S(1)}, u32[]{:S(2)}, u32[]{:S(2)}) collective-permute-start(f32[3,32,128]{2,1,0:T(8,128)S(1)} %get-tuple-element.117), channel_id=1, source_target_pairs={{1,2},{3,4},{5,6},{7,8},{9,10},{11,12},{13,14},{15,16},{17,18},{19... | collective-permute-start | bytes 147464 | tf_op jit(solution)/shard_map/ppermute | solution.py:604
  115.9 1.9 %collective-permute-start.17 = (f32[3,32,128]{2,1,0:T(8,128)S(1)}, f32[3,32,128]{2,1,0:T(8,128)S(1)}, u32[]{:S(2)}, u32[]{:S(2)}) collective-permute-start(f32[3,32,128]{2,1,0:T(8,128)S(1)} %get-tuple-element.118), channel_id=1, source_target_pairs={{0,1},{2,3},{4,5},{6,7},{8,9},{10,11},{12,13},{14,15},{16,17},{18,... | collective-permute-start | bytes 147464 | tf_op jit(solution)/shard_map/ppermute | solution.py:604
  117.8 0.5 last_inner.1.part
  118.3 2.7 %collective-permute-done.16.x_in = f32[3,32,128]{2,1,0:T(8,128)S(1)} collective-permute-done((f32[3,32,128]{2,1,0:T(8,128)S(1)}, f32[3,32,128]{2,1,0:T(8,128)S(1)}, u32[]{:S(2)}, u32[]{:S(2)}) %collective-permute-start.16) | collective-permute-done | bytes 49184 | tf_op jit(solution)/shard_map/ppermute | solution.py:604
  121.0 1.5 %last.1 = f32[5,24,576]{2,1,0:T(8,128)} custom-call(s32[128]{0:T(128)S(1)} %get-tuple-element.62.info, f32[5,24,640]{2,1,0:T(8,128)S(1)} %last_inner.1.part, f32[5,6,24,640]{3,2,1,0:T(8,128)S(1)} %get-tuple-element.76.g, f32[5,32,128]{2,1,0:T(8,128)S(1)} %get-tuple-element.116.faces_in, f32[3,32,128]{2,1,0:T(8,128)S(1)} %collective-permute-done.16.x_in, ...), custom_call_target="tpu_custom_call" | custom-call | flops 10000000 | bytes 4000000 | tf_op jit(solution)/shard_map/last/pallas_call | solution.py:590
  (8 shorter events, 0.0 us)
Async XLA Ops:
  2.1 3.2 %collective-permute-start = (f32[2,24,576]{2,1,0:T(8,128)S(1)}, f32[2,24,576]{2,1,0:T(8,128)S(1)}, u32[]{:S(2)}, u32[]{:S(2)}) collective-permute-start(f32[2,24,576]{2,1,0:T(8,128)S(1)} %get-tuple-element.66), channel_id=1, source_target_pairs={{0,1},{2,3},{4,5},{6,7},{8,9},{10,11},{12,13},{14,15},{16,17},{18,... | collective-permute-start | bytes 331784 | tf_op jit(solution)/shard_map/ppermute | solution.py:604
  4.0 1.3 %collective-permute-start.1 = (f32[2,24,576]{2,1,0:T(8,128)S(1)}, f32[2,24,576]{2,1,0:T(8,128)S(1)}, u32[]{:S(2)}, u32[]{:S(2)}) collective-permute-start(f32[2,24,576]{2,1,0:T(8,128)S(1)} %get-tuple-element.67), channel_id=1, source_target_pairs={{1,2},{3,4},{5,6},{7,8},{9,10},{11,12},{13,14},{15,16},{17,18},{19... | collective-permute-start | bytes 331784 | tf_op jit(solution)/shard_map/ppermute | solution.py:604
  6.0 16.9 %collective-permute-start.2 = (f32[3,32,128]{2,1,0:T(8,128)S(1)}, f32[3,32,128]{2,1,0:T(8,128)S(1)}, u32[]{:S(2)}, u32[]{:S(2)}) collective-permute-start(f32[3,32,128]{2,1,0:T(8,128)S(1)} %get-tuple-element.73), channel_id=1, source_target_pairs={{1,2},{3,4},{5,6},{7,8},{9,10},{11,12},{13,14},{15,16},{17,18},{19... | collective-permute-start | bytes 147464 | tf_op jit(solution)/shard_map/ppermute | solution.py:604
  19.9 3.1 %collective-permute-start.3 = (f32[3,32,128]{2,1,0:T(8,128)S(1)}, f32[3,32,128]{2,1,0:T(8,128)S(1)}, u32[]{:S(2)}, u32[]{:S(2)}) collective-permute-start(f32[3,32,128]{2,1,0:T(8,128)S(1)} %get-tuple-element.74), channel_id=1, source_target_pairs={{0,1},{2,3},{4,5},{6,7},{8,9},{10,11},{12,13},{14,15},{16,17},{18,... | collective-permute-start | bytes 147464 | tf_op jit(solution)/shard_map/ppermute | solution.py:604
  24.5 10.2 %collective-permute-start.4 = (f32[3,48,128]{2,1,0:T(8,128)S(1)}, f32[3,48,128]{2,1,0:T(8,128)S(1)}, u32[]{:S(2)}, u32[]{:S(2)}) collective-permute-start(f32[3,48,128]{2,1,0:T(8,128)S(1)} %get-tuple-element.79), channel_id=1, source_target_pairs={{1,2},{3,4},{5,6},{7,8},{9,10},{11,12},{13,14},{15,16},{17,18},{19... | collective-permute-start | bytes 221192 | tf_op jit(solution)/shard_map/ppermute | solution.py:604
  32.3 3.2 %collective-permute-start.5 = (f32[3,48,128]{2,1,0:T(8,128)S(1)}, f32[3,48,128]{2,1,0:T(8,128)S(1)}, u32[]{:S(2)}, u32[]{:S(2)}) collective-permute-start(f32[3,48,128]{2,1,0:T(8,128)S(1)} %get-tuple-element.80), channel_id=1, source_target_pairs={{0,1},{2,3},{4,5},{6,7},{8,9},{10,11},{12,13},{14,15},{16,17},{18,... | collective-permute-start | bytes 221192 | tf_op jit(solution)/shard_map/ppermute | solution.py:604
  36.3 10.2 %collective-permute-start.6 = (f32[3,32,128]{2,1,0:T(8,128)S(1)}, f32[3,32,128]{2,1,0:T(8,128)S(1)}, u32[]{:S(2)}, u32[]{:S(2)}) collective-permute-start(f32[3,32,128]{2,1,0:T(8,128)S(1)} %get-tuple-element.88), channel_id=1, source_target_pairs={{1,2},{3,4},{5,6},{7,8},{9,10},{11,12},{13,14},{15,16},{17,18},{19... | collective-permute-start | bytes 147464 | tf_op jit(solution)/shard_map/ppermute | solution.py:604
  43.0 3.4 %collective-permute-start.7 = (f32[3,32,128]{2,1,0:T(8,128)S(1)}, f32[3,32,128]{2,1,0:T(8,128)S(1)}, u32[]{:S(2)}, u32[]{:S(2)}) collective-permute-start(f32[3,32,128]{2,1,0:T(8,128)S(1)} %get-tuple-element.89), channel_id=1, source_target_pairs={{0,1},{2,3},{4,5},{6,7},{8,9},{10,11},{12,13},{14,15},{16,17},{18,... | collective-permute-start | bytes 147464 | tf_op jit(solution)/shard_map/ppermute | solution.py:604
  47.6 9.9 %collective-permute-start.8 = (f32[3,48,128]{2,1,0:T(8,128)S(1)}, f32[3,48,128]{2,1,0:T(8,128)S(1)}, u32[]{:S(2)}, u32[]{:S(2)}) collective-permute-start(f32[3,48,128]{2,1,0:T(8,128)S(1)} %get-tuple-element.93), channel_id=1, source_target_pairs={{1,2},{3,4},{5,6},{7,8},{9,10},{11,12},{13,14},{15,16},{17,18},{19... | collective-permute-start | bytes 221192 | tf_op jit(solution)/shard_map/ppermute | solution.py:604
  53.8 3.1 %collective-permute-start.9 = (f32[3,16,128]{2,1,0:T(8,128)S(1)}, f32[3,16,128]{2,1,0:T(8,128)S(1)}, u32[]{:S(2)}, u32[]{:S(2)}) collective-permute-start(f32[3,16,128]{2,1,0:T(8,128)S(1)} %get-tuple-element.94), channel_id=1, source_target_pairs={{0,1},{2,3},{4,5},{6,7},{8,9},{10,11},{12,13},{14,15},{16,17},{18,... | collective-permute-start | bytes 73736 | tf_op jit(solution)/shard_map/ppermute | solution.py:604
  58.3 9.4 %collective-permute-start.10 = (f32[3,16,128]{2,1,0:T(8,128)S(1)}, f32[3,16,128]{2,1,0:T(8,128)S(1)}, u32[]{:S(2)}, u32[]{:S(2)}) collective-permute-start(f32[3,16,128]{2,1,0:T(8,128)S(1)} %get-tuple-element.99), channel_id=1, source_target_pairs={{1,2},{3,4},{5,6},{7,8},{9,10},{11,12},{13,14},{15,16},{17,18},{19... | collective-permute-start | bytes 73736 | tf_op jit(solution)/shard_map/ppermute | solution.py:604
  64.5 3.2 %collective-permute-start.11 = (f32[3,16,128]{2,1,0:T(8,128)S(1)}, f32[3,16,128]{2,1,0:T(8,128)S(1)}, u32[]{:S(2)}, u32[]{:S(2)}) collective-permute-start(f32[3,16,128]{2,1,0:T(8,128)S(1)} %get-tuple-element.100), channel_id=1, source_target_pairs={{0,1},{2,3},{4,5},{6,7},{8,9},{10,11},{12,13},{14,15},{16,17},{18,... | collective-permute-start | bytes 73736 | tf_op jit(solution)/shard_map/ppermute | solution.py:604
  86.7 9.4 %collective-permute-start.12 = (f32[3,16,128]{2,1,0:T(8,128)S(1)}, f32[3,16,128]{2,1,0:T(8,128)S(1)}, u32[]{:S(2)}, u32[]{:S(2)}) collective-permute-start(f32[3,16,128]{2,1,0:T(8,128)S(1)} %get-tuple-element.106), channel_id=1, source_target_pairs={{1,2},{3,4},{5,6},{7,8},{9,10},{11,12},{13,14},{15,16},{17,18},{19... | collective-permute-start | bytes 73736 | tf_op jit(solution)/shard_map/ppermute | solution.py:604
  96.8 3.1 %collective-permute-start.13 = (f32[3,16,128]{2,1,0:T(8,128)S(1)}, f32[3,16,128]{2,1,0:T(8,128)S(1)}, u32[]{:S(2)}, u32[]{:S(2)}) collective-permute-start(f32[3,16,128]{2,1,0:T(8,128)S(1)} %get-tuple-element.110), channel_id=1, source_target_pairs={{0,1},{2,3},{4,5},{6,7},{8,9},{10,11},{12,13},{14,15},{16,17},{18,... | collective-permute-start | bytes 73736 | tf_op jit(solution)/shard_map/ppermute | solution.py:604
  100.9 9.6 %collective-permute-start.14 = (f32[3,32,128]{2,1,0:T(8,128)S(1)}, f32[3,32,128]{2,1,0:T(8,128)S(1)}, u32[]{:S(2)}, u32[]{:S(2)}) collective-permute-start(f32[3,32,128]{2,1,0:T(8,128)S(1)} %get-tuple-element.113), channel_id=1, source_target_pairs={{1,2},{3,4},{5,6},{7,8},{9,10},{11,12},{13,14},{15,16},{17,18},{19... | collective-permute-start | bytes 147464 | tf_op jit(solution)/shard_map/ppermute | solution.py:604
  105.5 5.1 %collective-permute-start.15 = (f32[3,32,128]{2,1,0:T(8,128)S(1)}, f32[3,32,128]{2,1,0:T(8,128)S(1)}, u32[]{:S(2)}, u32[]{:S(2)}) collective-permute-start(f32[3,32,128]{2,1,0:T(8,128)S(1)} %get-tuple-element.114), channel_id=1, source_target_pairs={{0,1},{2,3},{4,5},{6,7},{8,9},{10,11},{12,13},{14,15},{16,17},{18,... | collective-permute-start | bytes 147464 | tf_op jit(solution)/shard_map/ppermute | solution.py:604
  111.3 9.6 %collective-permute-start.16 = (f32[3,32,128]{2,1,0:T(8,128)S(1)}, f32[3,32,128]{2,1,0:T(8,128)S(1)}, u32[]{:S(2)}, u32[]{:S(2)}) collective-permute-start(f32[3,32,128]{2,1,0:T(8,128)S(1)} %get-tuple-element.117), channel_id=1, source_target_pairs={{1,2},{3,4},{5,6},{7,8},{9,10},{11,12},{13,14},{15,16},{17,18},{19... | collective-permute-start | bytes 147464 | tf_op jit(solution)/shard_map/ppermute | solution.py:604
  115.9 5.1 %collective-permute-start.17 = (f32[3,32,128]{2,1,0:T(8,128)S(1)}, f32[3,32,128]{2,1,0:T(8,128)S(1)}, u32[]{:S(2)}, u32[]{:S(2)}) collective-permute-start(f32[3,32,128]{2,1,0:T(8,128)S(1)} %get-tuple-element.118), channel_id=1, source_target_pairs={{0,1},{2,3},{4,5},{6,7},{8,9},{10,11},{12,13},{14,15},{16,17},{18,... | collective-permute-start | bytes 147464 | tf_op jit(solution)/shard_map/ppermute | solution.py:604

commit v8 on v6

--- a/solution.py
+++ b/solution.py
@@ -34,7 +34,7 @@
         self.factor = factor
 
 
-FINE = Level(24, 24, 640, 40, 24, 32, 40, 1.0)
+FINE = Level(24, 24, 640, 40, 16, 24, 32, 1.0)
 COARSE = Level(12, 16, 256, 68, 12, 14, 16, 0.25)
 BOTH_ROWS = FINE.face_rows + COARSE.face_rows
 
@@ -59,7 +59,13 @@
     move = lev.high_at - lev.last
     if move:
         tail = pltpu.roll(tail, move, 1)
-    faces[k, base : base + lev.rows, :] = jnp.where(lane < lev.side, y_field[:, :128], tail)
+    slab = jnp.where(lane < lev.side, y_field[:, :128], tail)
+    if lev is FINE:
+        pair = jnp.where(lane[0:8] < 64, slab[0:8], pltpu.roll(slab[8:16], 64, 1))
+        faces[k, base : base + 8, :] = pair
+        faces[k, base + 8 : base + 16, :] = slab[16:24]
+    else:
+        faces[k, base : base + lev.rows, :] = slab
     for j in range(lev.tiles):
         part = slice(128 * j, 128 * j + 128)
         low, high = base + lev.x_low + j, base + lev.x_high + j
@@ -87,12 +93,20 @@
     return jnp.concatenate([table[slot, pl.ds(first + j, 1), :] for j in range(lev.tiles)], axis=1)
 
 
+def y_slab(lev, table, slot, base):
+    if lev is not FINE:
+        return table[slot, pl.ds(base, lev.rows), :]
+    pair = table[slot, pl.ds(base, 8), :]
+    third = table[slot, pl.ds(base + 8, 8), :]
+    return jnp.concatenate([pair, pltpu.roll(pair, 64, 1), third], axis=0)
+
+
 def ghosts_of(lev, info, table, k, base):
     row = [info[TABLE + 4 * k + f] for f in range(4)]
     x_low = x_line(lev, table, row[0], base + lev.x_high)
     x_high = x_line(lev, table, row[1], base + lev.x_low)
-    y_low = pltpu.roll(table[row[2], pl.ds(base, lev.rows), :], 128 - lev.high_at, 1)
-    y_high = pltpu.roll(table[row[3], pl.ds(base, lev.rows), :], lev.last, 1)
+    y_low = pltpu.roll(y_slab(lev, table, row[2], base), 128 - lev.high_at, 1)
+    y_high = pltpu.roll(y_slab(lev, table, row[3], base), lev.last, 1)
     return row, x_low, x_high, y_low, y_high
 
 

time: 123 us -> 123 us (level)
  starting transfers between devices: 72.5 us -> 70.9 us
    ppermute x18, starting transfers between devices: 72.5 us -> 70.9 us  [swap(): lax.ppermute(block, axis, [(i, i + 1) for i in starts] + [(i + 1, i) for...]
  transfers between devices with their start and end apart: 18 -> 18, of which waited for: 8 -> 9; matrix products, arithmetic and copies ran while one was open for 0% -> 0% of each run, Pallas kernels for 5% -> 5%
where the time goes in v8:
time: 123 us; the launch traced here: 122 us
  starting transfers between devices  70.9 us (58%)
  Pallas kernels  20.5 us (17%)
  waiting for transfers between devices  15.4 us (13%)
  blocking collectives  15.4 us (13%)
    ppermute x18, starting transfers between devices, swap(): lax.ppermute(block, axis, [(i, i + 1) for i in starts] + [(i + 1, i) for...  70.9 us
    pallas_call x20, Pallas kernels, call(): pl.pallas_call(kernel, out_shape=outs if many else outs[0], in_specs=in_s...  20.5 us
    ppermute x18, waiting for transfers between devices, swap(): lax.ppermute(block, axis, [(i, i + 1) for i in starts] + [(i + 1, i) for...  15.4 us
    all_to_all x1, blocking collectives, body(): rows = lax.all_to_all(rows, 'curve', 0, 0, tiled=True)  15.4 us
  transfers between devices with their start and end apart: 18, of which 9 were waited for; matrix products, arithmetic and copies ran while one was open for 0% of the time, Pallas kernels for 5%

profile of v8, /device:TPU:24, one launch (start us, length us, event | category | flops | bytes accessed | tf_op | source)
XLA Modules:
  0.0 122.5 jit_solution(15040231536070440563)
XLA Ops:
  0.0 2.1 %owners.1 = (f32[2,24,576]{2,1,0:T(8,128)S(1)}, f32[2,24,576]{2,1,0:T(8,128)S(1)}, s32[128]{0:T(128)S(1)}, f32[7,24,576]{2,1,0:T(8,128)S(1)}, f32[7,24,576]{2,1,0:T(8,128)S(1)}) custom-call(s32[1,128]{1,0:T(1,128)} %new_in.1, s32[1,128]{1,0:T(1,128)} %old_in.1, s32[4,128]{1,0:T(4,128)} %bitcast.9, s32[1,128]{1,0:T(1,128)} %map_in.1, f32[7,24,576]{2,1,0:T(8,128)} %rhs_in.1, ...), custom_call_target="tpu_custom_call" | custom-call | flops 10000000 | bytes 4000000 | tf_op jit(solution)/shard_map/owners/pallas_call | solution.py:595
  2.1 1.9 %collective-permute-start = (f32[2,24,576]{2,1,0:T(8,128)S(1)}, f32[2,24,576]{2,1,0:T(8,128)S(1)}, u32[]{:S(2)}, u32[]{:S(2)}) collective-permute-start(f32[2,24,576]{2,1,0:T(8,128)S(1)} %get-tuple-element.65), channel_id=1, source_target_pairs={{0,1},{2,3},{4,5},{6,7},{8,9},{10,11},{12,13},{14,15},{16,17},{18,... | collective-permute-start | bytes 331784 | tf_op jit(solution)/shard_map/ppermute | solution.py:609
  4.0 0.7 collective-permute-start.1
  4.7 0.6 place.1
  5.3 0.6 collect.1
  6.0 13.9 %collective-permute-start.2 = (f32[3,32,128]{2,1,0:T(8,128)S(1)}, f32[3,32,128]{2,1,0:T(8,128)S(1)}, u32[]{:S(2)}, u32[]{:S(2)}) collective-permute-start(f32[3,32,128]{2,1,0:T(8,128)S(1)} %get-tuple-element.72), channel_id=1, source_target_pairs={{1,2},{3,4},{5,6},{7,8},{9,10},{11,12},{13,14},{15,16},{17,18},{19... | collective-permute-start | bytes 147464 | tf_op jit(solution)/shard_map/ppermute | solution.py:609
  19.9 1.9 %collective-permute-start.3 = (f32[3,32,128]{2,1,0:T(8,128)S(1)}, f32[3,32,128]{2,1,0:T(8,128)S(1)}, u32[]{:S(2)}, u32[]{:S(2)}) collective-permute-start(f32[3,32,128]{2,1,0:T(8,128)S(1)} %get-tuple-element.73), channel_id=1, source_target_pairs={{0,1},{2,3},{4,5},{6,7},{8,9},{10,11},{12,13},{14,15},{16,17},{18,... | collective-permute-start | bytes 147464 | tf_op jit(solution)/shard_map/ppermute | solution.py:609
  21.8 1.0 level.1
  22.9 0.1 collective-permute-done.3.y_in
  23.0 1.4 %start.1 = (f32[5,24,640]{2,1,0:T(8,128)S(1)}, f32[5,48,128]{2,1,0:T(8,128)S(1)}, f32[3,48,128]{2,1,0:T(8,128)S(1)}, f32[3,48,128]{2,1,0:T(8,128)S(1)}) custom-call(s32[128]{0:T(128)S(1)} %get-tuple-element.61.info, f32[5,24,640]{2,1,0:T(8,128)S(1)} %get-tuple-element.69.source, f32[5,24,640]{2,1,0:T(8,128)S(1)} %get-tuple-element.68.coef, ...), custom_call_target="tpu_custom_call" | custom-call | flops 10000000 | bytes 4000000 | tf_op jit(solution)/shard_map/start/pallas_call | solution.py:595
  24.4 7.8 %collective-permute-start.4 = (f32[3,48,128]{2,1,0:T(8,128)S(1)}, f32[3,48,128]{2,1,0:T(8,128)S(1)}, u32[]{:S(2)}, u32[]{:S(2)}) collective-permute-start(f32[3,48,128]{2,1,0:T(8,128)S(1)} %get-tuple-element.77), channel_id=1, source_target_pairs={{1,2},{3,4},{5,6},{7,8},{9,10},{11,12},{13,14},{15,16},{17,18},{19... | collective-permute-start | bytes 221192 | tf_op jit(solution)/shard_map/ppermute | solution.py:609
  32.2 1.9 %collective-permute-start.5 = (f32[3,48,128]{2,1,0:T(8,128)S(1)}, f32[3,48,128]{2,1,0:T(8,128)S(1)}, u32[]{:S(2)}, u32[]{:S(2)}) collective-permute-start(f32[3,48,128]{2,1,0:T(8,128)S(1)} %get-tuple-element.78), channel_id=1, source_target_pairs={{0,1},{2,3},{4,5},{6,7},{8,9},{10,11},{12,13},{14,15},{16,17},{18,... | collective-permute-start | bytes 221192 | tf_op jit(solution)/shard_map/ppermute | solution.py:609
  34.1 1.5 %conduct.1 = (f32[5,6,24,640]{3,2,1,0:T(8,128)S(1)}, f32[5,24,640]{2,1,0:T(8,128)S(1)}) custom-call(s32[128]{0:T(128)S(1)} %get-tuple-element.61.info, f32[5,24,640]{2,1,0:T(8,128)S(1)} %get-tuple-element.68.coef, f32[5,32,128]{2,1,0:T(8,128)S(1)} %get-tuple-element.70.faces_in, f32[3,32,128]{2,1,0:T(8,128)S(1)} %collective-permute-done.2.x_in, ...), custom_call_target="tpu_custom_call" | custom-call | flops 10000000 | bytes 4000000 | tf_op jit(solution)/shard_map/conduct/pallas_call | solution.py:595
  35.6 0.4 pre_inner.1.part
  36.1 0.8 pre.1
  36.9 6.0 %collective-permute-start.6 = (f32[3,32,128]{2,1,0:T(8,128)S(1)}, f32[3,32,128]{2,1,0:T(8,128)S(1)}, u32[]{:S(2)}, u32[]{:S(2)}) collective-permute-start(f32[3,32,128]{2,1,0:T(8,128)S(1)} %get-tuple-element.86), channel_id=1, source_target_pairs={{1,2},{3,4},{5,6},{7,8},{9,10},{11,12},{13,14},{15,16},{17,18},{19... | collective-permute-start | bytes 147464 | tf_op jit(solution)/shard_map/ppermute | solution.py:609
  42.9 1.9 %collective-permute-start.7 = (f32[3,32,128]{2,1,0:T(8,128)S(1)}, f32[3,32,128]{2,1,0:T(8,128)S(1)}, u32[]{:S(2)}, u32[]{:S(2)}) collective-permute-start(f32[3,32,128]{2,1,0:T(8,128)S(1)} %get-tuple-element.87), channel_id=1, source_target_pairs={{0,1},{2,3},{4,5},{6,7},{8,9},{10,11},{12,13},{14,15},{16,17},{18,... | collective-permute-start | bytes 147464 | tf_op jit(solution)/shard_map/ppermute | solution.py:609
  44.8 0.5 residual_inner.1.part
  45.3 1.0 coarse_conduct.1
  46.3 0.2 collective-permute-done.6.x_in
  46.5 1.1 residual.1
  47.6 6.0 %collective-permute-start.8 = (f32[3,48,128]{2,1,0:T(8,128)S(1)}, f32[3,48,128]{2,1,0:T(8,128)S(1)}, u32[]{:S(2)}, u32[]{:S(2)}) collective-permute-start(f32[3,48,128]{2,1,0:T(8,128)S(1)} %get-tuple-element.91), channel_id=1, source_target_pairs={{1,2},{3,4},{5,6},{7,8},{9,10},{11,12},{13,14},{15,16},{17,18},{19... | collective-permute-start | bytes 221192 | tf_op jit(solution)/shard_map/ppermute | solution.py:609
  53.7 1.9 %collective-permute-start.9 = (f32[3,16,128]{2,1,0:T(8,128)S(1)}, f32[3,16,128]{2,1,0:T(8,128)S(1)}, u32[]{:S(2)}, u32[]{:S(2)}) collective-permute-start(f32[3,16,128]{2,1,0:T(8,128)S(1)} %get-tuple-element.92), channel_id=1, source_target_pairs={{0,1},{2,3},{4,5},{6,7},{8,9},{10,11},{12,13},{14,15},{16,17},{18,... | collective-permute-start | bytes 73736 | tf_op jit(solution)/shard_map/ppermute | solution.py:609
  55.6 1.2 collective-permute-done.9.y_in
  56.8 0.8 collective-permute-done.8.x_in.g_in
  57.5 0.8 coarse_pre.1
  58.3 6.0 %collective-permute-start.10 = (f32[3,16,128]{2,1,0:T(8,128)S(1)}, f32[3,16,128]{2,1,0:T(8,128)S(1)}, u32[]{:S(2)}, u32[]{:S(2)}) collective-permute-start(f32[3,16,128]{2,1,0:T(8,128)S(1)} %get-tuple-element.97), channel_id=1, source_target_pairs={{1,2},{3,4},{5,6},{7,8},{9,10},{11,12},{13,14},{15,16},{17,18},{19... | collective-permute-start | bytes 73736 | tf_op jit(solution)/shard_map/ppermute | solution.py:609
  64.4 1.9 %collective-permute-start.11 = (f32[3,16,128]{2,1,0:T(8,128)S(1)}, f32[3,16,128]{2,1,0:T(8,128)S(1)}, u32[]{:S(2)}, u32[]{:S(2)}) collective-permute-start(f32[3,16,128]{2,1,0:T(8,128)S(1)} %get-tuple-element.98), channel_id=1, source_target_pairs={{0,1},{2,3},{4,5},{6,7},{8,9},{10,11},{12,13},{14,15},{16,17},{18,... | collective-permute-start | bytes 73736 | tf_op jit(solution)/shard_map/ppermute | solution.py:609
  66.3 1.4 %collective-permute-done.10.x_in = f32[3,16,128]{2,1,0:T(8,128)S(1)} collective-permute-done((f32[3,16,128]{2,1,0:T(8,128)S(1)}, f32[3,16,128]{2,1,0:T(8,128)S(1)}, u32[]{:S(2)}, u32[]{:S(2)}) %collective-permute-start.10) | collective-permute-done | bytes 24608 | tf_op jit(solution)/shard_map/ppermute | solution.py:609
  67.7 0.9 totals.1
  68.6 15.4 %all_to_all.11 = f32[32,1,128]{2,1,0:T(1,128)S(1)} all-to-all(f32[32,1,128]{2,1,0:T(1,128)S(1)} %bitcast.8), channel_id=1, replica_groups=mesh['group'=16,'curve'=32] {'curve'}, dimensions={0} | all-to-all | bytes 32768 | tf_op jit(solution)/shard_map/all_to_all | solution.py:703
  84.0 2.8 %solve.1 = (f32[5,16,256]{2,1,0:T(8,128)S(1)}, f32[32,128]{1,0:T(8,128)S(1)}, f32[5,16,128]{2,1,0:T(8,128)}, f32[3,16,128]{2,1,0:T(8,128)S(1)}) custom-call(s32[128]{0:T(128)S(1)} %get-tuple-element.61.info, f32[32,128]{1,0:T(8,128)S(1)} %bitcast.7, f32[5,16,256]{2,1,0:T(8,128)S(1)} %get-tuple-element.100.swept, f32[5,6,16,256]{3,2,1,0:T(8,128)S(1)} %get-tuple-element.89.g, ...), custom_call_target="tpu_custom_call" | custom-call | flops 10000000 | bytes 4000000 | tf_op jit(solution)/shard_map/solve/pallas_call | solution.py:595
  86.8 4.4 %collective-permute-start.12 = (f32[3,16,128]{2,1,0:T(8,128)S(1)}, f32[3,16,128]{2,1,0:T(8,128)S(1)}, u32[]{:S(2)}, u32[]{:S(2)}) collective-permute-start(f32[3,16,128]{2,1,0:T(8,128)S(1)} %get-tuple-element.104), channel_id=1, source_target_pairs={{1,2},{3,4},{5,6},{7,8},{9,10},{11,12},{13,14},{15,16},{17,18},{19... | collective-permute-start | bytes 73736 | tf_op jit(solution)/shard_map/ppermute | solution.py:609
  91.2 4.9 %collective-permute-done.12.x_in = f32[3,16,128]{2,1,0:T(8,128)S(1)} collective-permute-done((f32[3,16,128]{2,1,0:T(8,128)S(1)}, f32[3,16,128]{2,1,0:T(8,128)S(1)}, u32[]{:S(2)}, u32[]{:S(2)}) %collective-permute-start.12) | collective-permute-done | bytes 24608 | tf_op jit(solution)/shard_map/ppermute | solution.py:609
  96.1 0.7 across.1
  96.8 1.9 %collective-permute-start.13 = (f32[3,16,128]{2,1,0:T(8,128)S(1)}, f32[3,16,128]{2,1,0:T(8,128)S(1)}, u32[]{:S(2)}, u32[]{:S(2)}) collective-permute-start(f32[3,16,128]{2,1,0:T(8,128)S(1)} %get-tuple-element.108), channel_id=1, source_target_pairs={{0,1},{2,3},{4,5},{6,7},{8,9},{10,11},{12,13},{14,15},{16,17},{18,... | collective-permute-start | bytes 73736 | tf_op jit(solution)/shard_map/ppermute | solution.py:609
  98.8 1.2 collective-permute-done.13.y_in
  99.9 1.0 refine.1
  100.9 4.4 %collective-permute-start.14 = (f32[3,32,128]{2,1,0:T(8,128)S(1)}, f32[3,32,128]{2,1,0:T(8,128)S(1)}, u32[]{:S(2)}, u32[]{:S(2)}) collective-permute-start(f32[3,32,128]{2,1,0:T(8,128)S(1)} %get-tuple-element.111), channel_id=1, source_target_pairs={{1,2},{3,4},{5,6},{7,8},{9,10},{11,12},{13,14},{15,16},{17,18},{19... | collective-permute-start | bytes 147464 | tf_op jit(solution)/shard_map/ppermute | solution.py:609
  105.4 1.9 %collective-permute-start.15 = (f32[3,32,128]{2,1,0:T(8,128)S(1)}, f32[3,32,128]{2,1,0:T(8,128)S(1)}, u32[]{:S(2)}, u32[]{:S(2)}) collective-permute-start(f32[3,32,128]{2,1,0:T(8,128)S(1)} %get-tuple-element.112), channel_id=1, source_target_pairs={{0,1},{2,3},{4,5},{6,7},{8,9},{10,11},{12,13},{14,15},{16,17},{18,... | collective-permute-start | bytes 147464 | tf_op jit(solution)/shard_map/ppermute | solution.py:609
  107.3 0.4 post_inner.1.part
  107.8 2.8 %collective-permute-done.14.x_in = f32[3,32,128]{2,1,0:T(8,128)S(1)} collective-permute-done((f32[3,32,128]{2,1,0:T(8,128)S(1)}, f32[3,32,128]{2,1,0:T(8,128)S(1)}, u32[]{:S(2)}, u32[]{:S(2)}) %collective-permute-start.14) | collective-permute-done | bytes 49184 | tf_op jit(solution)/shard_map/ppermute | solution.py:609
  110.6 0.8 post.1
  111.4 4.4 %collective-permute-start.16 = (f32[3,32,128]{2,1,0:T(8,128)S(1)}, f32[3,32,128]{2,1,0:T(8,128)S(1)}, u32[]{:S(2)}, u32[]{:S(2)}) collective-permute-start(f32[3,32,128]{2,1,0:T(8,128)S(1)} %get-tuple-element.115), channel_id=1, source_target_pairs={{1,2},{3,4},{5,6},{7,8},{9,10},{11,12},{13,14},{15,16},{17,18},{19... | collective-permute-start | bytes 147464 | tf_op jit(solution)/shard_map/ppermute | solution.py:609
  115.8 1.9 %collective-permute-start.17 = (f32[3,32,128]{2,1,0:T(8,128)S(1)}, f32[3,32,128]{2,1,0:T(8,128)S(1)}, u32[]{:S(2)}, u32[]{:S(2)}) collective-permute-start(f32[3,32,128]{2,1,0:T(8,128)S(1)} %get-tuple-element.116), channel_id=1, source_target_pairs={{0,1},{2,3},{4,5},{6,7},{8,9},{10,11},{12,13},{14,15},{16,17},{18,... | collective-permute-start | bytes 147464 | tf_op jit(solution)/shard_map/ppermute | solution.py:609
  117.7 0.5 last_inner.1.part
  118.2 2.8 %collective-permute-done.16.x_in = f32[3,32,128]{2,1,0:T(8,128)S(1)} collective-permute-done((f32[3,32,128]{2,1,0:T(8,128)S(1)}, f32[3,32,128]{2,1,0:T(8,128)S(1)}, u32[]{:S(2)}, u32[]{:S(2)}) %collective-permute-start.16) | collective-permute-done | bytes 49184 | tf_op jit(solution)/shard_map/ppermute | solution.py:609
  121.0 1.5 %last.1 = f32[5,24,576]{2,1,0:T(8,128)} custom-call(s32[128]{0:T(128)S(1)} %get-tuple-element.61.info, f32[5,24,640]{2,1,0:T(8,128)S(1)} %last_inner.1.part, f32[5,6,24,640]{3,2,1,0:T(8,128)S(1)} %get-tuple-element.75.g, f32[5,32,128]{2,1,0:T(8,128)S(1)} %get-tuple-element.114.faces_in, f32[3,32,128]{2,1,0:T(8,128)S(1)} %collective-permute-done.16.x_in, ...), custom_call_target="tpu_custom_call" | custom-call | flops 10000000 | bytes 4000000 | tf_op jit(solution)/shard_map/last/pallas_call | solution.py:595
  (9 shorter events, 0.0 us)
Async XLA Ops:
  2.1 3.2 %collective-permute-start = (f32[2,24,576]{2,1,0:T(8,128)S(1)}, f32[2,24,576]{2,1,0:T(8,128)S(1)}, u32[]{:S(2)}, u32[]{:S(2)}) collective-permute-start(f32[2,24,576]{2,1,0:T(8,128)S(1)} %get-tuple-element.65), channel_id=1, source_target_pairs={{0,1},{2,3},{4,5},{6,7},{8,9},{10,11},{12,13},{14,15},{16,17},{18,... | collective-permute-start | bytes 331784 | tf_op jit(solution)/shard_map/ppermute | solution.py:609
  4.0 1.3 %collective-permute-start.1 = (f32[2,24,576]{2,1,0:T(8,128)S(1)}, f32[2,24,576]{2,1,0:T(8,128)S(1)}, u32[]{:S(2)}, u32[]{:S(2)}) collective-permute-start(f32[2,24,576]{2,1,0:T(8,128)S(1)} %get-tuple-element.66), channel_id=1, source_target_pairs={{1,2},{3,4},{5,6},{7,8},{9,10},{11,12},{13,14},{15,16},{17,18},{19... | collective-permute-start | bytes 331784 | tf_op jit(solution)/shard_map/ppermute | solution.py:609
  6.0 16.9 %collective-permute-start.2 = (f32[3,32,128]{2,1,0:T(8,128)S(1)}, f32[3,32,128]{2,1,0:T(8,128)S(1)}, u32[]{:S(2)}, u32[]{:S(2)}) collective-permute-start(f32[3,32,128]{2,1,0:T(8,128)S(1)} %get-tuple-element.72), channel_id=1, source_target_pairs={{1,2},{3,4},{5,6},{7,8},{9,10},{11,12},{13,14},{15,16},{17,18},{19... | collective-permute-start | bytes 147464 | tf_op jit(solution)/shard_map/ppermute | solution.py:609
  19.9 3.1 %collective-permute-start.3 = (f32[3,32,128]{2,1,0:T(8,128)S(1)}, f32[3,32,128]{2,1,0:T(8,128)S(1)}, u32[]{:S(2)}, u32[]{:S(2)}) collective-permute-start(f32[3,32,128]{2,1,0:T(8,128)S(1)} %get-tuple-element.73), channel_id=1, source_target_pairs={{0,1},{2,3},{4,5},{6,7},{8,9},{10,11},{12,13},{14,15},{16,17},{18,... | collective-permute-start | bytes 147464 | tf_op jit(solution)/shard_map/ppermute | solution.py:609
  24.4 11.6 %collective-permute-start.4 = (f32[3,48,128]{2,1,0:T(8,128)S(1)}, f32[3,48,128]{2,1,0:T(8,128)S(1)}, u32[]{:S(2)}, u32[]{:S(2)}) collective-permute-start(f32[3,48,128]{2,1,0:T(8,128)S(1)} %get-tuple-element.77), channel_id=1, source_target_pairs={{1,2},{3,4},{5,6},{7,8},{9,10},{11,12},{13,14},{15,16},{17,18},{19... | collective-permute-start | bytes 221192 | tf_op jit(solution)/shard_map/ppermute | solution.py:609
  32.2 3.8 %collective-permute-start.5 = (f32[3,48,128]{2,1,0:T(8,128)S(1)}, f32[3,48,128]{2,1,0:T(8,128)S(1)}, u32[]{:S(2)}, u32[]{:S(2)}) collective-permute-start(f32[3,48,128]{2,1,0:T(8,128)S(1)} %get-tuple-element.78), channel_id=1, source_target_pairs={{0,1},{2,3},{4,5},{6,7},{8,9},{10,11},{12,13},{14,15},{16,17},{18,... | collective-permute-start | bytes 221192 | tf_op jit(solution)/shard_map/ppermute | solution.py:609
  36.9 9.6 %collective-permute-start.6 = (f32[3,32,128]{2,1,0:T(8,128)S(1)}, f32[3,32,128]{2,1,0:T(8,128)S(1)}, u32[]{:S(2)}, u32[]{:S(2)}) collective-permute-start(f32[3,32,128]{2,1,0:T(8,128)S(1)} %get-tuple-element.86), channel_id=1, source_target_pairs={{1,2},{3,4},{5,6},{7,8},{9,10},{11,12},{13,14},{15,16},{17,18},{19... | collective-permute-start | bytes 147464 | tf_op jit(solution)/shard_map/ppermute | solution.py:609
  42.9 3.6 %collective-permute-start.7 = (f32[3,32,128]{2,1,0:T(8,128)S(1)}, f32[3,32,128]{2,1,0:T(8,128)S(1)}, u32[]{:S(2)}, u32[]{:S(2)}) collective-permute-start(f32[3,32,128]{2,1,0:T(8,128)S(1)} %get-tuple-element.87), channel_id=1, source_target_pairs={{0,1},{2,3},{4,5},{6,7},{8,9},{10,11},{12,13},{14,15},{16,17},{18,... | collective-permute-start | bytes 147464 | tf_op jit(solution)/shard_map/ppermute | solution.py:609
  47.6 9.9 %collective-permute-start.8 = (f32[3,48,128]{2,1,0:T(8,128)S(1)}, f32[3,48,128]{2,1,0:T(8,128)S(1)}, u32[]{:S(2)}, u32[]{:S(2)}) collective-permute-start(f32[3,48,128]{2,1,0:T(8,128)S(1)} %get-tuple-element.91), channel_id=1, source_target_pairs={{1,2},{3,4},{5,6},{7,8},{9,10},{11,12},{13,14},{15,16},{17,18},{19... | collective-permute-start | bytes 221192 | tf_op jit(solution)/shard_map/ppermute | solution.py:609
  53.7 3.1 %collective-permute-start.9 = (f32[3,16,128]{2,1,0:T(8,128)S(1)}, f32[3,16,128]{2,1,0:T(8,128)S(1)}, u32[]{:S(2)}, u32[]{:S(2)}) collective-permute-start(f32[3,16,128]{2,1,0:T(8,128)S(1)} %get-tuple-element.92), channel_id=1, source_target_pairs={{0,1},{2,3},{4,5},{6,7},{8,9},{10,11},{12,13},{14,15},{16,17},{18,... | collective-permute-start | bytes 73736 | tf_op jit(solution)/shard_map/ppermute | solution.py:609
  58.3 9.4 %collective-permute-start.10 = (f32[3,16,128]{2,1,0:T(8,128)S(1)}, f32[3,16,128]{2,1,0:T(8,128)S(1)}, u32[]{:S(2)}, u32[]{:S(2)}) collective-permute-start(f32[3,16,128]{2,1,0:T(8,128)S(1)} %get-tuple-element.97), channel_id=1, source_target_pairs={{1,2},{3,4},{5,6},{7,8},{9,10},{11,12},{13,14},{15,16},{17,18},{19... | collective-permute-start | bytes 73736 | tf_op jit(solution)/shard_map/ppermute | solution.py:609
  64.4 3.3 %collective-permute-start.11 = (f32[3,16,128]{2,1,0:T(8,128)S(1)}, f32[3,16,128]{2,1,0:T(8,128)S(1)}, u32[]{:S(2)}, u32[]{:S(2)}) collective-permute-start(f32[3,16,128]{2,1,0:T(8,128)S(1)} %get-tuple-element.98), channel_id=1, source_target_pairs={{0,1},{2,3},{4,5},{6,7},{8,9},{10,11},{12,13},{14,15},{16,17},{18,... | collective-permute-start | bytes 73736 | tf_op jit(solution)/shard_map/ppermute | solution.py:609
  86.8 9.4 %collective-permute-start.12 = (f32[3,16,128]{2,1,0:T(8,128)S(1)}, f32[3,16,128]{2,1,0:T(8,128)S(1)}, u32[]{:S(2)}, u32[]{:S(2)}) collective-permute-start(f32[3,16,128]{2,1,0:T(8,128)S(1)} %get-tuple-element.104), channel_id=1, source_target_pairs={{1,2},{3,4},{5,6},{7,8},{9,10},{11,12},{13,14},{15,16},{17,18},{19... | collective-permute-start | bytes 73736 | tf_op jit(solution)/shard_map/ppermute | solution.py:609
  96.8 3.1 %collective-permute-start.13 = (f32[3,16,128]{2,1,0:T(8,128)S(1)}, f32[3,16,128]{2,1,0:T(8,128)S(1)}, u32[]{:S(2)}, u32[]{:S(2)}) collective-permute-start(f32[3,16,128]{2,1,0:T(8,128)S(1)} %get-tuple-element.108), channel_id=1, source_target_pairs={{0,1},{2,3},{4,5},{6,7},{8,9},{10,11},{12,13},{14,15},{16,17},{18,... | collective-permute-start | bytes 73736 | tf_op jit(solution)/shard_map/ppermute | solution.py:609
  100.9 9.6 %collective-permute-start.14 = (f32[3,32,128]{2,1,0:T(8,128)S(1)}, f32[3,32,128]{2,1,0:T(8,128)S(1)}, u32[]{:S(2)}, u32[]{:S(2)}) collective-permute-start(f32[3,32,128]{2,1,0:T(8,128)S(1)} %get-tuple-element.111), channel_id=1, source_target_pairs={{1,2},{3,4},{5,6},{7,8},{9,10},{11,12},{13,14},{15,16},{17,18},{19... | collective-permute-start | bytes 147464 | tf_op jit(solution)/shard_map/ppermute | solution.py:609
  105.4 5.2 %collective-permute-start.15 = (f32[3,32,128]{2,1,0:T(8,128)S(1)}, f32[3,32,128]{2,1,0:T(8,128)S(1)}, u32[]{:S(2)}, u32[]{:S(2)}) collective-permute-start(f32[3,32,128]{2,1,0:T(8,128)S(1)} %get-tuple-element.112), channel_id=1, source_target_pairs={{0,1},{2,3},{4,5},{6,7},{8,9},{10,11},{12,13},{14,15},{16,17},{18,... | collective-permute-start | bytes 147464 | tf_op jit(solution)/shard_map/ppermute | solution.py:609
  111.4 9.6 %collective-permute-start.16 = (f32[3,32,128]{2,1,0:T(8,128)S(1)}, f32[3,32,128]{2,1,0:T(8,128)S(1)}, u32[]{:S(2)}, u32[]{:S(2)}) collective-permute-start(f32[3,32,128]{2,1,0:T(8,128)S(1)} %get-tuple-element.115), channel_id=1, source_target_pairs={{1,2},{3,4},{5,6},{7,8},{9,10},{11,12},{13,14},{15,16},{17,18},{19... | collective-permute-start | bytes 147464 | tf_op jit(solution)/shard_map/ppermute | solution.py:609
  115.8 5.2 %collective-permute-start.17 = (f32[3,32,128]{2,1,0:T(8,128)S(1)}, f32[3,32,128]{2,1,0:T(8,128)S(1)}, u32[]{:S(2)}, u32[]{:S(2)}) collective-permute-start(f32[3,32,128]{2,1,0:T(8,128)S(1)} %get-tuple-element.116), channel_id=1, source_target_pairs={{0,1},{2,3},{4,5},{6,7},{8,9},{10,11},{12,13},{14,15},{16,17},{18,... | collective-permute-start | bytes 147464 | tf_op jit(solution)/shard_map/ppermute | solution.py:609
